TPU v7x, 1024 devices: a whole 8x8x8 slice. The times are simulated.
1024 devices in a mesh: img: 64 (over z, x_lo, core), txt: 16 (over x_hi, y).
Axes of the slice: x: 8 (x_hi: 2, x_lo: 4; x = x_hi * 4 + x_lo), y: 8, z: 8, core: 2. Of those that a mesh axis runs over, the one named last changes fastest.
Arguments:
- image_embed: bfloat16 [8192, 1152], P(('img', 'txt')), may hold values from -8 to 8
- text_embed: bfloat16 [8192, 1152], P(('txt', 'img')), may hold values from -8 to 8
- pair_index: int32 [8192], P(('img', 'txt')), may hold values from 0 to 8191, as said below
- log_scale: float32 [1], replicated, may hold values from 2 to 2.6
- bias: float32 [1], replicated, may hold values from -9 to -6
Outputs:
- image_grad: float32 [8192, 1152], P(('img', 'txt'))
- text_grad: float32 [8192, 1152], P(('txt', 'img'))
- stats: float32 [3], replicated
Inputs may be any that keep to these rules, and one draw needn't show every extreme that they name: pair_index is a permutation of the text rows.
All inputs are finite; a program needn't handle non-finite values.
Results may differ from a plain program's by a relative error of at most 0.0026.
Values may be sent and summed in bfloat16 or wider, within the bound.
No kernel may reach another device: no remote copies, remote signals or barrier semaphores. Data moves between devices by JAX's collectives and lax.ppermute only.
A program may use at most 32 MiB of HBM per device.

v0:
```python
import jax
import jax.numpy as jnp
from jax import lax
from jax.sharding import PartitionSpec as P

EPS = 1e-06


def normalize(rows):
    values = rows.astype(jnp.float32)
    norm = jnp.sqrt(jnp.sum(values * values, axis=1, keepdims=True) + EPS)
    return (values / norm, norm)


def project(unit, norm, grad):
    return (grad - unit * jnp.sum(unit * grad, axis=1, keepdims=True)) / norm


def score_block(image_block, text_piece, pairs, columns, scale, shift):
    cosine = jnp.dot(image_block, text_piece.T, preferred_element_type=jnp.float32)
    logits = scale * cosine + shift
    sign = jnp.where(pairs[:, None] == columns[None, :], 1.0, -1.0).astype(jnp.float32)
    dlogit = -sign * jax.nn.sigmoid(-sign * logits)
    dlogit_low = dlogit.astype(jnp.bfloat16)
    extra = jnp.stack(
        [
            jnp.sum(jax.nn.softplus(-sign * logits)),
            jnp.sum(dlogit),
            jnp.sum(dlogit * scale * cosine),
        ]
    )
    image_part = scale * jnp.dot(dlogit_low, text_piece, preferred_element_type=jnp.float32)
    return (dlogit_low, image_part, extra)


def per_device(image_embed, text_embed, pair_index, log_scale, bias):
    scale = jnp.exp(log_scale[0])
    shift = bias[0]
    image_unit, image_norm = normalize(image_embed)
    text_unit, text_norm = normalize(text_embed)
    image_low = image_unit.astype(jnp.bfloat16)
    text_low = text_unit.astype(jnp.bfloat16)
    own_rows = text_low.shape[0]
    image_block, pairs = (
        lax.all_gather(image_low, "txt", axis=0, tiled=True),
        lax.all_gather(pair_index, "txt", axis=0, tiled=True),
    )
    text_width = own_rows * lax.axis_size("img")
    col_start = lax.axis_index("txt") * text_width
    text_block = lax.all_gather(text_low, "img", axis=0, tiled=True)
    columns = col_start + jnp.arange(text_width, dtype=jnp.int32)
    dlogit_low, image_part, sums = score_block(
        image_block, text_block, pairs, columns, scale, shift
    )
    text_part = scale * lax.dot_general(
        dlogit_low, image_block, (((0,), (0,)), ((), ())), preferred_element_type=jnp.float32
    )
    text_total = lax.psum_scatter(text_part, "img", scatter_dimension=0, tiled=True)
    image_total = lax.psum_scatter(image_part, "txt", scatter_dimension=0, tiled=True)
    loss_sum, bias_sum, scale_sum = lax.psum((sums[0], sums[1], sums[2]), ("img", "txt"))
    batch_total = own_rows * lax.axis_size("img") * lax.axis_size("txt")
    stats = jnp.stack([loss_sum, bias_sum, scale_sum]) / batch_total
    image_grad = project(image_unit, image_norm, image_total)
    text_grad = project(text_unit, text_norm, text_total)
    return (image_grad, text_grad, stats)


def solution(mesh):
    in_specs = (P(("img", "txt"), None), P(("txt", "img"), None), P(("img", "txt")), P(), P())
    out_specs = (P(("img", "txt"), None), P(("txt", "img"), None), P())
    return jax.shard_map(
        per_device, mesh=mesh, in_specs=in_specs, out_specs=out_specs, check_vma=False
    )
```

profile of v0, /device:TPU:1, one launch (start us, length us, event | category | flops | bytes accessed | tf_op | source)
XLA Modules:
  0.0 903.7 jit_solution(5189565545762428974)
XLA Ops:
  7.2 0.0 all-gather.2.cloned.1.call-start
  7.2 0.8 fusion.4
  8.1 1.4 fusion.6
  9.5 0.0 all-gather.2.cloned.1.call-update
  9.5 0.0 all-reduce.7.cloned.1.call-start
  10.9 1.4 fusion.8
  13.0 0.9 dynamic-update-slice
  13.8 18.9 %all-reduce = s32[128]{0:T(128)S(1)} all-reduce(s32[128]{0:T(128)S(1)} %dynamic-update-slice), channel_id=1, replica_groups=mesh['img'=64,'txt'=16] {'txt'}, use_global_device_ids=true, to_apply=%add | all-reduce | flops 128 | bytes 1024
  32.7 0.8 fusion.3
  33.6 0.8 fusion.5
  34.4 40.6 %all_gather.10 = bf16[128,1152]{1,0:T(8,128)(2,1)S(1)} all-gather(bf16[8,1152]{1,0:T(8,128)(2,1)S(1)} %fusion.5), channel_id=1, replica_groups=mesh['img'=64,'txt'=16] {'txt'}, dimensions={0}, use_global_device_ids=true | all-gather | bytes 313344 | tf_op jit(solution)/shard_map/all_gather | solution.py:45
  74.9 68.5 %all-gather.2.cloned.1.call-done = bf16[512,1152]{1,0:T(8,128)(2,1)} async-done(((bf16[8,1152]{1,0:T(8,128)(2,1)}), bf16[512,1152]{1,0:T(8,128)(2,1)}) %all-gather.2.cloned.1.call-update) | async-done | bytes 1179664 | tf_op jit(solution)/shard_map/all_gather | solution.py:50
  143.5 0.0 copy-start.2
  143.5 2.8 fusion
  146.2 0.0 copy-done.2
  146.2 1.3 convolution_multiply_fusion.1
  147.5 0.0 all-reduce.7.cloned.1.call-update
  147.5 0.0 all-reduce.9.cloned.1.call-start
  147.6 0.0 copy-start
  147.6 0.0 copy-start.1
  147.6 2.0 convolution_multiply_fusion
  149.6 0.0 all-reduce.9.cloned.1.call-update
  149.7 1.3 dynamic-slice.3
  152.3 115.1 %all-reduce.3 = (f32[1]{0:T(128)}, f32[1]{0:T(128)}, f32[1]{0:T(128)}) all-reduce(f32[1]{0:T(128)} %bitcast.5, f32[1]{0:T(128)} %bitcast.4, f32[1]{0:T(128)} %bitcast.3), channel_id=1, replica_groups=mesh['img'=64,'txt'=16] {'img','txt'}, use_global_device_ids=true, to_apply=%region_11.12 | all-reduce | flops 3 | bytes 24 | tf_op jit(solution)/shard_map/psum | solution.py:60
  267.4 2.6 maximum_multiply_fusion
  270.0 67.9 %all-reduce.7.cloned.1.call-done = f32[128,1152]{1,0:T(8,128)} async-done(((f32[128,1152]{1,0:T(8,128)}), f32[128,1152]{1,0:T(8,128)}) %all-reduce.7.cloned.1.call-update) | async-done | bytes 589840
  337.9 0.0 copy-done
  337.9 1.0 multiply_reduce_fusion.2
  338.8 1.5 subtract_divide_fusion.1
  340.3 554.4 %all-reduce.9.cloned.1.call-done = f32[512,1152]{1,0:T(8,128)} async-done(((f32[512,1152]{1,0:T(8,128)}), f32[512,1152]{1,0:T(8,128)}) %all-reduce.9.cloned.1.call-update) | async-done | bytes 2359312
  894.7 0.0 copy-done.1
  894.7 1.0 multiply_reduce_fusion.1
  895.7 1.5 subtract_divide_fusion
  (4 shorter events, 0.0 us)
Async XLA Ops:
  7.2 136.3 %all-gather.2.cloned.1.call-start = ((), (), s32[]{:S(2)}) async-start(), calls=%async_computation | async-start | bytes 1198080 | tf_op jit(solution)/shard_map/all_gather | solution.py:50
  9.5 328.4 %all-reduce.7.cloned.1.call-start = ((), (), s32[]{:S(2)}) async-start(), calls=%async_computation.1 | async-start | bytes 1179648
  143.5 2.8 copy-start.2
  147.5 747.2 %all-reduce.9.cloned.1.call-start = ((), (), s32[]{:S(2)}) async-start(), calls=%async_computation.2 | async-start | bytes 4718592
  147.6 190.3 %copy-start = (bf16[8,1152]{1,0:T(8,128)(2,1)S(1)}, bf16[8,1152]{1,0:T(8,128)(2,1)}, u32[]{:S(2)}) copy-start(bf16[8,1152]{1,0:T(8,128)(2,1)} %param.5) | copy-start | bytes 55300
  147.6 747.1 %copy-start.1 = (bf16[8,1152]{1,0:T(8,128)(2,1)S(1)}, bf16[8,1152]{1,0:T(8,128)(2,1)}, u32[]{:S(2)}) copy-start(bf16[8,1152]{1,0:T(8,128)(2,1)} %param.6) | copy-start | bytes 55300
Sparse Core Ops, SparseCore 0:
  11.3 132.1 all-gather.1
  147.7 190.1 all-reduce.6
  341.8 552.9 all-reduce.8
where the time goes:
time: 905 us; the launch traced here: 904 us
  waiting for transfers between devices  691 us (76%)
  blocking collectives  175 us (19%)
  between operations  17.1 us (2%)
  other arithmetic  11.4 us (1%)
    unnamed x5, waiting for transfers between devices  622 us
    psum x1, blocking collectives, per_device(): lax.psum((sums[0], sums[1], sums[2]), ('img', 'txt'))  115 us
    all_gather x1, waiting for transfers between devices, per_device(): text_block = lax.all_gather(text_low, 'img', axis=0, tiled=True)  68.5 us
    all_gather x1, blocking collectives, per_device(): lax.all_gather(image_low, 'txt', axis=0, tiled=True)  40.6 us
    unnamed x1, blocking collectives  18.9 us
  transfers between devices with their start and end apart: 3, of which 3 were waited for; matrix products, arithmetic and copies ran while one was open for 1% of the time, Pallas kernels for 0%

commit v1 on v0

v1 whole, which is shorter than its diff:
```python
import functools
import jax
import jax.numpy as jnp
from jax import lax
from jax.experimental import pallas as pl
from jax.experimental.pallas import tpu as pltpu
from jax.sharding import Mesh, PartitionSpec as P

EPS = 1e-06
EXTRA = 128
F32 = jnp.float32
BF16 = jnp.bfloat16
VMEM = pl.BlockSpec(memory_space=pltpu.VMEM)
SMEM = pl.BlockSpec(memory_space=pltpu.SMEM)


def unit_and_norm(rows):
    values = rows.astype(F32)
    norm = jnp.sqrt(jnp.sum(values * values, axis=1, keepdims=True) + EPS)
    return values / norm, norm


def lanes(rows):
    return lax.broadcasted_iota(jnp.int32, (rows, EXTRA), 1)


def pack_kernel(image_ref, text_ref, pair_ref, image_out, text_out):
    width = image_ref.shape[1]
    image_low, _ = unit_and_norm(image_ref[...])
    text_low, _ = unit_and_norm(text_ref[...])
    rows = image_ref.shape[0]
    row = lax.broadcasted_iota(jnp.int32, (rows, EXTRA), 0)
    pair = jnp.zeros((rows, EXTRA), jnp.int32)
    for r in range(rows):
        pair = jnp.where(row == r, pair_ref[r], pair)
    lane = lanes(rows)
    high = lax.shift_right_logical(pair, 7)
    low = lax.bitwise_and(pair, 127)
    extra = jnp.where(lane == 0, high, jnp.where(lane == 1, low, 0)).astype(F32)
    image_two = jnp.concatenate([image_low, image_low], axis=0).astype(BF16)
    text_two = jnp.concatenate([text_low, text_low], axis=0).astype(BF16)
    extra_two = jnp.concatenate([extra, extra], axis=0).astype(BF16)
    step = 2 * rows
    for k in range(image_out.shape[0] // step):
        image_out[k * step : (k + 1) * step, :width] = image_two
        image_out[k * step : (k + 1) * step, width:] = extra_two
    for k in range(text_out.shape[0] // step):
        text_out[k * step : (k + 1) * step, :] = text_two


def split_stats(lane, first, values):
    out = jnp.zeros(lane.shape, F32)
    for n, value in enumerate(values):
        high = value.astype(BF16).astype(F32)
        out = jnp.where(lane == first + n, high, out)
        out = jnp.where(lane == first + 3 + n, value - high, out)
    return out


def score_kernel(own_rows, core_size, row_size, mine_ref, other_ref, text_ref, log_scale_ref, bias_ref, text_out, mine_out, other_out):
    text = text_ref[...]
    count, width = text.shape
    scale = jnp.exp(jnp.zeros((8, 128), F32) + log_scale_ref[0])[0:1, 0:1]
    shift = bias_ref[0]
    base = (lax.axis_index("txt") * (row_size * core_size) + lax.axis_index("core")) * own_rows
    column = lax.broadcasted_iota(jnp.int32, (1, count), 1)
    column = base + (column // own_rows) * (own_rows * core_size) + column % own_rows
    column = column.astype(F32)
    text_part = None
    along_text = None
    totals = None
    for source, target in ((mine_ref, mine_out), (other_ref, other_out)):
        image = source[:, :width]
        extra = source[:, width:].astype(F32)
        pair = extra[:, 0:1] * 128.0 + extra[:, 1:2]
        cosine = lax.dot_general(image, text, (((1,), (1,)), ((), ())), preferred_element_type=F32)
        scaled = scale * cosine
        logits = scaled + shift
        match = pair == column
        arg = jnp.where(match, -logits, logits)
        small = jnp.exp(-jnp.abs(arg))
        inverse = 1.0 / (1.0 + small)
        prob = jnp.where(arg >= 0, inverse, small * inverse)
        dlogit = jnp.where(match, -prob, prob)
        loss = jnp.maximum(arg, 0.0) + jnp.log1p(small)
        low = dlogit.astype(BF16)
        product = low.astype(F32) * scaled
        sums = [
            jnp.sum(loss, axis=(0, 1), keepdims=True),
            jnp.sum(dlogit, axis=(0, 1), keepdims=True),
            jnp.sum(dlogit * scaled, axis=(0, 1), keepdims=True),
        ]
        totals = sums if totals is None else [a + b for a, b in zip(totals, sums)]
        along = jnp.sum(product, axis=1, keepdims=True)
        part = scale * jnp.dot(low, text, preferred_element_type=F32)
        target[:, :width] = part - along * image.astype(F32)
        target[:, width:] = jnp.where(lanes(image.shape[0]) == 0, along, 0.0)
        piece = lax.dot_general(low, image, (((0,), (0,)), ((), ())), preferred_element_type=F32)
        text_part = piece if text_part is None else text_part + piece
        sums = jnp.sum(product, axis=0, keepdims=True)
        along_text = sums if along_text is None else along_text + sums
    along_text = jnp.broadcast_to(along_text, (128, count)).T
    along_text = along_text.astype(BF16).astype(F32)
    text_out[:, :width] = (scale * text_part - along_text[:, 0:1] * text.astype(F32)).astype(BF16)
    lane = lanes(count)
    stats = split_stats(lane, 1, [jnp.broadcast_to(t, lane.shape) for t in totals])
    text_out[:, width:] = jnp.where(lane == 0, along_text, stats).astype(BF16)


def merge_stats(extra, rows):
    peers = extra.shape[0] // rows
    total = jnp.sum(extra.reshape(peers, rows, EXTRA), axis=0)
    return [total[0:1, n : n + 1] + total[0:1, n + 3 : n + 4] for n in (1, 2, 3)]


def join_kernel(own_rows, mine_ref, other_ref, text_extra_ref, out_ref):
    total = mine_ref[...] + other_ref[...]
    width = mine_ref.shape[1] - EXTRA
    out_ref[:, :width] = total[:, :width].astype(BF16)
    lane = lanes(mine_ref.shape[0])
    stats = merge_stats(text_extra_ref[...].astype(F32), own_rows)
    stats = split_stats(lane, 1, [jnp.broadcast_to(t, lane.shape) for t in stats])
    out_ref[:, width:] = jnp.where(lane == 0, total[:, width:], stats).astype(BF16)


def finish(parts_ref, embed_ref, grad_out):
    rows, width = embed_ref.shape
    peers = parts_ref.shape[0] // rows
    total = jnp.sum(parts_ref[...].astype(F32).reshape(peers, rows, width + EXTRA), axis=0)
    unit, norm = unit_and_norm(embed_ref[...])
    grad = total[:, :width] + total[:, width : width + 1] * unit.astype(BF16).astype(F32)
    grad_out[...] = (grad - unit * jnp.sum(unit * grad, axis=1, keepdims=True)) / norm


def stats_kernel(own_rows, extra_ref, out_ref):
    stats = merge_stats(extra_ref[...].astype(F32), own_rows)
    lane = lanes(8)
    out = jnp.zeros(lane.shape, F32)
    for n, value in enumerate(stats):
        out = jnp.where(lane == n, value, out)
    out_ref[...] = out


def shape(*dims, dtype=BF16):
    return jax.ShapeDtypeStruct(dims, dtype)


def per_device(image_embed, text_embed, pair_index, log_scale, bias):
    own_rows, width = image_embed.shape
    row_size, core_size, txt_size = (lax.axis_size(a) for a in ("row", "core", "txt"))
    wide = width + EXTRA
    image_count, text_count = txt_size * own_rows, row_size * own_rows
    image_send, text_send = pl.pallas_call(
        pack_kernel,
        out_shape=(shape(image_count, wide), shape(text_count, width)),
        in_specs=[VMEM, VMEM, SMEM],
        out_specs=(VMEM, VMEM),
    )(image_embed, text_embed, pair_index)
    mine = lax.all_to_all(image_send, "txt", 0, 0, tiled=True)
    text = lax.all_to_all(text_send, "row", 0, 0, tiled=True)
    swap = [(0, 1), (1, 0)]
    other = lax.ppermute(mine, "core", swap)
    text_parts, image_own, image_away = pl.pallas_call(
        functools.partial(score_kernel, own_rows, core_size, row_size),
        out_shape=(
            shape(text_count, wide),
            shape(image_count, wide, dtype=F32),
            shape(image_count, wide, dtype=F32),
        ),
        in_specs=[VMEM, VMEM, VMEM, SMEM, SMEM],
        out_specs=(VMEM, VMEM, VMEM),
    )(mine, other, text, log_scale, bias)
    text_back = lax.all_to_all(text_parts, "row", 0, 0, tiled=True)
    image_came = lax.ppermute(image_away, "core", swap)
    last = width // EXTRA
    image_parts = pl.pallas_call(
        functools.partial(join_kernel, own_rows),
        out_shape=shape(image_count, wide),
        grid=(1,),
        in_specs=[
            pl.BlockSpec((image_count, wide), lambda i: (0, 0)),
            pl.BlockSpec((image_count, wide), lambda i: (0, 0)),
            pl.BlockSpec((text_count, EXTRA), lambda i: (0, last)),
        ],
        out_specs=pl.BlockSpec((image_count, wide), lambda i: (0, 0)),
    )(image_own, image_came, text_back)
    image_back = lax.all_to_all(image_parts, "txt", 0, 0, tiled=True)
    text_grad = pl.pallas_call(
        finish, out_shape=shape(own_rows, width, dtype=F32), in_specs=[VMEM, VMEM], out_specs=VMEM
    )(text_back, text_embed)
    sums = pl.pallas_call(
        functools.partial(stats_kernel, own_rows),
        out_shape=shape(8, EXTRA, dtype=F32),
        grid=(1,),
        in_specs=[pl.BlockSpec((image_count, EXTRA), lambda i: (0, last))],
        out_specs=pl.BlockSpec((8, EXTRA), lambda i: (0, 0)),
    )(image_back)
    sums_came = lax.ppermute(sums, "core", swap)
    image_grad = pl.pallas_call(
        finish, out_shape=shape(own_rows, width, dtype=F32), in_specs=[VMEM, VMEM], out_specs=VMEM
    )(image_back, image_embed)
    batch = own_rows * row_size * core_size * txt_size
    stats = (sums + sums_came)[0, :3] / batch
    return (image_grad, text_grad, stats)


def solution(mesh):
    img, txt = mesh.shape["img"], mesh.shape["txt"]
    split = Mesh(mesh.devices.reshape(img // 2, 2, txt), ("row", "core", "txt"))
    image_spec = P(("row", "core", "txt"), None)
    text_spec = P(("txt", "row", "core"), None)
    return jax.shard_map(
        per_device,
        mesh=split,
        in_specs=(image_spec, text_spec, P(("row", "core", "txt")), P(), P()),
        out_specs=(image_spec, text_spec, P()),
        check_vma=False,
    )
```

time: 905 us -> 128 us (0.14)
  waiting for transfers between devices: 691 us -> 26.2 us
  blocking collectives: 175 us -> 41.6 us
  starting transfers between devices: 0.12 us -> 41.8 us
  between operations: 17.1 us -> 2.01 us
  Pallas kernels: 0 us -> 13.4 us
  other arithmetic: 11.4 us -> 0.52 us
    unnamed x5 -> x0, waiting for transfers between devices: 622 us -> none
    psum x1 -> x0, blocking collectives: 115 us -> none  [per_device(): lax.psum((sums[0], sums[1], sums[2]), ('img', 'txt'))]
    all_gather x1 -> x0, waiting for transfers between devices: 68.5 us -> none  [per_device(): text_block = lax.all_gather(text_low, 'img', axis=0, tiled=True)]
    all_to_all x0 -> x2, blocking collectives: none -> 41.6 us  [the longest x1 25.4 us: per_device(): mine = lax.all_to_all(image_send, 'txt', 0, 0, tiled=True)]
    all_gather x1 -> x0, blocking collectives: 40.6 us -> none  [per_device(): lax.all_gather(image_low, 'txt', axis=0, tiled=True)]
    all_to_all x0 -> x2, starting transfers between devices: none -> 28.4 us  [the longest x1 21.3 us: per_device(): text = lax.all_to_all(text_send, 'row', 0, 0, tiled=True)]
    all_to_all x0 -> x2, waiting for transfers between devices: none -> 24.4 us  [the longest x1 12.6 us: per_device(): text_back = lax.all_to_all(text_parts, 'row', 0, 0, tiled=True)]
    unnamed x1 -> x0, blocking collectives: 18.9 us -> none
  transfers between devices with their start and end apart: 3 -> 5, of which waited for: 3 -> 3; matrix products, arithmetic and copies ran while one was open for 1% -> 0% of each run, Pallas kernels for 0% -> 3%
where the time goes in v1:
time: 128 us; the launch traced here: 127 us
  starting transfers between devices  41.8 us (33%)
  blocking collectives  41.6 us (32%)
  waiting for transfers between devices  26.2 us (20%)
  Pallas kernels  13.4 us (10%)
  between operations  2.01 us (2%)
  local copies, waits for them, and re-layouts  1.7 us (1%)
    all_to_all x1, blocking collectives, per_device(): mine = lax.all_to_all(image_send, 'txt', 0, 0, tiled=True)  25.4 us
    all_to_all x1, starting transfers between devices, per_device(): text = lax.all_to_all(text_send, 'row', 0, 0, tiled=True)  21.3 us
    all_to_all x1, blocking collectives, per_device(): image_back = lax.all_to_all(image_parts, 'txt', 0, 0, tiled=True)  16.2 us
    all_to_all x1, waiting for transfers between devices, per_device(): text_back = lax.all_to_all(text_parts, 'row', 0, 0, tiled=True)  12.6 us
    all_to_all x1, waiting for transfers between devices, per_device(): text = lax.all_to_all(text_send, 'row', 0, 0, tiled=True)  11.9 us
    ppermute x1, starting transfers between devices, per_device(): sums_came = lax.ppermute(sums, 'core', swap)  7.13 us
    all_to_all x1, starting transfers between devices, per_device(): text_back = lax.all_to_all(text_parts, 'row', 0, 0, tiled=True)  7.1 us
    pallas_call x1, Pallas kernels, per_device(): pl.pallas_call(functools.partial(score_kernel, own_rows, core_size, row_s...  4.05 us
  transfers between devices with their start and end apart: 5, of which 3 were waited for; matrix products, arithmetic and copies ran while one was open for 0% of the time, Pallas kernels for 3%

profile of v1, /device:TPU:1, one launch (start us, length us, event | category | flops | bytes accessed | tf_op | source)
XLA Modules:
  0.0 127.1 jit_solution(4887225793390033944)
XLA Ops:
  0.6 1.8 %shard_map.76 = (bf16[128,1280]{1,0:T(8,128)(2,1)}, bf16[256,1152]{1,0:T(8,128)(2,1)}) custom-call(bf16[8,1152]{1,0:T(8,128)(2,1)} %embed_ref.2, bf16[8,1152]{1,0:T(8,128)(2,1)} %embed_ref.3, s32[8]{0:T(128)} %pair_ref.1), custom_call_target="tpu_custom_call" | custom-call | tf_op jit(solution)/shard_map/pallas_call | solution.py:153
  2.5 25.4 %all_to_all.44 = bf16[16,8,1280]{2,1,0:T(8,128)(2,1)S(1)} all-to-all(bf16[16,8,1280]{2,1,0:T(8,128)(2,1)} %bitcast.19), channel_id=1, replica_groups=mesh['row'=32,'core'=2,'txt'=16] {'txt'}, dimensions={0} | all-to-all | bytes 655360 | tf_op jit(solution)/shard_map/all_to_all | solution.py:159
  27.9 0.0 copy-start.2
  27.9 21.3 %all-to-all-start.1 = ((bf16[32,8,1152]{2,1,0:T(8,128)(2,1)}), bf16[32,8,1152]{2,1,0:T(8,128)(2,1)S(1)}, u32[]{:S(2)}, u32[]{:S(2)}) async-start(bf16[32,8,1152]{2,1,0:T(8,128)(2,1)} %bitcast.2), calls=%async_computation.1 | async-start | bytes 1179648 | tf_op jit(solution)/shard_map/all_to_all | solution.py:160
  49.2 0.0 copy-done.2
  49.2 3.0 %collective-permute-start = (bf16[128,1280]{1,0:T(8,128)(2,1)S(1)}, bf16[128,1280]{1,0:T(8,128)(2,1)S(1)}, u32[]{:S(2)}, u32[]{:S(2)}) collective-permute-start(bf16[128,1280]{1,0:T(8,128)(2,1)S(1)} %bitcast.16), channel_id=1, source_target_pairs={{0,16},{16,0},{1,17},{17,1},{2,18},{18,2},{3,19},{19,3},{4,20},{20... | collective-permute-start | bytes 983048 | tf_op jit(solution)/shard_map/ppermute | solution.py:162
  53.6 0.0 collective-permute-done.other_ref
  53.6 0.0 copy-start.4
  53.6 11.9 %all-to-all-done.1 = bf16[32,8,1152]{2,1,0:T(8,128)(2,1)S(1)} async-done(((bf16[32,8,1152]{2,1,0:T(8,128)(2,1)}), bf16[32,8,1152]{2,1,0:T(8,128)(2,1)S(1)}, u32[]{:S(2)}, u32[]{:S(2)}) %all-to-all-start.1) | async-done | bytes 589856 | tf_op jit(solution)/shard_map/all_to_all | solution.py:160
  65.4 0.0 copy-start.1
  65.4 0.0 copy-done.4
  65.4 0.8 copy-done.1
  66.3 4.0 %shard_map.77 = (bf16[256,1280]{1,0:T(8,128)(2,1)}, f32[128,1280]{1,0:T(8,128)}, f32[128,1280]{1,0:T(8,128)}) custom-call(bf16[128,1280]{1,0:T(8,128)(2,1)} %bitcast.17, bf16[128,1280]{1,0:T(8,128)(2,1)} %copy-done.4, bf16[256,1152]{1,0:T(8,128)(2,1)} %bitcast.14, f32[1]{0:T(128)S(6)} %copy.8.log_scale_ref, f32[1]{0:T(128)S(6)} %copy.9.bias_ref), custom_call_target="tpu_custom_call" | custom-call | tf_op jit(solution)/shard_map/pallas_call | solution.py:163
  70.3 0.0 copy-start.6
  70.3 7.1 %all-to-all-start.2 = ((bf16[32,8,1280]{2,1,0:T(8,128)(2,1)}), bf16[32,8,1280]{2,1,0:T(8,128)(2,1)S(1)}, u32[]{:S(2)}, u32[]{:S(2)}) async-start(bf16[32,8,1280]{2,1,0:T(8,128)(2,1)} %bitcast.18), calls=%async_computation.2 | async-start | bytes 1310720 | tf_op jit(solution)/shard_map/all_to_all | solution.py:173
  77.4 0.0 copy-done.6
  77.4 3.2 %collective-permute-start.1 = (f32[128,1280]{1,0:T(8,128)S(1)}, f32[128,1280]{1,0:T(8,128)S(1)}, u32[]{:S(2)}, u32[]{:S(2)}) collective-permute-start(f32[128,1280]{1,0:T(8,128)S(1)} %copy-done.6), channel_id=1, source_target_pairs={{0,16},{16,0},{1,17},{17,1},{2,18},{18,2},{3,19},{19,3},{4,20},{20... | collective-permute-start | bytes 1966088 | tf_op jit(solution)/shard_map/ppermute | solution.py:174
  80.7 1.7 %collective-permute-done.1.other_ref = f32[128,1280]{1,0:T(8,128)S(1)} collective-permute-done((f32[128,1280]{1,0:T(8,128)S(1)}, f32[128,1280]{1,0:T(8,128)S(1)}, u32[]{:S(2)}, u32[]{:S(2)}) %collective-permute-start.1) | collective-permute-done | bytes 655392 | tf_op jit(solution)/shard_map/ppermute | solution.py:174
  82.4 0.0 copy-start.3
  82.4 12.6 %all-to-all-done.2 = bf16[32,8,1280]{2,1,0:T(8,128)(2,1)S(1)} async-done(((bf16[32,8,1280]{2,1,0:T(8,128)(2,1)}), bf16[32,8,1280]{2,1,0:T(8,128)(2,1)S(1)}, u32[]{:S(2)}, u32[]{:S(2)}) %all-to-all-start.2) | async-done | bytes 655392 | tf_op jit(solution)/shard_map/all_to_all | solution.py:173
  95.0 0.0 copy-start
  95.0 0.0 copy-done.3
  95.0 0.9 copy-done
  95.8 2.2 %shard_map.78 = bf16[128,1280]{1,0:T(8,128)(2,1)} custom-call(f32[128,1280]{1,0:T(8,128)} %get-tuple-element.10.mine_ref, f32[128,1280]{1,0:T(8,128)} %copy-done.3, bf16[256,1280]{1,0:T(8,128)(2,1)} %bitcast.10), custom_call_target="tpu_custom_call" | custom-call | tf_op jit(solution)/shard_map/pallas_call | solution.py:176
  98.1 16.2 %all_to_all.45 = bf16[16,8,1280]{2,1,0:T(8,128)(2,1)} all-to-all(bf16[16,8,1280]{2,1,0:T(8,128)(2,1)} %bitcast.15), channel_id=1, replica_groups=mesh['row'=32,'core'=2,'txt'=16] {'txt'}, dimensions={0} | all-to-all | bytes 655360 | tf_op jit(solution)/shard_map/all_to_all | solution.py:187
  114.2 1.5 %shard_map.81 = f32[8,128]{1,0:T(8,128)} custom-call(bf16[128,1280]{1,0:T(8,128)(2,1)} %bitcast.12), custom_call_target="tpu_custom_call" | custom-call | tf_op jit(solution)/shard_map/pallas_call | solution.py:191
  115.8 7.1 %collective-permute-start.2 = (f32[8,128]{1,0:T(8,128)}, f32[8,128]{1,0:T(8,128)S(1)}, u32[]{:S(2)}, u32[]{:S(2)}) collective-permute-start(f32[8,128]{1,0:T(8,128)} %shard_map.81), channel_id=1, source_target_pairs={{0,16},{16,0},{1,17},{17,1},{2,18},{18,2},{3,19},{19,3},{4,20},{20... | collective-permute-start | bytes 12296 | tf_op jit(solution)/shard_map/ppermute | solution.py:198
  122.9 1.9 %shard_map.80 = f32[8,1152]{1,0:T(8,128)} custom-call(bf16[256,1280]{1,0:T(8,128)(2,1)} %bitcast.11, bf16[8,1152]{1,0:T(8,128)(2,1)} %embed_ref.3), custom_call_target="tpu_custom_call" | custom-call | tf_op jit(solution)/shard_map/pallas_call | solution.py:188
  124.8 0.0 copy-start.5
  124.8 1.8 %shard_map.79 = f32[8,1152]{1,0:T(8,128)} custom-call(bf16[128,1280]{1,0:T(8,128)(2,1)} %bitcast.13, bf16[8,1152]{1,0:T(8,128)(2,1)} %embed_ref.2), custom_call_target="tpu_custom_call" | custom-call | tf_op jit(solution)/shard_map/pallas_call | solution.py:199
  126.6 0.0 collective-permute-done.2
  126.6 0.0 copy-done.5
  126.6 0.5 multiply_bitcast_fusion
  (1 shorter events, 0.0 us)
Async XLA Ops:
  27.9 21.3 %copy-start.2 = (bf16[16,8,1280]{2,1,0:T(8,128)(2,1)}, bf16[16,8,1280]{2,1,0:T(8,128)(2,1)S(1)}, u32[]{:S(2)}) copy-start(bf16[16,8,1280]{2,1,0:T(8,128)(2,1)S(1)} %all_to_all.44) | copy-start | bytes 983044
  27.9 37.5 %all-to-all-start.1 = ((bf16[32,8,1152]{2,1,0:T(8,128)(2,1)}), bf16[32,8,1152]{2,1,0:T(8,128)(2,1)S(1)}, u32[]{:S(2)}, u32[]{:S(2)}) async-start(bf16[32,8,1152]{2,1,0:T(8,128)(2,1)} %bitcast.2), calls=%async_computation.1 | async-start | bytes 1179648 | tf_op jit(solution)/shard_map/all_to_all | solution.py:160
  49.2 4.3 %collective-permute-start = (bf16[128,1280]{1,0:T(8,128)(2,1)S(1)}, bf16[128,1280]{1,0:T(8,128)(2,1)S(1)}, u32[]{:S(2)}, u32[]{:S(2)}) collective-permute-start(bf16[128,1280]{1,0:T(8,128)(2,1)S(1)} %bitcast.16), channel_id=1, source_target_pairs={{0,16},{16,0},{1,17},{17,1},{2,18},{18,2},{3,19},{19,3},{4,20},{20... | collective-permute-start | bytes 983048 | tf_op jit(solution)/shard_map/ppermute | solution.py:162
  53.6 11.9 %copy-start.4 = (bf16[128,1280]{1,0:T(8,128)(2,1)}, bf16[128,1280]{1,0:T(8,128)(2,1)S(1)}, u32[]{:S(2)}) copy-start(bf16[128,1280]{1,0:T(8,128)(2,1)S(1)} %collective-permute-done.other_ref) | copy-start | bytes 983044
  65.4 0.8 copy-start.1
  70.3 7.1 %copy-start.6 = (f32[128,1280]{1,0:T(8,128)S(1)}, f32[128,1280]{1,0:T(8,128)}, u32[]{:S(2)}) copy-start(f32[128,1280]{1,0:T(8,128)} %get-tuple-element.11) | copy-start | bytes 1966084
  70.3 24.6 %all-to-all-start.2 = ((bf16[32,8,1280]{2,1,0:T(8,128)(2,1)}), bf16[32,8,1280]{2,1,0:T(8,128)(2,1)S(1)}, u32[]{:S(2)}, u32[]{:S(2)}) async-start(bf16[32,8,1280]{2,1,0:T(8,128)(2,1)} %bitcast.18), calls=%async_computation.2 | async-start | bytes 1310720 | tf_op jit(solution)/shard_map/all_to_all | solution.py:173
  77.4 4.9 %collective-permute-start.1 = (f32[128,1280]{1,0:T(8,128)S(1)}, f32[128,1280]{1,0:T(8,128)S(1)}, u32[]{:S(2)}, u32[]{:S(2)}) collective-permute-start(f32[128,1280]{1,0:T(8,128)S(1)} %copy-done.6), channel_id=1, source_target_pairs={{0,16},{16,0},{1,17},{17,1},{2,18},{18,2},{3,19},{19,3},{4,20},{20... | collective-permute-start | bytes 1966088 | tf_op jit(solution)/shard_map/ppermute | solution.py:174
  82.4 12.6 %copy-start.3 = (f32[128,1280]{1,0:T(8,128)}, f32[128,1280]{1,0:T(8,128)S(1)}, u32[]{:S(2)}) copy-start(f32[128,1280]{1,0:T(8,128)S(1)} %collective-permute-done.1.other_ref) | copy-start | bytes 1966084
  95.0 0.9 copy-start
  115.8 10.9 %collective-permute-start.2 = (f32[8,128]{1,0:T(8,128)}, f32[8,128]{1,0:T(8,128)S(1)}, u32[]{:S(2)}, u32[]{:S(2)}) collective-permute-start(f32[8,128]{1,0:T(8,128)} %shard_map.81), channel_id=1, source_target_pairs={{0,16},{16,0},{1,17},{17,1},{2,18},{18,2},{3,19},{19,3},{4,20},{20... | collective-permute-start | bytes 12296 | tf_op jit(solution)/shard_map/ppermute | solution.py:198
  124.8 1.8 %copy-start.5 = (f32[8,128]{1,0:T(8,128)S(1)}, f32[8,128]{1,0:T(8,128)}, u32[]{:S(2)}) copy-start(f32[8,128]{1,0:T(8,128)} %shard_map.81) | copy-start | bytes 12292

commit v2 on v0

v2 whole, which is shorter than its diff:
```python
import functools
import jax
import jax.numpy as jnp
from jax import lax
from jax.experimental import pallas as pl
from jax.experimental.pallas import tpu as pltpu
from jax.sharding import Mesh, PartitionSpec as P

EPS = 1e-06
EXTRA = 128
F32 = jnp.float32
BF16 = jnp.bfloat16
IMAGE_ORDER = ("z", "x1", "x0", "core", "xh", "y")
TEXT_ORDER = ("xh", "y", "z", "x1", "x0", "core")
TEXT_GROUP = ("z", "x1", "xh")
VMEM = pl.BlockSpec(memory_space=pltpu.VMEM)
SMEM = pl.BlockSpec(memory_space=pltpu.SMEM)


def unit_and_norm(rows):
    values = rows.astype(F32)
    norm = jnp.sqrt(jnp.sum(values * values, axis=1, keepdims=True) + EPS)
    return values / norm, norm


def lanes(rows):
    return lax.broadcasted_iota(jnp.int32, (rows, EXTRA), 1)


def pack_kernel(image_ref, text_ref, pair_ref, image_out, text_out, image_unit, image_norm, text_unit, text_norm):
    rows, width = image_ref.shape
    image_unit[...], image_norm[...] = unit_and_norm(image_ref[...])
    text_unit[...], text_norm[...] = unit_and_norm(text_ref[...])
    row = lax.broadcasted_iota(jnp.int32, (rows, EXTRA), 0)
    pair = jnp.zeros((rows, EXTRA), jnp.int32)
    for r in range(rows):
        pair = jnp.where(row == r, pair_ref[r], pair)
    lane = lanes(rows)
    high = lax.shift_right_logical(pair, 7)
    low = lax.bitwise_and(pair, 127)
    extra = jnp.where(lane == 0, high, jnp.where(lane == 1, low, 0)).astype(F32)
    image_two = jnp.concatenate([image_unit[...]] * 2, axis=0).astype(BF16)
    text_two = jnp.concatenate([text_unit[...]] * 2, axis=0).astype(BF16)
    extra_two = jnp.concatenate([extra] * 2, axis=0).astype(BF16)
    step = 2 * rows
    for k in range(image_out.shape[0] // step):
        image_out[k * step : (k + 1) * step, :width] = image_two
        image_out[k * step : (k + 1) * step, width:] = extra_two
    for k in range(text_out.shape[0] // step):
        text_out[k * step : (k + 1) * step, :] = text_two


def split_stats(lane, first, values):
    out = jnp.zeros(lane.shape, F32)
    for n, value in enumerate(values):
        high = value.astype(BF16).astype(F32)
        out = jnp.where(lane == first + n, high, out)
        out = jnp.where(lane == first + 3 + n, value - high, out)
    return out


def text_columns(own_rows, sizes, count):
    place = lax.broadcasted_iota(jnp.int32, (1, count), 1)
    peer, row = place // own_rows, place % own_rows
    index = {a: lax.axis_index(a) for a in ("x0", "core", "y")}
    index["xh"] = peer % sizes["xh"]
    index["x1"] = (peer // sizes["xh"]) % sizes["x1"]
    index["z"] = peer // (sizes["xh"] * sizes["x1"])
    owner = 0
    for a in TEXT_ORDER:
        owner = owner * sizes[a] + index[a]
    return owner * own_rows + row


def score_kernel(own_rows, sizes, piece_refs, text_ref, log_scale_ref, bias_ref, text_out, stay_out, away_out):
    text = text_ref[...]
    count, width = text.shape
    scale = jnp.exp(jnp.zeros((8, 128), F32) + log_scale_ref[0])[0:1, 0:1]
    column = text_columns(own_rows, sizes, count).astype(F32)
    image = jnp.concatenate([r[:, :width] for r in piece_refs], axis=0)
    extra = jnp.concatenate([r[:, width:] for r in piece_refs], axis=0).astype(F32)
    pair = extra[:, 0:1] * 128.0 + extra[:, 1:2]
    cosine = lax.dot_general(image, text, (((1,), (1,)), ((), ())), preferred_element_type=F32)
    scaled = scale * cosine
    logits = scaled + bias_ref[0]
    match = pair == column
    arg = jnp.where(match, -logits, logits)
    small = jnp.exp(-jnp.abs(arg))
    inverse = 1.0 / (1.0 + small)
    prob = jnp.where(arg >= 0, inverse, small * inverse)
    dlogit = jnp.where(match, -prob, prob)
    loss = jnp.maximum(arg, 0.0) + jnp.log1p(small)
    low = dlogit.astype(BF16)
    product = low.astype(F32) * scaled
    totals = [jnp.sum(v, axis=(0, 1), keepdims=True) for v in (loss, dlogit, dlogit * scaled)]
    along_image = jnp.sum(product, axis=1, keepdims=True)
    along_text = jnp.broadcast_to(jnp.sum(product, axis=0, keepdims=True), (128, count)).T
    along_text = along_text.astype(BF16).astype(F32)
    low_turned = dlogit.T.astype(BF16)
    half = image.shape[0] // 2
    block = width // 3
    for first in range(0, width, block):
        cols = slice(first, first + block)
        part = scale * jnp.dot(low, text[:, cols], preferred_element_type=F32)
        part = part - along_image * image[:, cols].astype(F32)
        stay_out[:, cols] = part[:half]
        away_out[:, cols] = part[half:]
        part = scale * jnp.dot(low_turned, image[:, cols], preferred_element_type=F32)
        text_out[:, cols] = (part - along_text[:, 0:1] * text[:, cols].astype(F32)).astype(BF16)
    kept = jnp.where(lanes(2 * half) == 0, along_image, 0.0)
    stay_out[:, width:] = kept[:half]
    away_out[:, width:] = kept[half:]
    lane = lanes(count)
    stats = split_stats(lane, 1, [jnp.broadcast_to(t, lane.shape) for t in totals])
    text_out[:, width:] = jnp.where(lane == 0, along_text, stats).astype(BF16)


def merge_stats(extra, rows):
    peers = extra.shape[0] // rows
    total = jnp.sum(extra.reshape(peers, rows, EXTRA), axis=0)
    return [total[0:1, n : n + 1] + total[0:1, n + 3 : n + 4] for n in (1, 2, 3)]


def add_kernel(stay_ref, came_ref, keep_out, send_out):
    half = keep_out.shape[0]
    keep_out[...] = stay_ref[:half, :] + came_ref[:half, :]
    send_out[...] = stay_ref[half:, :] + came_ref[half:, :]


def join_kernel(own_rows, keep_ref, came_ref, text_back_ref, out_ref):
    width = keep_ref.shape[1] - EXTRA
    out_ref[:, :width] = (keep_ref[:, :width] + came_ref[:, :width]).astype(BF16)
    lane = lanes(keep_ref.shape[0])
    stats = merge_stats(text_back_ref[:, width:].astype(F32), own_rows)
    stats = split_stats(lane, 1, [jnp.broadcast_to(t, lane.shape) for t in stats])
    along = keep_ref[:, width:] + came_ref[:, width:]
    out_ref[:, width:] = jnp.where(lane == 0, along, stats).astype(BF16)


def finish_kernel(parts_ref, unit_ref, norm_ref, grad_out):
    rows, width = unit_ref.shape
    peers = parts_ref.shape[0] // rows
    total = jnp.sum(parts_ref[...].astype(F32).reshape(peers, rows, width + EXTRA), axis=0)
    unit = unit_ref[...]
    grad = total[:, :width] + total[:, width : width + 1] * unit.astype(BF16).astype(F32)
    grad_out[...] = (grad - unit * jnp.sum(unit * grad, axis=1, keepdims=True)) / norm_ref[...]


def stats_kernel(own_rows, parts_ref, out_ref):
    width = parts_ref.shape[1] - EXTRA
    lane = lanes(8)
    out = jnp.zeros(lane.shape, F32)
    for n, value in enumerate(merge_stats(parts_ref[:, width:].astype(F32), own_rows)):
        out = jnp.where(lane == n, value, out)
    out_ref[...] = jnp.broadcast_to(out[None], out_ref.shape)


def shape(*dims, dtype=BF16):
    return jax.ShapeDtypeStruct(dims, dtype)


def call(kernel, outs, *args, scalars=0, flops=0):
    size = sum(a.size * a.dtype.itemsize for a in args)
    return pl.pallas_call(
        kernel,
        out_shape=outs,
        in_specs=[VMEM] * (len(args) - scalars) + [SMEM] * scalars,
        out_specs=jax.tree.map(lambda _: VMEM, outs),
        cost_estimate=pl.CostEstimate(flops=flops, bytes_accessed=4 * size, transcendentals=0),
        compiler_params=pltpu.CompilerParams(vmem_limit_bytes=40 * 1024 * 1024),
    )(*args)


def per_device(image_embed, text_embed, pair_index, log_scale, bias):
    own_rows, width = image_embed.shape
    sizes = {a: lax.axis_size(a) for a in IMAGE_ORDER}
    wide = width + EXTRA
    row_count = sizes["y"] * own_rows
    text_count = own_rows
    for a in TEXT_GROUP:
        text_count *= sizes[a]
    unit_shape, norm_shape = shape(own_rows, width, dtype=F32), shape(own_rows, 1, dtype=F32)
    image_send, text_send, image_unit, image_norm, text_unit, text_norm = call(
        pack_kernel,
        (shape(row_count, wide), shape(text_count, width), unit_shape, norm_shape, unit_shape, norm_shape),
        image_embed, text_embed, pair_index, scalars=1,
    )
    swap = [(0, 1), (1, 0)]
    piece = lax.all_to_all(image_send, "y", 0, 0, tiled=True)
    text = lax.all_to_all(text_send, TEXT_GROUP, 0, 0, tiled=True)
    piece_x = lax.ppermute(piece, "x0", swap)
    piece_core = lax.ppermute(piece, "core", swap)
    piece_both = lax.ppermute(piece_x, "core", swap)

    def score(a, b, c, d, text_ref, *rest):
        score_kernel(own_rows, sizes, (a, b, c, d), text_ref, *rest)

    text_parts, stay, away = call(
        score,
        (shape(text_count, wide), shape(2 * row_count, wide, dtype=F32), shape(2 * row_count, wide, dtype=F32)),
        piece, piece_x, piece_core, piece_both, text, log_scale, bias,
        scalars=2, flops=3 * 2 * 4 * row_count * text_count * width,
    )
    text_back = lax.all_to_all(text_parts, TEXT_GROUP, 0, 0, tiled=True)
    came = lax.ppermute(away, "core", swap)
    quarter = shape(row_count, wide, dtype=F32)
    keep, send = call(add_kernel, (quarter, quarter), stay, came)
    came_x = lax.ppermute(send, "x0", swap)
    image_parts = call(
        functools.partial(join_kernel, own_rows), shape(row_count, wide), keep, came_x, text_back
    )
    image_back = lax.all_to_all(image_parts, "y", 0, 0, tiled=True)
    text_grad = call(finish_kernel, unit_shape, text_back, text_unit, text_norm)
    four = sizes["x0"] * sizes["core"]
    sums = call(functools.partial(stats_kernel, own_rows), shape(four, 8, EXTRA, dtype=F32), image_back)
    sums = lax.all_to_all(sums, ("x0", "core"), 0, 0, tiled=True)
    image_grad = call(finish_kernel, unit_shape, image_back, image_unit, image_norm)
    batch = own_rows
    for a in IMAGE_ORDER:
        batch *= sizes[a]
    stats = jnp.sum(sums[:, 0, :3], axis=0) / batch
    return (image_grad, text_grad, stats)


def solution(mesh):
    img, txt = mesh.shape["img"], mesh.shape["txt"]
    parts = (img // 8, 2, 2, 2, 2, txt // 2)
    split = Mesh(mesh.devices.reshape(parts), IMAGE_ORDER)
    image_spec, text_spec = P(IMAGE_ORDER, None), P(TEXT_ORDER, None)
    return jax.shard_map(
        per_device,
        mesh=split,
        in_specs=(image_spec, text_spec, P(IMAGE_ORDER), P(), P()),
        out_specs=(image_spec, text_spec, P()),
        check_vma=False,
    )
```

time: 905 us -> 122 us (0.13)
  waiting for transfers between devices: 691 us -> 26.7 us
  blocking collectives: 175 us -> 27 us
  starting transfers between devices: 0.12 us -> 56.6 us
  between operations: 17.1 us -> 2.03 us
  other arithmetic: 11.4 us -> 0.54 us
    unnamed x5 -> x0, waiting for transfers between devices: 622 us -> none
    psum x1 -> x0, blocking collectives: 115 us -> none  [per_device(): lax.psum((sums[0], sums[1], sums[2]), ('img', 'txt'))]
    all_gather x1 -> x0, waiting for transfers between devices: 68.5 us -> none  [per_device(): text_block = lax.all_gather(text_low, 'img', axis=0, tiled=True)]
    all_gather x1 -> x0, blocking collectives: 40.6 us -> none  [per_device(): lax.all_gather(image_low, 'txt', axis=0, tiled=True)]
    all_to_all x0 -> x3, starting transfers between devices: none -> 39.7 us  [the longest x1 21.6 us: per_device(): text = lax.all_to_all(text_send, TEXT_GROUP, 0, 0, tiled=True)]
    all_to_all x0 -> x2, blocking collectives: none -> 27 us  [the longest x1 16.2 us: per_device(): piece = lax.all_to_all(image_send, 'y', 0, 0, tiled=True)]
    ppermute x0 -> x5, waiting for transfers between devices: none -> 25.2 us  [the longest x1 15.9 us: per_device(): came_x = lax.ppermute(send, 'x0', swap)]
    unnamed x1 -> x0, blocking collectives: 18.9 us -> none
  transfers between devices with their start and end apart: 3 -> 8, of which waited for: 3 -> 4; matrix products, arithmetic and copies ran while one was open for 1% -> 0% of each run, Pallas kernels for 0% -> 1%
where the time goes in v2:
time: 122 us; the launch traced here: 121 us
  starting transfers between devices  56.6 us (46%)
  blocking collectives  27 us (22%)
  waiting for transfers between devices  26.7 us (22%)
  Pallas kernels  6.46 us (5%)
  local copies, waits for them, and re-layouts  2.09 us (2%)
  between operations  2.03 us (2%)
    all_to_all x1, starting transfers between devices, per_device(): text = lax.all_to_all(text_send, TEXT_GROUP, 0, 0, tiled=True)  21.6 us
    all_to_all x1, blocking collectives, per_device(): piece = lax.all_to_all(image_send, 'y', 0, 0, tiled=True)  16.2 us
    ppermute x1, waiting for transfers between devices, per_device(): came_x = lax.ppermute(send, 'x0', swap)  15.9 us
    all_to_all x1, starting transfers between devices, per_device(): text_back = lax.all_to_all(text_parts, TEXT_GROUP, 0, 0, tiled=True)  11.7 us
    all_to_all x1, blocking collectives, per_device(): image_back = lax.all_to_all(image_parts, 'y', 0, 0, tiled=True)  10.9 us
    ppermute x1, waiting for transfers between devices, per_device(): piece_x = lax.ppermute(piece, 'x0', swap)  7.52 us
    pallas_call x7, Pallas kernels, call(): pl.pallas_call(kernel, out_shape=outs, in_specs=[VMEM] * (len(args) - sca...  6.46 us
    all_to_all x1, starting transfers between devices, per_device(): sums = lax.all_to_all(sums, ('x0', 'core'), 0, 0, tiled=True)  6.4 us
  transfers between devices with their start and end apart: 8, of which 4 were waited for; matrix products, arithmetic and copies ran while one was open for 0% of the time, Pallas kernels for 1%

profile of v2, /device:TPU:1, one launch (start us, length us, event | category | flops | bytes accessed | tf_op | source)
XLA Modules:
  0.0 121.4 jit_solution(15075839978863017023)
XLA Ops:
  0.6 0.0 copy-start
  0.6 0.7 copy-done
  1.4 0.0 copy-start.1
  1.4 0.7 copy-done.1
  2.1 0.0 copy-start.2
  2.1 0.7 copy-done.2
  2.7 1.5 %shard_map.76 = (bf16[64,1280]{1,0:T(8,128)(2,1)S(1)}, bf16[256,1152]{1,0:T(8,128)(2,1)}, f32[8,1152]{1,0:T(8,128)S(1)}, f32[8,1]{1,0:T(8,128)S(1)}, f32[8,1152]{1,0:T(8,128)S(1)}, /*index=5*/f32[8,1]{1,0:T(8,128)S(1)}) custom-call(bf16[8,1152]{1,0:T(8,128)(2,1)S(1)} %copy-done, bf16[8,1152]{1,0:T(8,128)(2,1)S(1)} %copy-done.1, s32[8]{0:T(128)S(1)} %copy-done.2), custom_call_target="tpu_custom_call" | custom-call | bytes 147584 | tf_op jit(solution)/shard_map/pallas_call | solution.py:164
  4.2 16.2 %all_to_all.49 = bf16[8,8,1280]{2,1,0:T(8,128)(2,1)S(1)} all-to-all(bf16[8,8,1280]{2,1,0:T(8,128)(2,1)S(1)} %bitcast.17), channel_id=1, replica_groups=mesh['z'=8,'x1'=2,'x0'=2,'core'=2,'xh'=2,'y'=8] {'y'}, dimensions={0} | all-to-all | bytes 327680 | tf_op jit(solution)/shard_map/all_to_all | solution.py:189
  20.4 21.6 %all-to-all-start.1 = ((bf16[32,8,1152]{2,1,0:T(8,128)(2,1)}), bf16[32,8,1152]{2,1,0:T(8,128)(2,1)S(1)}, u32[]{:S(2)}, u32[]{:S(2)}) async-start(bf16[32,8,1152]{2,1,0:T(8,128)(2,1)} %bitcast.2), calls=%async_computation.1 | async-start | bytes 1179648 | tf_op jit(solution)/shard_map/all_to_all | solution.py:190
  42.0 2.2 %collective-permute-start = (bf16[64,1280]{1,0:T(8,128)(2,1)S(1)}, bf16[64,1280]{1,0:T(8,128)(2,1)S(1)}, u32[]{:S(2)}, u32[]{:S(2)}) collective-permute-start(bf16[64,1280]{1,0:T(8,128)(2,1)S(1)} %bitcast.14), channel_id=1, source_target_pairs={{0,32},{32,0},{1,33},{33,1},{2,34},{34,2},{3,35},{35,3},{4,36},{36... | collective-permute-start | bytes 491528 | tf_op jit(solution)/shard_map/ppermute | solution.py:191
  44.2 5.0 %collective-permute-start.1 = (bf16[64,1280]{1,0:T(8,128)(2,1)S(1)}, bf16[64,1280]{1,0:T(8,128)(2,1)S(1)}, u32[]{:S(2)}, u32[]{:S(2)}) collective-permute-start(bf16[64,1280]{1,0:T(8,128)(2,1)S(1)} %bitcast.15), channel_id=1, source_target_pairs={{0,16},{16,0},{1,17},{17,1},{2,18},{18,2},{3,19},{19,3},{4,20},{20... | collective-permute-start | bytes 491528 | tf_op jit(solution)/shard_map/ppermute | solution.py:192
  49.3 7.5 %collective-permute-done.b = bf16[64,1280]{1,0:T(8,128)(2,1)S(1)} collective-permute-done((bf16[64,1280]{1,0:T(8,128)(2,1)S(1)}, bf16[64,1280]{1,0:T(8,128)(2,1)S(1)}, u32[]{:S(2)}, u32[]{:S(2)}) %collective-permute-start) | collective-permute-done | bytes 163872 | tf_op jit(solution)/shard_map/ppermute | solution.py:191
  56.8 5.2 %collective-permute-start.2 = (bf16[64,1280]{1,0:T(8,128)(2,1)S(1)}, bf16[64,1280]{1,0:T(8,128)(2,1)S(1)}, u32[]{:S(2)}, u32[]{:S(2)}) collective-permute-start(bf16[64,1280]{1,0:T(8,128)(2,1)S(1)} %collective-permute-done.b), channel_id=1, source_target_pairs={{0,16},{16,0},{1,17},{17,1},{2,18},{18,2},{3,19},{19,3},{4,20},{20... | collective-permute-start | bytes 491528 | tf_op jit(solution)/shard_map/ppermute | solution.py:193
  63.3 0.0 collective-permute-done.1.c
  63.3 0.0 collective-permute-done.2.d
  63.3 0.0 all-to-all-done.1
  63.3 2.3 %shard_map.77 = (bf16[256,1280]{1,0:T(8,128)(2,1)}, f32[128,1280]{1,0:T(8,128)S(1)}, f32[128,1280]{1,0:T(8,128)S(1)}) custom-call(bf16[64,1280]{1,0:T(8,128)(2,1)S(1)} %bitcast.16, bf16[64,1280]{1,0:T(8,128)(2,1)S(1)} %collective-permute-done.b, bf16[64,1280]{1,0:T(8,128)(2,1)S(1)} %collective-permute-done.1.c, ...), custom_call_target="tpu_custom_call" | custom-call | flops 452984832 | bytes 4980768 | tf_op jit(solution)/shard_map/pallas_call | solution.py:164
  65.6 11.7 %all-to-all-start.2 = ((bf16[32,8,1280]{2,1,0:T(8,128)(2,1)}), bf16[32,8,1280]{2,1,0:T(8,128)(2,1)S(1)}, u32[]{:S(2)}, u32[]{:S(2)}) async-start(bf16[32,8,1280]{2,1,0:T(8,128)(2,1)} %bitcast.4), calls=%async_computation.2 | async-start | bytes 1310720 | tf_op jit(solution)/shard_map/all_to_all | solution.py:204
  77.3 2.2 %collective-permute-start.3 = (f32[128,1280]{1,0:T(8,128)S(1)}, f32[128,1280]{1,0:T(8,128)S(1)}, u32[]{:S(2)}, u32[]{:S(2)}) collective-permute-start(f32[128,1280]{1,0:T(8,128)S(1)} %get-tuple-element.17), channel_id=1, source_target_pairs={{0,16},{16,0},{1,17},{17,1},{2,18},{18,2},{3,19},{19,3},{4,20},{20... | collective-permute-start | bytes 1966088 | tf_op jit(solution)/shard_map/ppermute | solution.py:205
  79.6 1.7 %collective-permute-done.3.came_ref = f32[128,1280]{1,0:T(8,128)S(1)} collective-permute-done((f32[128,1280]{1,0:T(8,128)S(1)}, f32[128,1280]{1,0:T(8,128)S(1)}, u32[]{:S(2)}, u32[]{:S(2)}) %collective-permute-start.3) | collective-permute-done | bytes 655392 | tf_op jit(solution)/shard_map/ppermute | solution.py:205
  81.3 0.1 shard_map.78
  81.4 2.2 %collective-permute-start.4 = (f32[64,1280]{1,0:T(8,128)S(1)}, f32[64,1280]{1,0:T(8,128)S(1)}, u32[]{:S(2)}, u32[]{:S(2)}) collective-permute-start(f32[64,1280]{1,0:T(8,128)S(1)} %get-tuple-element.19), channel_id=1, source_target_pairs={{0,32},{32,0},{1,33},{33,1},{2,34},{34,2},{3,35},{35,3},{4,36},{36... | collective-permute-start | bytes 983048 | tf_op jit(solution)/shard_map/ppermute | solution.py:208
  83.6 15.9 %collective-permute-done.4.came_ref = f32[64,1280]{1,0:T(8,128)S(1)} collective-permute-done((f32[64,1280]{1,0:T(8,128)S(1)}, f32[64,1280]{1,0:T(8,128)S(1)}, u32[]{:S(2)}, u32[]{:S(2)}) %collective-permute-start.4) | collective-permute-done | bytes 327712 | tf_op jit(solution)/shard_map/ppermute | solution.py:208
  99.5 0.0 all-to-all-done.2
  99.5 0.2 shard_map.79
  99.7 10.9 %all_to_all.50 = bf16[8,8,1280]{2,1,0:T(8,128)(2,1)S(1)} all-to-all(bf16[8,8,1280]{2,1,0:T(8,128)(2,1)S(1)} %bitcast.12), channel_id=1, replica_groups=mesh['z'=8,'x1'=2,'x0'=2,'core'=2,'xh'=2,'y'=8] {'y'}, dimensions={0} | all-to-all | bytes 327680 | tf_op jit(solution)/shard_map/all_to_all | solution.py:212
  110.6 0.8 shard_map.82
  111.4 6.4 %all-to-all-start.4 = ((f32[4,8,128]{2,1,0:T(8,128)}), f32[4,8,128]{2,1,0:T(8,128)S(1)}, u32[]{:S(2)}, u32[]{:S(2)}) async-start(f32[4,8,128]{2,1,0:T(8,128)} %shard_map.82), calls=%async_computation.4 | async-start | bytes 32768 | tf_op jit(solution)/shard_map/all_to_all | solution.py:216
  117.8 0.8 shard_map.81
  118.6 0.8 shard_map.80
  119.4 1.5 %all-to-all-done.4 = f32[4,8,128]{2,1,0:T(8,128)S(1)} async-done(((f32[4,8,128]{2,1,0:T(8,128)}), f32[4,8,128]{2,1,0:T(8,128)S(1)}, u32[]{:S(2)}, u32[]{:S(2)}) %all-to-all-start.4) | async-done | bytes 16416 | tf_op jit(solution)/shard_map/all_to_all | solution.py:216
  120.9 0.5 broadcast_multiply_fusion
  (1 shorter events, 0.0 us)
Async XLA Ops:
  0.6 0.7 copy-start
  1.4 0.7 copy-start.1
  2.1 0.7 copy-start.2
  20.4 42.9 %all-to-all-start.1 = ((bf16[32,8,1152]{2,1,0:T(8,128)(2,1)}), bf16[32,8,1152]{2,1,0:T(8,128)(2,1)S(1)}, u32[]{:S(2)}, u32[]{:S(2)}) async-start(bf16[32,8,1152]{2,1,0:T(8,128)(2,1)} %bitcast.2), calls=%async_computation.1 | async-start | bytes 1179648 | tf_op jit(solution)/shard_map/all_to_all | solution.py:190
  42.0 14.8 %collective-permute-start = (bf16[64,1280]{1,0:T(8,128)(2,1)S(1)}, bf16[64,1280]{1,0:T(8,128)(2,1)S(1)}, u32[]{:S(2)}, u32[]{:S(2)}) collective-permute-start(bf16[64,1280]{1,0:T(8,128)(2,1)S(1)} %bitcast.14), channel_id=1, source_target_pairs={{0,32},{32,0},{1,33},{33,1},{2,34},{34,2},{3,35},{35,3},{4,36},{36... | collective-permute-start | bytes 491528 | tf_op jit(solution)/shard_map/ppermute | solution.py:191
  44.2 19.1 %collective-permute-start.1 = (bf16[64,1280]{1,0:T(8,128)(2,1)S(1)}, bf16[64,1280]{1,0:T(8,128)(2,1)S(1)}, u32[]{:S(2)}, u32[]{:S(2)}) collective-permute-start(bf16[64,1280]{1,0:T(8,128)(2,1)S(1)} %bitcast.15), channel_id=1, source_target_pairs={{0,16},{16,0},{1,17},{17,1},{2,18},{18,2},{3,19},{19,3},{4,20},{20... | collective-permute-start | bytes 491528 | tf_op jit(solution)/shard_map/ppermute | solution.py:192
  56.8 6.5 %collective-permute-start.2 = (bf16[64,1280]{1,0:T(8,128)(2,1)S(1)}, bf16[64,1280]{1,0:T(8,128)(2,1)S(1)}, u32[]{:S(2)}, u32[]{:S(2)}) collective-permute-start(bf16[64,1280]{1,0:T(8,128)(2,1)S(1)} %collective-permute-done.b), channel_id=1, source_target_pairs={{0,16},{16,0},{1,17},{17,1},{2,18},{18,2},{3,19},{19,3},{4,20},{20... | collective-permute-start | bytes 491528 | tf_op jit(solution)/shard_map/ppermute | solution.py:193
  65.6 33.9 %all-to-all-start.2 = ((bf16[32,8,1280]{2,1,0:T(8,128)(2,1)}), bf16[32,8,1280]{2,1,0:T(8,128)(2,1)S(1)}, u32[]{:S(2)}, u32[]{:S(2)}) async-start(bf16[32,8,1280]{2,1,0:T(8,128)(2,1)} %bitcast.4), calls=%async_computation.2 | async-start | bytes 1310720 | tf_op jit(solution)/shard_map/all_to_all | solution.py:204
  77.3 4.0 %collective-permute-start.3 = (f32[128,1280]{1,0:T(8,128)S(1)}, f32[128,1280]{1,0:T(8,128)S(1)}, u32[]{:S(2)}, u32[]{:S(2)}) collective-permute-start(f32[128,1280]{1,0:T(8,128)S(1)} %get-tuple-element.17), channel_id=1, source_target_pairs={{0,16},{16,0},{1,17},{17,1},{2,18},{18,2},{3,19},{19,3},{4,20},{20... | collective-permute-start | bytes 1966088 | tf_op jit(solution)/shard_map/ppermute | solution.py:205
  81.4 18.1 %collective-permute-start.4 = (f32[64,1280]{1,0:T(8,128)S(1)}, f32[64,1280]{1,0:T(8,128)S(1)}, u32[]{:S(2)}, u32[]{:S(2)}) collective-permute-start(f32[64,1280]{1,0:T(8,128)S(1)} %get-tuple-element.19), channel_id=1, source_target_pairs={{0,32},{32,0},{1,33},{33,1},{2,34},{34,2},{3,35},{35,3},{4,36},{36... | collective-permute-start | bytes 983048 | tf_op jit(solution)/shard_map/ppermute | solution.py:208
  111.4 9.5 %all-to-all-start.4 = ((f32[4,8,128]{2,1,0:T(8,128)}), f32[4,8,128]{2,1,0:T(8,128)S(1)}, u32[]{:S(2)}, u32[]{:S(2)}) async-start(f32[4,8,128]{2,1,0:T(8,128)} %shard_map.82), calls=%async_computation.4 | async-start | bytes 32768 | tf_op jit(solution)/shard_map/all_to_all | solution.py:216

commit v3 on v2

--- a/solution.py
+++ b/solution.py
@@ -1,4 +1,5 @@
 import functools
+import math
 import jax
 import jax.numpy as jnp
 from jax import lax
@@ -10,9 +11,11 @@
 EXTRA = 128
 F32 = jnp.float32
 BF16 = jnp.bfloat16
-IMAGE_ORDER = ("z", "x1", "x0", "core", "xh", "y")
-TEXT_ORDER = ("xh", "y", "z", "x1", "x0", "core")
+IMAGE_ORDER = ("z", "x1", "x0", "core", "xh", "yh", "y0")
+TEXT_ORDER = ("xh", "yh", "y0", "z", "x1", "x0", "core")
 TEXT_GROUP = ("z", "x1", "xh")
+IMAGE_GROUP = ("x0", "yh")
+PAIR = "y0"
 VMEM = pl.BlockSpec(memory_space=pltpu.VMEM)
 SMEM = pl.BlockSpec(memory_space=pltpu.SMEM)
 
@@ -62,10 +65,10 @@
 def text_columns(own_rows, sizes, count):
     place = lax.broadcasted_iota(jnp.int32, (1, count), 1)
     peer, row = place // own_rows, place % own_rows
-    index = {a: lax.axis_index(a) for a in ("x0", "core", "y")}
-    index["xh"] = peer % sizes["xh"]
-    index["x1"] = (peer // sizes["xh"]) % sizes["x1"]
-    index["z"] = peer // (sizes["xh"] * sizes["x1"])
+    index = {a: lax.axis_index(a) for a in IMAGE_GROUP + (PAIR, "core")}
+    for a in reversed(TEXT_GROUP):
+        index[a] = peer % sizes[a]
+        peer = peer // sizes[a]
     owner = 0
     for a in TEXT_ORDER:
         owner = owner * sizes[a] + index[a]
@@ -159,7 +162,7 @@
     return jax.ShapeDtypeStruct(dims, dtype)
 
 
-def call(kernel, outs, *args, scalars=0, flops=0):
+def call(kernel, outs, *args, scalars=0, flops=0, limit=40 * 1024 * 1024):
     size = sum(a.size * a.dtype.itemsize for a in args)
     return pl.pallas_call(
         kernel,
@@ -167,7 +170,7 @@
         in_specs=[VMEM] * (len(args) - scalars) + [SMEM] * scalars,
         out_specs=jax.tree.map(lambda _: VMEM, outs),
         cost_estimate=pl.CostEstimate(flops=flops, bytes_accessed=4 * size, transcendentals=0),
-        compiler_params=pltpu.CompilerParams(vmem_limit_bytes=40 * 1024 * 1024),
+        compiler_params=pltpu.CompilerParams(vmem_limit_bytes=limit),
     )(*args)
 
 
@@ -175,22 +178,20 @@
     own_rows, width = image_embed.shape
     sizes = {a: lax.axis_size(a) for a in IMAGE_ORDER}
     wide = width + EXTRA
-    row_count = sizes["y"] * own_rows
-    text_count = own_rows
-    for a in TEXT_GROUP:
-        text_count *= sizes[a]
+    row_count = math.prod(sizes[a] for a in IMAGE_GROUP) * own_rows
+    text_count = math.prod(sizes[a] for a in TEXT_GROUP) * own_rows
     unit_shape, norm_shape = shape(own_rows, width, dtype=F32), shape(own_rows, 1, dtype=F32)
     image_send, text_send, image_unit, image_norm, text_unit, text_norm = call(
         pack_kernel,
         (shape(row_count, wide), shape(text_count, width), unit_shape, norm_shape, unit_shape, norm_shape),
-        image_embed, text_embed, pair_index, scalars=1,
+        image_embed, text_embed, pair_index, scalars=1, limit=None,
     )
     swap = [(0, 1), (1, 0)]
-    piece = lax.all_to_all(image_send, "y", 0, 0, tiled=True)
+    piece = lax.all_to_all(image_send, IMAGE_GROUP, 0, 0, tiled=True)
     text = lax.all_to_all(text_send, TEXT_GROUP, 0, 0, tiled=True)
-    piece_x = lax.ppermute(piece, "x0", swap)
+    piece_pair = lax.ppermute(piece, PAIR, swap)
     piece_core = lax.ppermute(piece, "core", swap)
-    piece_both = lax.ppermute(piece_x, "core", swap)
+    piece_both = lax.ppermute(piece_pair, "core", swap)
 
     def score(a, b, c, d, text_ref, *rest):
         score_kernel(own_rows, sizes, (a, b, c, d), text_ref, *rest)
@@ -198,33 +199,31 @@
     text_parts, stay, away = call(
         score,
         (shape(text_count, wide), shape(2 * row_count, wide, dtype=F32), shape(2 * row_count, wide, dtype=F32)),
-        piece, piece_x, piece_core, piece_both, text, log_scale, bias,
+        piece, piece_pair, piece_core, piece_both, text, log_scale, bias,
         scalars=2, flops=3 * 2 * 4 * row_count * text_count * width,
     )
     text_back = lax.all_to_all(text_parts, TEXT_GROUP, 0, 0, tiled=True)
     came = lax.ppermute(away, "core", swap)
     quarter = shape(row_count, wide, dtype=F32)
     keep, send = call(add_kernel, (quarter, quarter), stay, came)
-    came_x = lax.ppermute(send, "x0", swap)
+    came_pair = lax.ppermute(send, PAIR, swap)
     image_parts = call(
-        functools.partial(join_kernel, own_rows), shape(row_count, wide), keep, came_x, text_back
-    )
-    image_back = lax.all_to_all(image_parts, "y", 0, 0, tiled=True)
+        functools.partial(join_kernel, own_rows), shape(row_count, wide), keep, came_pair, text_back
+    )
+    image_back = lax.all_to_all(image_parts, IMAGE_GROUP, 0, 0, tiled=True)
     text_grad = call(finish_kernel, unit_shape, text_back, text_unit, text_norm)
-    four = sizes["x0"] * sizes["core"]
+    four = sizes[PAIR] * sizes["core"]
     sums = call(functools.partial(stats_kernel, own_rows), shape(four, 8, EXTRA, dtype=F32), image_back)
-    sums = lax.all_to_all(sums, ("x0", "core"), 0, 0, tiled=True)
+    sums = lax.all_to_all(sums, (PAIR, "core"), 0, 0, tiled=True)
     image_grad = call(finish_kernel, unit_shape, image_back, image_unit, image_norm)
-    batch = own_rows
-    for a in IMAGE_ORDER:
-        batch *= sizes[a]
+    batch = own_rows * math.prod(sizes.values())
     stats = jnp.sum(sums[:, 0, :3], axis=0) / batch
     return (image_grad, text_grad, stats)
 
 
 def solution(mesh):
     img, txt = mesh.shape["img"], mesh.shape["txt"]
-    parts = (img // 8, 2, 2, 2, 2, txt // 2)
+    parts = (img // 8, 2, 2, 2, 2, txt // 4, 2)
     split = Mesh(mesh.devices.reshape(parts), IMAGE_ORDER)
     image_spec, text_spec = P(IMAGE_ORDER, None), P(TEXT_ORDER, None)
     return jax.shard_map(

time: 122 us -> 117 us (0.959)
  blocking collectives: 27 us -> 38.6 us
  waiting for transfers between devices: 26.7 us -> 16.2 us
  starting transfers between devices: 56.6 us -> 52.1 us
  local copies, waits for them, and re-layouts: 2.09 us -> 0.02 us
    ppermute x3, waiting for transfers between devices: 23.4 us -> 8.55 us  [the longest x1 8.55 us: per_device(): came_pair = lax.ppermute(send, PAIR, swap)]
    all_to_all x2, blocking collectives: 27 us -> 38.6 us  [the longest x1 21.6 us: per_device(): image_back = lax.all_to_all(image_parts, IMAGE_GROUP, 0, 0, tiled=True)]
    all_to_all x1, waiting for transfers between devices: 0.01 us -> 4.08 us  [per_device(): text = lax.all_to_all(text_send, TEXT_GROUP, 0, 0, tiled=True)]
    all_to_all x1, starting transfers between devices: 11.7 us -> 8.26 us  [per_device(): text_back = lax.all_to_all(text_parts, TEXT_GROUP, 0, 0, tiled=True)]
    unnamed x6 -> x8, local copies, waits for them, and re-layouts: 2.09 us -> 0.02 us
    ppermute x1, starting transfers between devices: 2.24 us -> 3.8 us  [per_device(): came = lax.ppermute(away, 'core', swap)]
  transfers between devices with their start and end apart: 8 -> 8, of which waited for: 4 -> 5; matrix products, arithmetic and copies ran while one was open for 0% -> 0% of each run, Pallas kernels for 1% -> 1%
where the time goes in v3:
time: 117 us; the launch traced here: 116 us
  starting transfers between devices  52.1 us (45%)
  blocking collectives  38.6 us (33%)
  waiting for transfers between devices  16.2 us (14%)
  Pallas kernels  6.77 us (6%)
  between operations  2.04 us (2%)
    all_to_all x1, blocking collectives, per_device(): image_back = lax.all_to_all(image_parts, IMAGE_GROUP, 0, 0, tiled=True)  21.6 us
    all_to_all x1, starting transfers between devices, per_device(): text = lax.all_to_all(text_send, TEXT_GROUP, 0, 0, tiled=True)  21.1 us
    all_to_all x1, blocking collectives, per_device(): piece = lax.all_to_all(image_send, IMAGE_GROUP, 0, 0, tiled=True)  17 us
    ppermute x1, waiting for transfers between devices, per_device(): came_pair = lax.ppermute(send, PAIR, swap)  8.55 us
    all_to_all x1, starting transfers between devices, per_device(): text_back = lax.all_to_all(text_parts, TEXT_GROUP, 0, 0, tiled=True)  8.26 us
    pallas_call x7, Pallas kernels, call(): pl.pallas_call(kernel, out_shape=outs, in_specs=[VMEM] * (len(args) - sca...  6.77 us
    all_to_all x1, starting transfers between devices, per_device(): sums = lax.all_to_all(sums, (PAIR, 'core'), 0, 0, tiled=True)  5.32 us
    ppermute x1, starting transfers between devices, per_device(): piece_core = lax.ppermute(piece, 'core', swap)  4.69 us
  transfers between devices with their start and end apart: 8, of which 5 were waited for; matrix products, arithmetic and copies ran while one was open for 0% of the time, Pallas kernels for 1%

profile of v3, /device:TPU:1, one launch (start us, length us, event | category | flops | bytes accessed | tf_op | source)
XLA Modules:
  0.0 116.3 jit_solution(10092622073976397598)
XLA Ops:
  0.6 1.8 %shard_map.76 = (bf16[64,1280]{1,0:T(8,128)(2,1)}, bf16[256,1152]{1,0:T(8,128)(2,1)}, f32[8,1152]{1,0:T(8,128)}, f32[8,1]{1,0:T(8,128)}, f32[8,1152]{1,0:T(8,128)}, /*index=5*/f32[8,1]{1,0:T(8,128)}) custom-call(bf16[8,1152]{1,0:T(8,128)(2,1)} %image_ref.1, bf16[8,1152]{1,0:T(8,128)(2,1)} %text_ref.1, s32[8]{0:T(128)} %pair_ref.1), custom_call_target="tpu_custom_call" | custom-call | bytes 147584 | tf_op jit(solution)/shard_map/pallas_call | solution.py:167
  2.5 17.0 %all_to_all.49 = bf16[8,8,1280]{2,1,0:T(8,128)(2,1)S(1)} all-to-all(bf16[8,8,1280]{2,1,0:T(8,128)(2,1)} %bitcast.18), channel_id=1, replica_groups=mesh['z'=8,'x1'=2,'x0'=2,'core'=2,'xh'=2,'yh'=4,'y0'=2] {'x0','yh'}, dimensions={0} | all-to-all | bytes 327680 | tf_op jit(solution)/shard_map/all_to_all | solution.py:190
  19.5 21.1 %all-to-all-start.1 = ((bf16[32,8,1152]{2,1,0:T(8,128)(2,1)}), bf16[32,8,1152]{2,1,0:T(8,128)(2,1)S(1)}, u32[]{:S(2)}, u32[]{:S(2)}) async-start(bf16[32,8,1152]{2,1,0:T(8,128)(2,1)} %bitcast.17), calls=%async_computation.1 | async-start | bytes 1179648 | tf_op jit(solution)/shard_map/all_to_all | solution.py:191
  40.6 2.6 %collective-permute-start = (bf16[64,1280]{1,0:T(8,128)(2,1)S(1)}, bf16[64,1280]{1,0:T(8,128)(2,1)S(1)}, u32[]{:S(2)}, u32[]{:S(2)}) collective-permute-start(bf16[64,1280]{1,0:T(8,128)(2,1)S(1)} %bitcast.14), channel_id=1, source_target_pairs={{0,1},{1,0},{2,3},{3,2},{4,5},{5,4},{6,7},{7,6},{8,9},{9,8},{10,11... | collective-permute-start | bytes 491528 | tf_op jit(solution)/shard_map/ppermute | solution.py:192
  43.2 4.7 %collective-permute-start.1 = (bf16[64,1280]{1,0:T(8,128)(2,1)S(1)}, bf16[64,1280]{1,0:T(8,128)(2,1)S(1)}, u32[]{:S(2)}, u32[]{:S(2)}) collective-permute-start(bf16[64,1280]{1,0:T(8,128)(2,1)S(1)} %bitcast.15), channel_id=1, source_target_pairs={{0,16},{16,0},{1,17},{17,1},{2,18},{18,2},{3,19},{19,3},{4,20},{20... | collective-permute-start | bytes 491528 | tf_op jit(solution)/shard_map/ppermute | solution.py:193
  47.9 0.0 collective-permute-done.b
  47.9 4.0 %collective-permute-start.2 = (bf16[64,1280]{1,0:T(8,128)(2,1)S(1)}, bf16[64,1280]{1,0:T(8,128)(2,1)S(1)}, u32[]{:S(2)}, u32[]{:S(2)}) collective-permute-start(bf16[64,1280]{1,0:T(8,128)(2,1)S(1)} %collective-permute-done.b), channel_id=1, source_target_pairs={{0,16},{16,0},{1,17},{17,1},{2,18},{18,2},{3,19},{19,3},{4,20},{20... | collective-permute-start | bytes 491528 | tf_op jit(solution)/shard_map/ppermute | solution.py:194
  53.3 0.0 collective-permute-done.1.c
  53.3 0.0 collective-permute-done.2.d
  53.3 4.1 %all-to-all-done.1 = bf16[32,8,1152]{2,1,0:T(8,128)(2,1)S(1)} async-done(((bf16[32,8,1152]{2,1,0:T(8,128)(2,1)}), bf16[32,8,1152]{2,1,0:T(8,128)(2,1)S(1)}, u32[]{:S(2)}, u32[]{:S(2)}) %all-to-all-start.1) | async-done | bytes 589856 | tf_op jit(solution)/shard_map/all_to_all | solution.py:191
  57.4 2.3 %shard_map.77 = (bf16[256,1280]{1,0:T(8,128)(2,1)}, f32[128,1280]{1,0:T(8,128)S(1)}, f32[128,1280]{1,0:T(8,128)S(1)}) custom-call(bf16[64,1280]{1,0:T(8,128)(2,1)S(1)} %bitcast.16, bf16[64,1280]{1,0:T(8,128)(2,1)S(1)} %collective-permute-done.b, bf16[64,1280]{1,0:T(8,128)(2,1)S(1)} %collective-permute-done.1.c, ...), custom_call_target="tpu_custom_call" | custom-call | flops 452984832 | bytes 4980768 | tf_op jit(solution)/shard_map/pallas_call | solution.py:167
  59.7 8.3 %all-to-all-start.2 = ((bf16[32,8,1280]{2,1,0:T(8,128)(2,1)}), bf16[32,8,1280]{2,1,0:T(8,128)(2,1)S(1)}, u32[]{:S(2)}, u32[]{:S(2)}) async-start(bf16[32,8,1280]{2,1,0:T(8,128)(2,1)} %bitcast.4), calls=%async_computation.2 | async-start | bytes 1310720 | tf_op jit(solution)/shard_map/all_to_all | solution.py:205
  67.9 3.8 %collective-permute-start.3 = (f32[128,1280]{1,0:T(8,128)S(1)}, f32[128,1280]{1,0:T(8,128)S(1)}, u32[]{:S(2)}, u32[]{:S(2)}) collective-permute-start(f32[128,1280]{1,0:T(8,128)S(1)} %get-tuple-element.17), channel_id=1, source_target_pairs={{0,16},{16,0},{1,17},{17,1},{2,18},{18,2},{3,19},{19,3},{4,20},{20... | collective-permute-start | bytes 1966088 | tf_op jit(solution)/shard_map/ppermute | solution.py:206
  71.7 1.7 %collective-permute-done.3.came_ref = f32[128,1280]{1,0:T(8,128)S(1)} collective-permute-done((f32[128,1280]{1,0:T(8,128)S(1)}, f32[128,1280]{1,0:T(8,128)S(1)}, u32[]{:S(2)}, u32[]{:S(2)}) %collective-permute-start.3) | collective-permute-done | bytes 655392 | tf_op jit(solution)/shard_map/ppermute | solution.py:206
  73.4 0.1 shard_map.78
  73.5 2.3 %collective-permute-start.4 = (f32[64,1280]{1,0:T(8,128)S(1)}, f32[64,1280]{1,0:T(8,128)S(1)}, u32[]{:S(2)}, u32[]{:S(2)}) collective-permute-start(f32[64,1280]{1,0:T(8,128)S(1)} %get-tuple-element.19), channel_id=1, source_target_pairs={{0,1},{1,0},{2,3},{3,2},{4,5},{5,4},{6,7},{7,6},{8,9},{9,8},{10,11... | collective-permute-start | bytes 983048 | tf_op jit(solution)/shard_map/ppermute | solution.py:209
  75.8 8.5 %collective-permute-done.4.came_ref = f32[64,1280]{1,0:T(8,128)S(1)} collective-permute-done((f32[64,1280]{1,0:T(8,128)S(1)}, f32[64,1280]{1,0:T(8,128)S(1)}, u32[]{:S(2)}, u32[]{:S(2)}) %collective-permute-start.4) | collective-permute-done | bytes 327712 | tf_op jit(solution)/shard_map/ppermute | solution.py:209
  84.3 0.4 all-to-all-done.2
  84.7 0.2 shard_map.79
  85.0 21.6 %all_to_all.50 = bf16[8,8,1280]{2,1,0:T(8,128)(2,1)S(1)} all-to-all(bf16[8,8,1280]{2,1,0:T(8,128)(2,1)S(1)} %bitcast.12), channel_id=1, replica_groups=mesh['z'=8,'x1'=2,'x0'=2,'core'=2,'xh'=2,'yh'=4,'y0'=2] {'x0','yh'}, dimensions={0} | all-to-all | bytes 327680 | tf_op jit(solution)/shard_map/all_to_all | solution.py:213
  106.5 0.0 copy-start
  106.5 0.8 shard_map.82
  107.3 0.0 copy-start.3
  107.3 5.3 %all-to-all-start.4 = ((f32[4,8,128]{2,1,0:T(8,128)}), f32[4,8,128]{2,1,0:T(8,128)S(1)}, u32[]{:S(2)}, u32[]{:S(2)}) async-start(f32[4,8,128]{2,1,0:T(8,128)} %shard_map.82), calls=%async_computation.4 | async-start | bytes 32768 | tf_op jit(solution)/shard_map/all_to_all | solution.py:217
  112.6 0.0 copy-done
  112.6 0.0 copy-done.3
  112.6 0.0 copy-start.1
  112.7 0.0 copy-start.2
  112.7 0.8 shard_map.81
  113.5 0.0 copy-done.1
  113.5 0.0 copy-done.2
  113.5 0.8 shard_map.80
  114.3 1.5 %all-to-all-done.4 = f32[4,8,128]{2,1,0:T(8,128)S(1)} async-done(((f32[4,8,128]{2,1,0:T(8,128)}), f32[4,8,128]{2,1,0:T(8,128)S(1)}, u32[]{:S(2)}, u32[]{:S(2)}) %all-to-all-start.4) | async-done | bytes 16416 | tf_op jit(solution)/shard_map/all_to_all | solution.py:217
  115.8 0.5 broadcast_multiply_fusion
  (1 shorter events, 0.0 us)
Async XLA Ops:
  19.5 37.9 %all-to-all-start.1 = ((bf16[32,8,1152]{2,1,0:T(8,128)(2,1)}), bf16[32,8,1152]{2,1,0:T(8,128)(2,1)S(1)}, u32[]{:S(2)}, u32[]{:S(2)}) async-start(bf16[32,8,1152]{2,1,0:T(8,128)(2,1)} %bitcast.17), calls=%async_computation.1 | async-start | bytes 1179648 | tf_op jit(solution)/shard_map/all_to_all | solution.py:191
  40.6 7.3 %collective-permute-start = (bf16[64,1280]{1,0:T(8,128)(2,1)S(1)}, bf16[64,1280]{1,0:T(8,128)(2,1)S(1)}, u32[]{:S(2)}, u32[]{:S(2)}) collective-permute-start(bf16[64,1280]{1,0:T(8,128)(2,1)S(1)} %bitcast.14), channel_id=1, source_target_pairs={{0,1},{1,0},{2,3},{3,2},{4,5},{5,4},{6,7},{7,6},{8,9},{9,8},{10,11... | collective-permute-start | bytes 491528 | tf_op jit(solution)/shard_map/ppermute | solution.py:192
  43.2 10.1 %collective-permute-start.1 = (bf16[64,1280]{1,0:T(8,128)(2,1)S(1)}, bf16[64,1280]{1,0:T(8,128)(2,1)S(1)}, u32[]{:S(2)}, u32[]{:S(2)}) collective-permute-start(bf16[64,1280]{1,0:T(8,128)(2,1)S(1)} %bitcast.15), channel_id=1, source_target_pairs={{0,16},{16,0},{1,17},{17,1},{2,18},{18,2},{3,19},{19,3},{4,20},{20... | collective-permute-start | bytes 491528 | tf_op jit(solution)/shard_map/ppermute | solution.py:193
  47.9 5.4 %collective-permute-start.2 = (bf16[64,1280]{1,0:T(8,128)(2,1)S(1)}, bf16[64,1280]{1,0:T(8,128)(2,1)S(1)}, u32[]{:S(2)}, u32[]{:S(2)}) collective-permute-start(bf16[64,1280]{1,0:T(8,128)(2,1)S(1)} %collective-permute-done.b), channel_id=1, source_target_pairs={{0,16},{16,0},{1,17},{17,1},{2,18},{18,2},{3,19},{19,3},{4,20},{20... | collective-permute-start | bytes 491528 | tf_op jit(solution)/shard_map/ppermute | solution.py:194
  59.7 25.1 %all-to-all-start.2 = ((bf16[32,8,1280]{2,1,0:T(8,128)(2,1)}), bf16[32,8,1280]{2,1,0:T(8,128)(2,1)S(1)}, u32[]{:S(2)}, u32[]{:S(2)}) async-start(bf16[32,8,1280]{2,1,0:T(8,128)(2,1)} %bitcast.4), calls=%async_computation.2 | async-start | bytes 1310720 | tf_op jit(solution)/shard_map/all_to_all | solution.py:205
  67.9 5.5 %collective-permute-start.3 = (f32[128,1280]{1,0:T(8,128)S(1)}, f32[128,1280]{1,0:T(8,128)S(1)}, u32[]{:S(2)}, u32[]{:S(2)}) collective-permute-start(f32[128,1280]{1,0:T(8,128)S(1)} %get-tuple-element.17), channel_id=1, source_target_pairs={{0,16},{16,0},{1,17},{17,1},{2,18},{18,2},{3,19},{19,3},{4,20},{20... | collective-permute-start | bytes 1966088 | tf_op jit(solution)/shard_map/ppermute | solution.py:206
  73.5 10.8 %collective-permute-start.4 = (f32[64,1280]{1,0:T(8,128)S(1)}, f32[64,1280]{1,0:T(8,128)S(1)}, u32[]{:S(2)}, u32[]{:S(2)}) collective-permute-start(f32[64,1280]{1,0:T(8,128)S(1)} %get-tuple-element.19), channel_id=1, source_target_pairs={{0,1},{1,0},{2,3},{3,2},{4,5},{5,4},{6,7},{7,6},{8,9},{9,8},{10,11... | collective-permute-start | bytes 983048 | tf_op jit(solution)/shard_map/ppermute | solution.py:209
  106.5 6.1 %copy-start = (f32[8,1152]{1,0:T(8,128)S(1)}, f32[8,1152]{1,0:T(8,128)}, u32[]{:S(2)}) copy-start(f32[8,1152]{1,0:T(8,128)} %get-tuple-element.23.unit_ref) | copy-start | bytes 110596
  107.3 5.3 %copy-start.3 = (f32[8,1]{1,0:T(8,128)S(1)}, f32[8,1]{1,0:T(8,128)}, u32[]{:S(2)}) copy-start(f32[8,1]{1,0:T(8,128)} %get-tuple-element.24.norm_ref) | copy-start | bytes 100
  107.3 8.5 %all-to-all-start.4 = ((f32[4,8,128]{2,1,0:T(8,128)}), f32[4,8,128]{2,1,0:T(8,128)S(1)}, u32[]{:S(2)}, u32[]{:S(2)}) async-start(f32[4,8,128]{2,1,0:T(8,128)} %shard_map.82), calls=%async_computation.4 | async-start | bytes 32768 | tf_op jit(solution)/shard_map/all_to_all | solution.py:217
  112.6 0.8 copy-start.1
  112.7 0.8 copy-start.2

commit v4 on v3

--- a/solution.py
+++ b/solution.py
@@ -11,11 +11,11 @@
 EXTRA = 128
 F32 = jnp.float32
 BF16 = jnp.bfloat16
-IMAGE_ORDER = ("z", "x1", "x0", "core", "xh", "yh", "y0")
-TEXT_ORDER = ("xh", "yh", "y0", "z", "x1", "x0", "core")
-TEXT_GROUP = ("z", "x1", "xh")
-IMAGE_GROUP = ("x0", "yh")
-PAIR = "y0"
+IMAGE_ORDER = ("zh", "z0", "xl", "core", "xh", "yh", "y0")
+TEXT_ORDER = ("xh", "yh", "y0", "zh", "z0", "xl", "core")
+TEXT_GROUP = ("xh", "xl", "yh")
+IMAGE_GROUP = ("zh", "y0")
+PAIR = "z0"
 VMEM = pl.BlockSpec(memory_space=pltpu.VMEM)
 SMEM = pl.BlockSpec(memory_space=pltpu.SMEM)
 
@@ -223,7 +223,7 @@
 
 def solution(mesh):
     img, txt = mesh.shape["img"], mesh.shape["txt"]
-    parts = (img // 8, 2, 2, 2, 2, txt // 4, 2)
+    parts = (img // 16, 2, 4, 2, 2, txt // 4, 2)
     split = Mesh(mesh.devices.reshape(parts), IMAGE_ORDER)
     image_spec, text_spec = P(IMAGE_ORDER, None), P(TEXT_ORDER, None)
     return jax.shard_map(

time: 117 us -> 112 us (0.957)
  starting transfers between devices: 52.1 us -> 47.5 us
    all_to_all x1, starting transfers between devices: 21.1 us -> 11.7 us  [per_device(): text = lax.all_to_all(text_send, TEXT_GROUP, 0, 0, tiled=True)]
    all_to_all x1, blocking collectives: 21.6 us -> 13 us  [per_device(): image_back = lax.all_to_all(image_parts, IMAGE_GROUP, 0, 0, tiled=True)]
    all_to_all x1, blocking collectives: 17 us -> 25.6 us  [per_device(): piece = lax.all_to_all(image_send, IMAGE_GROUP, 0, 0, tiled=True)]
    all_to_all x1, starting transfers between devices: 5.32 us -> 7.81 us  [per_device(): sums = lax.all_to_all(sums, (PAIR, 'core'), 0, 0, tiled=True)]
    ppermute x1, starting transfers between devices: 2.26 us -> 4.62 us  [per_device(): came_pair = lax.ppermute(send, PAIR, swap)]
    ppermute x1, starting transfers between devices: 2.59 us -> 3.9 us  [per_device(): piece_pair = lax.ppermute(piece, PAIR, swap)]
  transfers between devices with their start and end apart: 8 -> 8, of which waited for: 5 -> 5; matrix products, arithmetic and copies ran while one was open for 0% -> 0% of each run, Pallas kernels for 1% -> 2%
where the time goes in v4:
time: 112 us; the launch traced here: 111 us
  starting transfers between devices  47.5 us (42%)
  blocking collectives  38.6 us (34%)
  waiting for transfers between devices  15.2 us (14%)
  Pallas kernels  6.77 us (6%)
  between operations  2.04 us (2%)
    all_to_all x1, blocking collectives, per_device(): piece = lax.all_to_all(image_send, IMAGE_GROUP, 0, 0, tiled=True)  25.6 us
    all_to_all x1, blocking collectives, per_device(): image_back = lax.all_to_all(image_parts, IMAGE_GROUP, 0, 0, tiled=True)  13 us
    all_to_all x1, starting transfers between devices, per_device(): text = lax.all_to_all(text_send, TEXT_GROUP, 0, 0, tiled=True)  11.7 us
    all_to_all x1, starting transfers between devices, per_device(): text_back = lax.all_to_all(text_parts, TEXT_GROUP, 0, 0, tiled=True)  8 us
    all_to_all x1, starting transfers between devices, per_device(): sums = lax.all_to_all(sums, (PAIR, 'core'), 0, 0, tiled=True)  7.81 us
    ppermute x1, waiting for transfers between devices, per_device(): came_pair = lax.ppermute(send, PAIR, swap)  7.77 us
    pallas_call x7, Pallas kernels, call(): pl.pallas_call(kernel, out_shape=outs, in_specs=[VMEM] * (len(args) - sca...  6.77 us
    ppermute x1, starting transfers between devices, per_device(): came_pair = lax.ppermute(send, PAIR, swap)  4.62 us
  transfers between devices with their start and end apart: 8, of which 5 were waited for; matrix products, arithmetic and copies ran while one was open for 0% of the time, Pallas kernels for 2%

profile of v4, /device:TPU:1, one launch (start us, length us, event | category | flops | bytes accessed | tf_op | source)
XLA Modules:
  0.0 110.6 jit_solution(5787416115633302363)
XLA Ops:
  0.6 1.8 %shard_map.76 = (bf16[64,1280]{1,0:T(8,128)(2,1)}, bf16[256,1152]{1,0:T(8,128)(2,1)}, f32[8,1152]{1,0:T(8,128)}, f32[8,1]{1,0:T(8,128)}, f32[8,1152]{1,0:T(8,128)}, /*index=5*/f32[8,1]{1,0:T(8,128)}) custom-call(bf16[8,1152]{1,0:T(8,128)(2,1)} %image_ref.1, bf16[8,1152]{1,0:T(8,128)(2,1)} %text_ref.1, s32[8]{0:T(128)} %pair_ref.1), custom_call_target="tpu_custom_call" | custom-call | bytes 147584 | tf_op jit(solution)/shard_map/pallas_call | solution.py:167
  2.5 25.6 %all_to_all.49 = bf16[8,8,1280]{2,1,0:T(8,128)(2,1)S(1)} all-to-all(bf16[8,8,1280]{2,1,0:T(8,128)(2,1)} %bitcast.18), channel_id=1, replica_groups=mesh['zh'=4,'z0'=2,'xl'=4,'core'=2,'xh'=2,'yh'=4,'y0'=2] {'zh','y0'}, dimensions={0} | all-to-all | bytes 327680 | tf_op jit(solution)/shard_map/all_to_all | solution.py:190
  28.0 11.7 %all-to-all-start.1 = ((bf16[32,8,1152]{2,1,0:T(8,128)(2,1)}), bf16[32,8,1152]{2,1,0:T(8,128)(2,1)S(1)}, u32[]{:S(2)}, u32[]{:S(2)}) async-start(bf16[32,8,1152]{2,1,0:T(8,128)(2,1)} %bitcast.17), calls=%async_computation.1 | async-start | bytes 1179648 | tf_op jit(solution)/shard_map/all_to_all | solution.py:191
  39.7 3.9 %collective-permute-start = (bf16[64,1280]{1,0:T(8,128)(2,1)S(1)}, bf16[64,1280]{1,0:T(8,128)(2,1)S(1)}, u32[]{:S(2)}, u32[]{:S(2)}) collective-permute-start(bf16[64,1280]{1,0:T(8,128)(2,1)S(1)} %bitcast.14), channel_id=1, source_target_pairs={{0,128},{128,0},{1,129},{129,1},{2,130},{130,2},{3,131},{131,3},{4... | collective-permute-start | bytes 491528 | tf_op jit(solution)/shard_map/ppermute | solution.py:192
  43.6 4.5 %collective-permute-start.1 = (bf16[64,1280]{1,0:T(8,128)(2,1)S(1)}, bf16[64,1280]{1,0:T(8,128)(2,1)S(1)}, u32[]{:S(2)}, u32[]{:S(2)}) collective-permute-start(bf16[64,1280]{1,0:T(8,128)(2,1)S(1)} %bitcast.15), channel_id=1, source_target_pairs={{0,16},{16,0},{1,17},{17,1},{2,18},{18,2},{3,19},{19,3},{4,20},{20... | collective-permute-start | bytes 491528 | tf_op jit(solution)/shard_map/ppermute | solution.py:193
  48.2 0.0 collective-permute-done.b
  48.2 3.3 %collective-permute-start.2 = (bf16[64,1280]{1,0:T(8,128)(2,1)S(1)}, bf16[64,1280]{1,0:T(8,128)(2,1)S(1)}, u32[]{:S(2)}, u32[]{:S(2)}) collective-permute-start(bf16[64,1280]{1,0:T(8,128)(2,1)S(1)} %collective-permute-done.b), channel_id=1, source_target_pairs={{0,16},{16,0},{1,17},{17,1},{2,18},{18,2},{3,19},{19,3},{4,20},{20... | collective-permute-start | bytes 491528 | tf_op jit(solution)/shard_map/ppermute | solution.py:194
  52.8 0.0 collective-permute-done.1.c
  52.8 0.0 collective-permute-done.2.d
  52.8 3.9 %all-to-all-done.1 = bf16[32,8,1152]{2,1,0:T(8,128)(2,1)S(1)} async-done(((bf16[32,8,1152]{2,1,0:T(8,128)(2,1)}), bf16[32,8,1152]{2,1,0:T(8,128)(2,1)S(1)}, u32[]{:S(2)}, u32[]{:S(2)}) %all-to-all-start.1) | async-done | bytes 589856 | tf_op jit(solution)/shard_map/all_to_all | solution.py:191
  56.7 2.3 %shard_map.77 = (bf16[256,1280]{1,0:T(8,128)(2,1)}, f32[128,1280]{1,0:T(8,128)S(1)}, f32[128,1280]{1,0:T(8,128)S(1)}) custom-call(bf16[64,1280]{1,0:T(8,128)(2,1)S(1)} %bitcast.16, bf16[64,1280]{1,0:T(8,128)(2,1)S(1)} %collective-permute-done.b, bf16[64,1280]{1,0:T(8,128)(2,1)S(1)} %collective-permute-done.1.c, ...), custom_call_target="tpu_custom_call" | custom-call | flops 452984832 | bytes 4980768 | tf_op jit(solution)/shard_map/pallas_call | solution.py:167
  59.0 8.0 %all-to-all-start.2 = ((bf16[32,8,1280]{2,1,0:T(8,128)(2,1)}), bf16[32,8,1280]{2,1,0:T(8,128)(2,1)S(1)}, u32[]{:S(2)}, u32[]{:S(2)}) async-start(bf16[32,8,1280]{2,1,0:T(8,128)(2,1)} %bitcast.4), calls=%async_computation.2 | async-start | bytes 1310720 | tf_op jit(solution)/shard_map/all_to_all | solution.py:205
  67.0 3.7 %collective-permute-start.3 = (f32[128,1280]{1,0:T(8,128)S(1)}, f32[128,1280]{1,0:T(8,128)S(1)}, u32[]{:S(2)}, u32[]{:S(2)}) collective-permute-start(f32[128,1280]{1,0:T(8,128)S(1)} %get-tuple-element.17), channel_id=1, source_target_pairs={{0,16},{16,0},{1,17},{17,1},{2,18},{18,2},{3,19},{19,3},{4,20},{20... | collective-permute-start | bytes 1966088 | tf_op jit(solution)/shard_map/ppermute | solution.py:206
  70.7 1.7 %collective-permute-done.3.came_ref = f32[128,1280]{1,0:T(8,128)S(1)} collective-permute-done((f32[128,1280]{1,0:T(8,128)S(1)}, f32[128,1280]{1,0:T(8,128)S(1)}, u32[]{:S(2)}, u32[]{:S(2)}) %collective-permute-start.3) | collective-permute-done | bytes 655392 | tf_op jit(solution)/shard_map/ppermute | solution.py:206
  72.4 0.1 shard_map.78
  72.5 4.6 %collective-permute-start.4 = (f32[64,1280]{1,0:T(8,128)S(1)}, f32[64,1280]{1,0:T(8,128)S(1)}, u32[]{:S(2)}, u32[]{:S(2)}) collective-permute-start(f32[64,1280]{1,0:T(8,128)S(1)} %get-tuple-element.19), channel_id=1, source_target_pairs={{0,128},{128,0},{1,129},{129,1},{2,130},{130,2},{3,131},{131,3},{4... | collective-permute-start | bytes 983048 | tf_op jit(solution)/shard_map/ppermute | solution.py:209
  77.1 7.8 %collective-permute-done.4.came_ref = f32[64,1280]{1,0:T(8,128)S(1)} collective-permute-done((f32[64,1280]{1,0:T(8,128)S(1)}, f32[64,1280]{1,0:T(8,128)S(1)}, u32[]{:S(2)}, u32[]{:S(2)}) %collective-permute-start.4) | collective-permute-done | bytes 327712 | tf_op jit(solution)/shard_map/ppermute | solution.py:209
  84.9 0.3 all-to-all-done.2
  85.1 0.2 shard_map.79
  85.4 13.0 %all_to_all.50 = bf16[8,8,1280]{2,1,0:T(8,128)(2,1)S(1)} all-to-all(bf16[8,8,1280]{2,1,0:T(8,128)(2,1)S(1)} %bitcast.12), channel_id=1, replica_groups=mesh['zh'=4,'z0'=2,'xl'=4,'core'=2,'xh'=2,'yh'=4,'y0'=2] {'zh','y0'}, dimensions={0} | all-to-all | bytes 327680 | tf_op jit(solution)/shard_map/all_to_all | solution.py:213
  98.3 0.0 copy-start
  98.3 0.8 shard_map.82
  99.1 0.0 copy-start.3
  99.1 7.8 %all-to-all-start.4 = ((f32[4,8,128]{2,1,0:T(8,128)}), f32[4,8,128]{2,1,0:T(8,128)S(1)}, u32[]{:S(2)}, u32[]{:S(2)}) async-start(f32[4,8,128]{2,1,0:T(8,128)} %shard_map.82), calls=%async_computation.4 | async-start | bytes 32768 | tf_op jit(solution)/shard_map/all_to_all | solution.py:217
  106.9 0.0 copy-done
  106.9 0.0 copy-done.3
  106.9 0.0 copy-start.1
  106.9 0.0 copy-start.2
  106.9 0.8 shard_map.81
  107.8 0.0 copy-done.1
  107.8 0.0 copy-done.2
  107.8 0.8 shard_map.80
  108.6 1.5 %all-to-all-done.4 = f32[4,8,128]{2,1,0:T(8,128)S(1)} async-done(((f32[4,8,128]{2,1,0:T(8,128)}), f32[4,8,128]{2,1,0:T(8,128)S(1)}, u32[]{:S(2)}, u32[]{:S(2)}) %all-to-all-start.4) | async-done | bytes 16416 | tf_op jit(solution)/shard_map/all_to_all | solution.py:217
  110.1 0.5 broadcast_multiply_fusion
  (1 shorter events, 0.0 us)
Async XLA Ops:
  28.0 28.7 %all-to-all-start.1 = ((bf16[32,8,1152]{2,1,0:T(8,128)(2,1)}), bf16[32,8,1152]{2,1,0:T(8,128)(2,1)S(1)}, u32[]{:S(2)}, u32[]{:S(2)}) async-start(bf16[32,8,1152]{2,1,0:T(8,128)(2,1)} %bitcast.17), calls=%async_computation.1 | async-start | bytes 1179648 | tf_op jit(solution)/shard_map/all_to_all | solution.py:191
  39.7 8.5 %collective-permute-start = (bf16[64,1280]{1,0:T(8,128)(2,1)S(1)}, bf16[64,1280]{1,0:T(8,128)(2,1)S(1)}, u32[]{:S(2)}, u32[]{:S(2)}) collective-permute-start(bf16[64,1280]{1,0:T(8,128)(2,1)S(1)} %bitcast.14), channel_id=1, source_target_pairs={{0,128},{128,0},{1,129},{129,1},{2,130},{130,2},{3,131},{131,3},{4... | collective-permute-start | bytes 491528 | tf_op jit(solution)/shard_map/ppermute | solution.py:192
  43.6 9.1 %collective-permute-start.1 = (bf16[64,1280]{1,0:T(8,128)(2,1)S(1)}, bf16[64,1280]{1,0:T(8,128)(2,1)S(1)}, u32[]{:S(2)}, u32[]{:S(2)}) collective-permute-start(bf16[64,1280]{1,0:T(8,128)(2,1)S(1)} %bitcast.15), channel_id=1, source_target_pairs={{0,16},{16,0},{1,17},{17,1},{2,18},{18,2},{3,19},{19,3},{4,20},{20... | collective-permute-start | bytes 491528 | tf_op jit(solution)/shard_map/ppermute | solution.py:193
  48.2 4.6 %collective-permute-start.2 = (bf16[64,1280]{1,0:T(8,128)(2,1)S(1)}, bf16[64,1280]{1,0:T(8,128)(2,1)S(1)}, u32[]{:S(2)}, u32[]{:S(2)}) collective-permute-start(bf16[64,1280]{1,0:T(8,128)(2,1)S(1)} %collective-permute-done.b), channel_id=1, source_target_pairs={{0,16},{16,0},{1,17},{17,1},{2,18},{18,2},{3,19},{19,3},{4,20},{20... | collective-permute-start | bytes 491528 | tf_op jit(solution)/shard_map/ppermute | solution.py:194
  59.0 26.2 %all-to-all-start.2 = ((bf16[32,8,1280]{2,1,0:T(8,128)(2,1)}), bf16[32,8,1280]{2,1,0:T(8,128)(2,1)S(1)}, u32[]{:S(2)}, u32[]{:S(2)}) async-start(bf16[32,8,1280]{2,1,0:T(8,128)(2,1)} %bitcast.4), calls=%async_computation.2 | async-start | bytes 1310720 | tf_op jit(solution)/shard_map/all_to_all | solution.py:205
  67.0 5.4 %collective-permute-start.3 = (f32[128,1280]{1,0:T(8,128)S(1)}, f32[128,1280]{1,0:T(8,128)S(1)}, u32[]{:S(2)}, u32[]{:S(2)}) collective-permute-start(f32[128,1280]{1,0:T(8,128)S(1)} %get-tuple-element.17), channel_id=1, source_target_pairs={{0,16},{16,0},{1,17},{17,1},{2,18},{18,2},{3,19},{19,3},{4,20},{20... | collective-permute-start | bytes 1966088 | tf_op jit(solution)/shard_map/ppermute | solution.py:206
  72.5 12.4 %collective-permute-start.4 = (f32[64,1280]{1,0:T(8,128)S(1)}, f32[64,1280]{1,0:T(8,128)S(1)}, u32[]{:S(2)}, u32[]{:S(2)}) collective-permute-start(f32[64,1280]{1,0:T(8,128)S(1)} %get-tuple-element.19), channel_id=1, source_target_pairs={{0,128},{128,0},{1,129},{129,1},{2,130},{130,2},{3,131},{131,3},{4... | collective-permute-start | bytes 983048 | tf_op jit(solution)/shard_map/ppermute | solution.py:209
  98.3 8.6 %copy-start = (f32[8,1152]{1,0:T(8,128)S(1)}, f32[8,1152]{1,0:T(8,128)}, u32[]{:S(2)}) copy-start(f32[8,1152]{1,0:T(8,128)} %get-tuple-element.23.unit_ref) | copy-start | bytes 110596
  99.1 7.8 %copy-start.3 = (f32[8,1]{1,0:T(8,128)S(1)}, f32[8,1]{1,0:T(8,128)}, u32[]{:S(2)}) copy-start(f32[8,1]{1,0:T(8,128)} %get-tuple-element.24.norm_ref) | copy-start | bytes 100
  99.1 10.9 %all-to-all-start.4 = ((f32[4,8,128]{2,1,0:T(8,128)}), f32[4,8,128]{2,1,0:T(8,128)S(1)}, u32[]{:S(2)}, u32[]{:S(2)}) async-start(f32[4,8,128]{2,1,0:T(8,128)} %shard_map.82), calls=%async_computation.4 | async-start | bytes 32768 | tf_op jit(solution)/shard_map/all_to_all | solution.py:217
  106.9 0.8 copy-start.1
  106.9 0.8 copy-start.2

commit v5 on v4

--- a/solution.py
+++ b/solution.py
@@ -30,10 +30,9 @@
     return lax.broadcasted_iota(jnp.int32, (rows, EXTRA), 1)
 
 
-def pack_kernel(image_ref, text_ref, pair_ref, image_out, text_out, image_unit, image_norm, text_unit, text_norm):
+def pack_image_kernel(image_ref, pair_ref, image_out, image_unit, image_norm):
     rows, width = image_ref.shape
     image_unit[...], image_norm[...] = unit_and_norm(image_ref[...])
-    text_unit[...], text_norm[...] = unit_and_norm(text_ref[...])
     row = lax.broadcasted_iota(jnp.int32, (rows, EXTRA), 0)
     pair = jnp.zeros((rows, EXTRA), jnp.int32)
     for r in range(rows):
@@ -43,12 +42,17 @@
     low = lax.bitwise_and(pair, 127)
     extra = jnp.where(lane == 0, high, jnp.where(lane == 1, low, 0)).astype(F32)
     image_two = jnp.concatenate([image_unit[...]] * 2, axis=0).astype(BF16)
-    text_two = jnp.concatenate([text_unit[...]] * 2, axis=0).astype(BF16)
     extra_two = jnp.concatenate([extra] * 2, axis=0).astype(BF16)
     step = 2 * rows
     for k in range(image_out.shape[0] // step):
         image_out[k * step : (k + 1) * step, :width] = image_two
         image_out[k * step : (k + 1) * step, width:] = extra_two
+
+
+def pack_text_kernel(text_ref, text_out, text_unit, text_norm):
+    text_unit[...], text_norm[...] = unit_and_norm(text_ref[...])
+    text_two = jnp.concatenate([text_unit[...]] * 2, axis=0).astype(BF16)
+    step = text_two.shape[0]
     for k in range(text_out.shape[0] // step):
         text_out[k * step : (k + 1) * step, :] = text_two
 
@@ -75,13 +79,21 @@
     return owner * own_rows + row
 
 
-def score_kernel(own_rows, sizes, piece_refs, text_ref, log_scale_ref, bias_ref, text_out, stay_out, away_out):
+def stacked(piece_refs, cols):
+    return jnp.concatenate([r[:, cols] for r in piece_refs], axis=0)
+
+
+def scale_of(log_scale_ref):
+    return jnp.exp(jnp.zeros((8, 128), F32) + log_scale_ref[0])[0:1, 0:1]
+
+
+def score_kernel(own_rows, sizes, piece_refs, text_ref, log_scale_ref, bias_ref, text_out, low_out, along_out):
     text = text_ref[...]
     count, width = text.shape
-    scale = jnp.exp(jnp.zeros((8, 128), F32) + log_scale_ref[0])[0:1, 0:1]
+    scale = scale_of(log_scale_ref)
     column = text_columns(own_rows, sizes, count).astype(F32)
-    image = jnp.concatenate([r[:, :width] for r in piece_refs], axis=0)
-    extra = jnp.concatenate([r[:, width:] for r in piece_refs], axis=0).astype(F32)
+    image = stacked(piece_refs, slice(0, width))
+    extra = stacked(piece_refs, slice(width, width + EXTRA)).astype(F32)
     pair = extra[:, 0:1] * 128.0 + extra[:, 1:2]
     cosine = lax.dot_general(image, text, (((1,), (1,)), ((), ())), preferred_element_type=F32)
     scaled = scale * cosine
@@ -96,26 +108,37 @@
     low = dlogit.astype(BF16)
     product = low.astype(F32) * scaled
     totals = [jnp.sum(v, axis=(0, 1), keepdims=True) for v in (loss, dlogit, dlogit * scaled)]
+    low_out[...] = low
     along_image = jnp.sum(product, axis=1, keepdims=True)
+    along_out[...] = jnp.where(lanes(image.shape[0]) == 0, along_image, 0.0)
     along_text = jnp.broadcast_to(jnp.sum(product, axis=0, keepdims=True), (128, count)).T
     along_text = along_text.astype(BF16).astype(F32)
     low_turned = dlogit.T.astype(BF16)
-    half = image.shape[0] // 2
     block = width // 3
     for first in range(0, width, block):
         cols = slice(first, first + block)
-        part = scale * jnp.dot(low, text[:, cols], preferred_element_type=F32)
-        part = part - along_image * image[:, cols].astype(F32)
-        stay_out[:, cols] = part[:half]
-        away_out[:, cols] = part[half:]
         part = scale * jnp.dot(low_turned, image[:, cols], preferred_element_type=F32)
         text_out[:, cols] = (part - along_text[:, 0:1] * text[:, cols].astype(F32)).astype(BF16)
-    kept = jnp.where(lanes(2 * half) == 0, along_image, 0.0)
-    stay_out[:, width:] = kept[:half]
-    away_out[:, width:] = kept[half:]
     lane = lanes(count)
     stats = split_stats(lane, 1, [jnp.broadcast_to(t, lane.shape) for t in totals])
     text_out[:, width:] = jnp.where(lane == 0, along_text, stats).astype(BF16)
+
+
+def image_kernel(piece_refs, text_ref, low_ref, along_ref, log_scale_ref, stay_out, away_out):
+    width = text_ref.shape[1]
+    scale = scale_of(log_scale_ref)
+    half = low_ref.shape[0] // 2
+    for target, pieces, rows in (
+        (away_out, piece_refs[2:], slice(half, 2 * half)),
+        (stay_out, piece_refs[:2], slice(0, half)),
+    ):
+        low, along = low_ref[rows, :], along_ref[rows, :]
+        block = width // 3
+        for first in range(0, width, block):
+            cols = slice(first, first + block)
+            part = scale * jnp.dot(low, text_ref[:, cols], preferred_element_type=F32)
+            target[:, cols] = part - along[:, 0:1] * stacked(pieces, cols).astype(F32)
+        target[:, width:] = along
 
 
 def merge_stats(extra, rows):
@@ -127,16 +150,16 @@
 def add_kernel(stay_ref, came_ref, keep_out, send_out):
     half = keep_out.shape[0]
     keep_out[...] = stay_ref[:half, :] + came_ref[:half, :]
-    send_out[...] = stay_ref[half:, :] + came_ref[half:, :]
+    send_out[...] = (stay_ref[half:, :] + came_ref[half:, :]).astype(BF16)
 
 
 def join_kernel(own_rows, keep_ref, came_ref, text_back_ref, out_ref):
     width = keep_ref.shape[1] - EXTRA
-    out_ref[:, :width] = (keep_ref[:, :width] + came_ref[:, :width]).astype(BF16)
+    out_ref[:, :width] = (keep_ref[:, :width] + came_ref[:, :width].astype(F32)).astype(BF16)
     lane = lanes(keep_ref.shape[0])
     stats = merge_stats(text_back_ref[:, width:].astype(F32), own_rows)
     stats = split_stats(lane, 1, [jnp.broadcast_to(t, lane.shape) for t in stats])
-    along = keep_ref[:, width:] + came_ref[:, width:]
+    along = keep_ref[:, width:] + came_ref[:, width:].astype(F32)
     out_ref[:, width:] = jnp.where(lane == 0, along, stats).astype(BF16)
 
 
@@ -149,12 +172,12 @@
     grad_out[...] = (grad - unit * jnp.sum(unit * grad, axis=1, keepdims=True)) / norm_ref[...]
 
 
-def stats_kernel(own_rows, parts_ref, out_ref):
+def stats_kernel(own_rows, batch, parts_ref, out_ref):
     width = parts_ref.shape[1] - EXTRA
     lane = lanes(8)
     out = jnp.zeros(lane.shape, F32)
     for n, value in enumerate(merge_stats(parts_ref[:, width:].astype(F32), own_rows)):
-        out = jnp.where(lane == n, value, out)
+        out = jnp.where(lane == n, value / batch, out)
     out_ref[...] = jnp.broadcast_to(out[None], out_ref.shape)
 
 
@@ -181,31 +204,40 @@
     row_count = math.prod(sizes[a] for a in IMAGE_GROUP) * own_rows
     text_count = math.prod(sizes[a] for a in TEXT_GROUP) * own_rows
     unit_shape, norm_shape = shape(own_rows, width, dtype=F32), shape(own_rows, 1, dtype=F32)
-    image_send, text_send, image_unit, image_norm, text_unit, text_norm = call(
-        pack_kernel,
-        (shape(row_count, wide), shape(text_count, width), unit_shape, norm_shape, unit_shape, norm_shape),
-        image_embed, text_embed, pair_index, scalars=1, limit=None,
-    )
-    swap = [(0, 1), (1, 0)]
+    image_send, image_unit, image_norm = call(
+        pack_image_kernel, (shape(row_count, wide), unit_shape, norm_shape),
+        image_embed, pair_index, scalars=1, limit=None,
+    )
+    text_send, text_unit, text_norm = call(
+        pack_text_kernel, (shape(text_count, width), unit_shape, norm_shape), text_embed, limit=None
+    )
     piece = lax.all_to_all(image_send, IMAGE_GROUP, 0, 0, tiled=True)
     text = lax.all_to_all(text_send, TEXT_GROUP, 0, 0, tiled=True)
+    swap = [(0, 1), (1, 0)]
     piece_pair = lax.ppermute(piece, PAIR, swap)
     piece_core = lax.ppermute(piece, "core", swap)
     piece_both = lax.ppermute(piece_pair, "core", swap)
 
-    def score(a, b, c, d, text_ref, *rest):
-        score_kernel(own_rows, sizes, (a, b, c, d), text_ref, *rest)
-
-    text_parts, stay, away = call(
+    def score(a, b, c, d, *rest):
+        score_kernel(own_rows, sizes, (a, b, c, d), *rest)
+
+    def image_partials(a, b, c, d, *rest):
+        image_kernel((a, b, c, d), *rest)
+
+    pieces = (piece, piece_pair, piece_core, piece_both)
+    work = 2 * 4 * row_count * text_count * width
+    text_parts, low, along = call(
         score,
-        (shape(text_count, wide), shape(2 * row_count, wide, dtype=F32), shape(2 * row_count, wide, dtype=F32)),
-        piece, piece_pair, piece_core, piece_both, text, log_scale, bias,
-        scalars=2, flops=3 * 2 * 4 * row_count * text_count * width,
+        (shape(text_count, wide), shape(4 * row_count, text_count), shape(4 * row_count, EXTRA, dtype=F32)),
+        *pieces, text, log_scale, bias, scalars=2, flops=2 * work,
     )
     text_back = lax.all_to_all(text_parts, TEXT_GROUP, 0, 0, tiled=True)
+    half = shape(2 * row_count, wide, dtype=F32)
+    stay, away = call(image_partials, (half, half), *pieces, text, low, along, log_scale, scalars=1, flops=work)
     came = lax.ppermute(away, "core", swap)
-    quarter = shape(row_count, wide, dtype=F32)
-    keep, send = call(add_kernel, (quarter, quarter), stay, came)
+    keep, send = call(
+        add_kernel, (shape(row_count, wide, dtype=F32), shape(row_count, wide)), stay, came
+    )
     came_pair = lax.ppermute(send, PAIR, swap)
     image_parts = call(
         functools.partial(join_kernel, own_rows), shape(row_count, wide), keep, came_pair, text_back
@@ -213,11 +245,11 @@
     image_back = lax.all_to_all(image_parts, IMAGE_GROUP, 0, 0, tiled=True)
     text_grad = call(finish_kernel, unit_shape, text_back, text_unit, text_norm)
     four = sizes[PAIR] * sizes["core"]
-    sums = call(functools.partial(stats_kernel, own_rows), shape(four, 8, EXTRA, dtype=F32), image_back)
+    batch = own_rows * math.prod(sizes.values())
+    sums = call(functools.partial(stats_kernel, own_rows, batch), shape(four, 8, EXTRA, dtype=F32), image_back)
     sums = lax.all_to_all(sums, (PAIR, "core"), 0, 0, tiled=True)
     image_grad = call(finish_kernel, unit_shape, image_back, image_unit, image_norm)
-    batch = own_rows * math.prod(sizes.values())
-    stats = jnp.sum(sums[:, 0, :3], axis=0) / batch
+    stats = jnp.sum(sums[:, 0, :3], axis=0)
     return (image_grad, text_grad, stats)
 
 

time: 112 us -> 111 us (level)
  blocking collectives: 38.6 us -> 13 us
  starting transfers between devices: 47.5 us -> 65 us
  waiting for transfers between devices: 15.2 us -> 21.2 us
  Pallas kernels: 6.77 us -> 8.45 us
    all_to_all x1 -> x0, blocking collectives: 25.6 us -> none  [per_device(): piece = lax.all_to_all(image_send, IMAGE_GROUP, 0, 0, tiled=True)]
    all_to_all x0 -> x1, starting transfers between devices: none -> 17.4 us  [per_device(): piece = lax.all_to_all(image_send, IMAGE_GROUP, 0, 0, tiled=True)]
    all_to_all x0 -> x1, waiting for transfers between devices: none -> 6.45 us  [per_device(): piece = lax.all_to_all(image_send, IMAGE_GROUP, 0, 0, tiled=True)]
    ppermute x1, waiting for transfers between devices: 7.77 us -> 4.26 us  [per_device(): came_pair = lax.ppermute(send, PAIR, swap)]
    all_to_all x1, waiting for transfers between devices: 0.27 us -> 3.42 us  [per_device(): text_back = lax.all_to_all(text_parts, TEXT_GROUP, 0, 0, tiled=True)]
    pallas_call x7 -> x9, Pallas kernels: 6.77 us -> 8.45 us  [call(): pl.pallas_call(kernel, out_shape=outs, in_specs=[VMEM] * (len(args) - sca...]
  transfers between devices with their start and end apart: 8 -> 9, of which waited for: 5 -> 6; matrix products, arithmetic and copies ran while one was open for 0% -> 0% of each run, Pallas kernels for 2% -> 3%
where the time goes in v5:
time: 111 us; the launch traced here: 110 us
  starting transfers between devices  65 us (59%)
  waiting for transfers between devices  21.2 us (19%)
  blocking collectives  13 us (12%)
  Pallas kernels  8.45 us (8%)
  between operations  2.04 us (2%)
    all_to_all x1, starting transfers between devices, per_device(): piece = lax.all_to_all(image_send, IMAGE_GROUP, 0, 0, tiled=True)  17.4 us
    all_to_all x1, blocking collectives, per_device(): image_back = lax.all_to_all(image_parts, IMAGE_GROUP, 0, 0, tiled=True)  13 us
    all_to_all x1, starting transfers between devices, per_device(): text = lax.all_to_all(text_send, TEXT_GROUP, 0, 0, tiled=True)  11.7 us
    pallas_call x9, Pallas kernels, call(): pl.pallas_call(kernel, out_shape=outs, in_specs=[VMEM] * (len(args) - sca...  8.45 us
    all_to_all x1, starting transfers between devices, per_device(): text_back = lax.all_to_all(text_parts, TEXT_GROUP, 0, 0, tiled=True)  8.01 us
    all_to_all x1, starting transfers between devices, per_device(): sums = lax.all_to_all(sums, (PAIR, 'core'), 0, 0, tiled=True)  7.82 us
    all_to_all x1, waiting for transfers between devices, per_device(): piece = lax.all_to_all(image_send, IMAGE_GROUP, 0, 0, tiled=True)  6.45 us
    ppermute x1, starting transfers between devices, per_device(): came_pair = lax.ppermute(send, PAIR, swap)  4.62 us
  transfers between devices with their start and end apart: 9, of which 6 were waited for; matrix products, arithmetic and copies ran while one was open for 0% of the time, Pallas kernels for 3%

profile of v5, /device:TPU:1, one launch (start us, length us, event | category | flops | bytes accessed | tf_op | source)
XLA Modules:
  0.0 110.2 jit_solution(13114780936553223026)
XLA Ops:
  0.6 1.6 %shard_map.76 = (bf16[64,1280]{1,0:T(8,128)(2,1)}, f32[8,1152]{1,0:T(8,128)}, f32[8,1]{1,0:T(8,128)}) custom-call(bf16[8,1152]{1,0:T(8,128)(2,1)} %image_ref.1, s32[8]{0:T(128)} %pair_ref.1), custom_call_target="tpu_custom_call" | custom-call | bytes 73856 | tf_op jit(solution)/shard_map/pallas_call | solution.py:190
  2.2 17.4 %all-to-all-start = ((bf16[8,8,1280]{2,1,0:T(8,128)(2,1)}), bf16[8,8,1280]{2,1,0:T(8,128)(2,1)S(1)}, u32[]{:S(2)}, u32[]{:S(2)}) async-start(bf16[8,8,1280]{2,1,0:T(8,128)(2,1)} %bitcast.20), calls=%async_computation | async-start | bytes 327680 | tf_op jit(solution)/shard_map/all_to_all | solution.py:214
  19.6 1.7 %shard_map.77 = (bf16[256,1152]{1,0:T(8,128)(2,1)}, f32[8,1152]{1,0:T(8,128)}, f32[8,1]{1,0:T(8,128)}) custom-call(bf16[8,1152]{1,0:T(8,128)(2,1)} %text_ref.1), custom_call_target="tpu_custom_call" | custom-call | bytes 73728 | tf_op jit(solution)/shard_map/pallas_call | solution.py:190
  21.3 6.4 %all-to-all-done = bf16[8,8,1280]{2,1,0:T(8,128)(2,1)S(1)} async-done(((bf16[8,8,1280]{2,1,0:T(8,128)(2,1)}), bf16[8,8,1280]{2,1,0:T(8,128)(2,1)S(1)}, u32[]{:S(2)}, u32[]{:S(2)}) %all-to-all-start) | async-done | bytes 163872 | tf_op jit(solution)/shard_map/all_to_all | solution.py:214
  27.8 11.7 %all-to-all-start.1 = ((bf16[32,8,1152]{2,1,0:T(8,128)(2,1)}), bf16[32,8,1152]{2,1,0:T(8,128)(2,1)S(1)}, u32[]{:S(2)}, u32[]{:S(2)}) async-start(bf16[32,8,1152]{2,1,0:T(8,128)(2,1)} %bitcast.19), calls=%async_computation.1 | async-start | bytes 1179648 | tf_op jit(solution)/shard_map/all_to_all | solution.py:215
  39.5 3.9 %collective-permute-start = (bf16[64,1280]{1,0:T(8,128)(2,1)S(1)}, bf16[64,1280]{1,0:T(8,128)(2,1)S(1)}, u32[]{:S(2)}, u32[]{:S(2)}) collective-permute-start(bf16[64,1280]{1,0:T(8,128)(2,1)S(1)} %bitcast.14), channel_id=1, source_target_pairs={{0,128},{128,0},{1,129},{129,1},{2,130},{130,2},{3,131},{131,3},{4... | collective-permute-start | bytes 491528 | tf_op jit(solution)/shard_map/ppermute | solution.py:217
  43.4 4.5 %collective-permute-start.1 = (bf16[64,1280]{1,0:T(8,128)(2,1)S(1)}, bf16[64,1280]{1,0:T(8,128)(2,1)S(1)}, u32[]{:S(2)}, u32[]{:S(2)}) collective-permute-start(bf16[64,1280]{1,0:T(8,128)(2,1)S(1)} %bitcast.15), channel_id=1, source_target_pairs={{0,16},{16,0},{1,17},{17,1},{2,18},{18,2},{3,19},{19,3},{4,20},{20... | collective-permute-start | bytes 491528 | tf_op jit(solution)/shard_map/ppermute | solution.py:218
  48.0 0.0 collective-permute-done.b
  48.0 3.3 %collective-permute-start.2 = (bf16[64,1280]{1,0:T(8,128)(2,1)S(1)}, bf16[64,1280]{1,0:T(8,128)(2,1)S(1)}, u32[]{:S(2)}, u32[]{:S(2)}) collective-permute-start(bf16[64,1280]{1,0:T(8,128)(2,1)S(1)} %collective-permute-done.b), channel_id=1, source_target_pairs={{0,16},{16,0},{1,17},{17,1},{2,18},{18,2},{3,19},{19,3},{4,20},{20... | collective-permute-start | bytes 491528 | tf_op jit(solution)/shard_map/ppermute | solution.py:219
  52.5 0.0 collective-permute-done.1.c
  52.5 0.0 collective-permute-done.2.d
  52.5 3.9 %all-to-all-done.1 = bf16[32,8,1152]{2,1,0:T(8,128)(2,1)S(1)} async-done(((bf16[32,8,1152]{2,1,0:T(8,128)(2,1)}), bf16[32,8,1152]{2,1,0:T(8,128)(2,1)S(1)}, u32[]{:S(2)}, u32[]{:S(2)}) %all-to-all-start.1) | async-done | bytes 589856 | tf_op jit(solution)/shard_map/all_to_all | solution.py:215
  56.4 2.2 %shard_map.78 = (bf16[256,1280]{1,0:T(8,128)(2,1)}, bf16[256,256]{1,0:T(8,128)(2,1)S(1)}, f32[256,128]{1,0:T(8,128)S(1)}) custom-call(bf16[64,1280]{1,0:T(8,128)(2,1)S(1)} %bitcast.16, bf16[64,1280]{1,0:T(8,128)(2,1)S(1)} %collective-permute-done.b, bf16[64,1280]{1,0:T(8,128)(2,1)S(1)} %collective-permute-done.1.c, ...), custom_call_target="tpu_custom_call" | custom-call | flops 301989888 | bytes 4980768 | tf_op jit(solution)/shard_map/pallas_call | solution.py:190
  58.6 8.0 %all-to-all-start.2 = ((bf16[32,8,1280]{2,1,0:T(8,128)(2,1)}), bf16[32,8,1280]{2,1,0:T(8,128)(2,1)S(1)}, u32[]{:S(2)}, u32[]{:S(2)}) async-start(bf16[32,8,1280]{2,1,0:T(8,128)(2,1)} %bitcast.4), calls=%async_computation.2 | async-start | bytes 1310720 | tf_op jit(solution)/shard_map/all_to_all | solution.py:234
  66.6 0.4 shard_map.79
  67.0 3.7 %collective-permute-start.3 = (f32[128,1280]{1,0:T(8,128)S(1)}, f32[128,1280]{1,0:T(8,128)S(1)}, u32[]{:S(2)}, u32[]{:S(2)}) collective-permute-start(f32[128,1280]{1,0:T(8,128)S(1)} %get-tuple-element.21), channel_id=1, source_target_pairs={{0,16},{16,0},{1,17},{17,1},{2,18},{18,2},{3,19},{19,3},{4,20},{20... | collective-permute-start | bytes 1966088 | tf_op jit(solution)/shard_map/ppermute | solution.py:237
  70.7 1.7 %collective-permute-done.3.came_ref = f32[128,1280]{1,0:T(8,128)S(1)} collective-permute-done((f32[128,1280]{1,0:T(8,128)S(1)}, f32[128,1280]{1,0:T(8,128)S(1)}, u32[]{:S(2)}, u32[]{:S(2)}) %collective-permute-start.3) | collective-permute-done | bytes 655392 | tf_op jit(solution)/shard_map/ppermute | solution.py:237
  72.4 0.1 shard_map.80
  72.5 4.6 %collective-permute-start.4 = (bf16[64,1280]{1,0:T(8,128)(2,1)S(1)}, bf16[64,1280]{1,0:T(8,128)(2,1)S(1)}, u32[]{:S(2)}, u32[]{:S(2)}) collective-permute-start(bf16[64,1280]{1,0:T(8,128)(2,1)S(1)} %get-tuple-element.23), channel_id=1, source_target_pairs={{0,128},{128,0},{1,129},{129,1},{2,130},{130,2},{3,131},{131,3},{4... | collective-permute-start | bytes 491528 | tf_op jit(solution)/shard_map/ppermute | solution.py:241
  77.1 4.3 %collective-permute-done.4.came_ref = bf16[64,1280]{1,0:T(8,128)(2,1)S(1)} collective-permute-done((bf16[64,1280]{1,0:T(8,128)(2,1)S(1)}, bf16[64,1280]{1,0:T(8,128)(2,1)S(1)}, u32[]{:S(2)}, u32[]{:S(2)}) %collective-permute-start.4) | collective-permute-done | bytes 163872 | tf_op jit(solution)/shard_map/ppermute | solution.py:241
  81.4 3.4 %all-to-all-done.2 = bf16[32,8,1280]{2,1,0:T(8,128)(2,1)S(1)} async-done(((bf16[32,8,1280]{2,1,0:T(8,128)(2,1)}), bf16[32,8,1280]{2,1,0:T(8,128)(2,1)S(1)}, u32[]{:S(2)}, u32[]{:S(2)}) %all-to-all-start.2) | async-done | bytes 655392 | tf_op jit(solution)/shard_map/all_to_all | solution.py:234
  84.8 0.2 shard_map.81
  85.0 13.0 %all_to_all.49 = bf16[8,8,1280]{2,1,0:T(8,128)(2,1)S(1)} all-to-all(bf16[8,8,1280]{2,1,0:T(8,128)(2,1)S(1)} %bitcast.18), channel_id=1, replica_groups=mesh['zh'=4,'z0'=2,'xl'=4,'core'=2,'xh'=2,'yh'=4,'y0'=2] {'zh','y0'}, dimensions={0} | all-to-all | bytes 327680 | tf_op jit(solution)/shard_map/all_to_all | solution.py:245
  98.0 0.0 copy-start
  98.0 0.8 shard_map.84
  98.8 0.0 copy-start.3
  98.8 7.8 %all-to-all-start.4 = ((f32[4,8,128]{2,1,0:T(8,128)}), f32[4,8,128]{2,1,0:T(8,128)S(1)}, u32[]{:S(2)}, u32[]{:S(2)}) async-start(f32[4,8,128]{2,1,0:T(8,128)} %shard_map.84), calls=%async_computation.4 | async-start | bytes 32768 | tf_op jit(solution)/shard_map/all_to_all | solution.py:250
  106.6 0.0 copy-done
  106.6 0.0 copy-done.3
  106.6 0.0 copy-start.1
  106.6 0.0 copy-start.2
  106.6 0.8 shard_map.83
  107.4 0.0 copy-done.1
  107.4 0.0 copy-done.2
  107.4 0.8 shard_map.82
  108.2 1.5 %all-to-all-done.4 = f32[4,8,128]{2,1,0:T(8,128)S(1)} async-done(((f32[4,8,128]{2,1,0:T(8,128)}), f32[4,8,128]{2,1,0:T(8,128)S(1)}, u32[]{:S(2)}, u32[]{:S(2)}) %all-to-all-start.4) | async-done | bytes 16416 | tf_op jit(solution)/shard_map/all_to_all | solution.py:250
  109.7 0.5 slice_reduce_fusion
Async XLA Ops:
  2.2 25.6 %all-to-all-start = ((bf16[8,8,1280]{2,1,0:T(8,128)(2,1)}), bf16[8,8,1280]{2,1,0:T(8,128)(2,1)S(1)}, u32[]{:S(2)}, u32[]{:S(2)}) async-start(bf16[8,8,1280]{2,1,0:T(8,128)(2,1)} %bitcast.20), calls=%async_computation | async-start | bytes 327680 | tf_op jit(solution)/shard_map/all_to_all | solution.py:214
  27.8 28.7 %all-to-all-start.1 = ((bf16[32,8,1152]{2,1,0:T(8,128)(2,1)}), bf16[32,8,1152]{2,1,0:T(8,128)(2,1)S(1)}, u32[]{:S(2)}, u32[]{:S(2)}) async-start(bf16[32,8,1152]{2,1,0:T(8,128)(2,1)} %bitcast.19), calls=%async_computation.1 | async-start | bytes 1179648 | tf_op jit(solution)/shard_map/all_to_all | solution.py:215
  39.5 8.5 %collective-permute-start = (bf16[64,1280]{1,0:T(8,128)(2,1)S(1)}, bf16[64,1280]{1,0:T(8,128)(2,1)S(1)}, u32[]{:S(2)}, u32[]{:S(2)}) collective-permute-start(bf16[64,1280]{1,0:T(8,128)(2,1)S(1)} %bitcast.14), channel_id=1, source_target_pairs={{0,128},{128,0},{1,129},{129,1},{2,130},{130,2},{3,131},{131,3},{4... | collective-permute-start | bytes 491528 | tf_op jit(solution)/shard_map/ppermute | solution.py:217
  43.4 9.1 %collective-permute-start.1 = (bf16[64,1280]{1,0:T(8,128)(2,1)S(1)}, bf16[64,1280]{1,0:T(8,128)(2,1)S(1)}, u32[]{:S(2)}, u32[]{:S(2)}) collective-permute-start(bf16[64,1280]{1,0:T(8,128)(2,1)S(1)} %bitcast.15), channel_id=1, source_target_pairs={{0,16},{16,0},{1,17},{17,1},{2,18},{18,2},{3,19},{19,3},{4,20},{20... | collective-permute-start | bytes 491528 | tf_op jit(solution)/shard_map/ppermute | solution.py:218
  48.0 4.6 %collective-permute-start.2 = (bf16[64,1280]{1,0:T(8,128)(2,1)S(1)}, bf16[64,1280]{1,0:T(8,128)(2,1)S(1)}, u32[]{:S(2)}, u32[]{:S(2)}) collective-permute-start(bf16[64,1280]{1,0:T(8,128)(2,1)S(1)} %collective-permute-done.b), channel_id=1, source_target_pairs={{0,16},{16,0},{1,17},{17,1},{2,18},{18,2},{3,19},{19,3},{4,20},{20... | collective-permute-start | bytes 491528 | tf_op jit(solution)/shard_map/ppermute | solution.py:219
  58.6 26.2 %all-to-all-start.2 = ((bf16[32,8,1280]{2,1,0:T(8,128)(2,1)}), bf16[32,8,1280]{2,1,0:T(8,128)(2,1)S(1)}, u32[]{:S(2)}, u32[]{:S(2)}) async-start(bf16[32,8,1280]{2,1,0:T(8,128)(2,1)} %bitcast.4), calls=%async_computation.2 | async-start | bytes 1310720 | tf_op jit(solution)/shard_map/all_to_all | solution.py:234
  67.0 5.4 %collective-permute-start.3 = (f32[128,1280]{1,0:T(8,128)S(1)}, f32[128,1280]{1,0:T(8,128)S(1)}, u32[]{:S(2)}, u32[]{:S(2)}) collective-permute-start(f32[128,1280]{1,0:T(8,128)S(1)} %get-tuple-element.21), channel_id=1, source_target_pairs={{0,16},{16,0},{1,17},{17,1},{2,18},{18,2},{3,19},{19,3},{4,20},{20... | collective-permute-start | bytes 1966088 | tf_op jit(solution)/shard_map/ppermute | solution.py:237
  72.5 8.9 %collective-permute-start.4 = (bf16[64,1280]{1,0:T(8,128)(2,1)S(1)}, bf16[64,1280]{1,0:T(8,128)(2,1)S(1)}, u32[]{:S(2)}, u32[]{:S(2)}) collective-permute-start(bf16[64,1280]{1,0:T(8,128)(2,1)S(1)} %get-tuple-element.23), channel_id=1, source_target_pairs={{0,128},{128,0},{1,129},{129,1},{2,130},{130,2},{3,131},{131,3},{4... | collective-permute-start | bytes 491528 | tf_op jit(solution)/shard_map/ppermute | solution.py:241
  98.0 8.6 %copy-start = (f32[8,1152]{1,0:T(8,128)S(1)}, f32[8,1152]{1,0:T(8,128)}, u32[]{:S(2)}) copy-start(f32[8,1152]{1,0:T(8,128)} %get-tuple-element.27.unit_ref) | copy-start | bytes 110596
  98.8 7.8 %copy-start.3 = (f32[8,1]{1,0:T(8,128)S(1)}, f32[8,1]{1,0:T(8,128)}, u32[]{:S(2)}) copy-start(f32[8,1]{1,0:T(8,128)} %get-tuple-element.28.norm_ref) | copy-start | bytes 100
  98.8 10.9 %all-to-all-start.4 = ((f32[4,8,128]{2,1,0:T(8,128)}), f32[4,8,128]{2,1,0:T(8,128)S(1)}, u32[]{:S(2)}, u32[]{:S(2)}) async-start(f32[4,8,128]{2,1,0:T(8,128)} %shard_map.84), calls=%async_computation.4 | async-start | bytes 32768 | tf_op jit(solution)/shard_map/all_to_all | solution.py:250
  106.6 0.8 copy-start.1
  106.6 0.8 copy-start.2

commit v6 on v5

--- a/solution.py
+++ b/solution.py
@@ -11,11 +11,11 @@
 EXTRA = 128
 F32 = jnp.float32
 BF16 = jnp.bfloat16
-IMAGE_ORDER = ("zh", "z0", "xl", "core", "xh", "yh", "y0")
-TEXT_ORDER = ("xh", "yh", "y0", "zh", "z0", "xl", "core")
-TEXT_GROUP = ("xh", "xl", "yh")
-IMAGE_GROUP = ("zh", "y0")
-PAIR = "z0"
+IMAGE_ORDER = ("zh", "z0", "x1", "x0", "core", "xh", "yh", "y0")
+TEXT_ORDER = ("xh", "yh", "y0", "zh", "z0", "x1", "x0", "core")
+TEXT_GROUP = ("xh", "x1", "x0", "z0")
+IMAGE_GROUP = ("zh", "yh")
+PAIR = "y0"
 VMEM = pl.BlockSpec(memory_space=pltpu.VMEM)
 SMEM = pl.BlockSpec(memory_space=pltpu.SMEM)
 
@@ -67,9 +67,11 @@
 
 
 def text_columns(own_rows, sizes, count):
-    place = lax.broadcasted_iota(jnp.int32, (1, count), 1)
-    peer, row = place // own_rows, place % own_rows
+    place = lax.broadcasted_iota(jnp.int32, (1, 2 * count), 1)
+    away = place // count
+    peer, row = (place % count) // own_rows, place % own_rows
     index = {a: lax.axis_index(a) for a in IMAGE_GROUP + (PAIR, "core")}
+    index["core"] = index["core"] + away - 2 * index["core"] * away
     for a in reversed(TEXT_GROUP):
         index[a] = peer % sizes[a]
         peer = peer // sizes[a]
@@ -87,13 +89,15 @@
     return jnp.exp(jnp.zeros((8, 128), F32) + log_scale_ref[0])[0:1, 0:1]
 
 
-def score_kernel(own_rows, sizes, piece_refs, text_ref, log_scale_ref, bias_ref, text_out, low_out, along_out):
-    text = text_ref[...]
-    count, width = text.shape
+def score_kernel(
+    own_rows, sizes, image_refs, text_refs, log_scale_ref, bias_ref, away_out, stay_out, low_out, along_out
+):
+    count, width = text_refs[0].shape
     scale = scale_of(log_scale_ref)
     column = text_columns(own_rows, sizes, count).astype(F32)
-    image = stacked(piece_refs, slice(0, width))
-    extra = stacked(piece_refs, slice(width, width + EXTRA)).astype(F32)
+    image = stacked(image_refs, slice(0, width))
+    text = stacked(text_refs, slice(0, width))
+    extra = stacked(image_refs, slice(width, width + EXTRA)).astype(F32)
     pair = extra[:, 0:1] * 128.0 + extra[:, 1:2]
     cosine = lax.dot_general(image, text, (((1,), (1,)), ((), ())), preferred_element_type=F32)
     scaled = scale * cosine
@@ -111,46 +115,53 @@
     low_out[...] = low
     along_image = jnp.sum(product, axis=1, keepdims=True)
     along_out[...] = jnp.where(lanes(image.shape[0]) == 0, along_image, 0.0)
-    along_text = jnp.broadcast_to(jnp.sum(product, axis=0, keepdims=True), (128, count)).T
-    along_text = along_text.astype(BF16).astype(F32)
+    along_text = jnp.broadcast_to(jnp.sum(product, axis=0, keepdims=True), (128, 2 * count)).T
     low_turned = dlogit.T.astype(BF16)
+    lane = lanes(count)
     block = width // 3
-    for first in range(0, width, block):
-        cols = slice(first, first + block)
-        part = scale * jnp.dot(low_turned, image[:, cols], preferred_element_type=F32)
-        text_out[:, cols] = (part - along_text[:, 0:1] * text[:, cols].astype(F32)).astype(BF16)
-    lane = lanes(count)
-    stats = split_stats(lane, 1, [jnp.broadcast_to(t, lane.shape) for t in totals])
-    text_out[:, width:] = jnp.where(lane == 0, along_text, stats).astype(BF16)
-
-
-def image_kernel(piece_refs, text_ref, low_ref, along_ref, log_scale_ref, stay_out, away_out):
-    width = text_ref.shape[1]
+    for target, rows in ((away_out, slice(count, 2 * count)), (stay_out, slice(0, count))):
+        along = along_text[rows, 0:1]
+        for first in range(0, width, block):
+            cols = slice(first, first + block)
+            part = scale * jnp.dot(low_turned[rows], image[:, cols], preferred_element_type=F32)
+            target[:, cols] = part - along * text[rows, cols].astype(F32)
+        kept = jnp.where(lane == 0, along, 0.0)
+        for n, total in enumerate(totals):
+            kept = jnp.where(lane == 1 + n, total, kept)
+        target[:, width:] = kept
+
+
+def join_text_kernel(stay_ref, came_ref, out_ref):
+    width = stay_ref.shape[1] - EXTRA
+    out_ref[:, :width] = (stay_ref[:, :width] + came_ref[:, :width]).astype(BF16)
+    lane = lanes(stay_ref.shape[0])
+    extra = stay_ref[:, width:] + came_ref[:, width:]
+    stats = split_stats(lane, 1, [jnp.broadcast_to(extra[:, n : n + 1], lane.shape) for n in (1, 2, 3)])
+    out_ref[:, width:] = jnp.where(lane == 0, extra, stats).astype(BF16)
+
+
+def image_kernel(image_refs, text_refs, low_ref, along_ref, log_scale_ref, away_out, stay_out):
+    count, width = text_refs[0].shape
     scale = scale_of(log_scale_ref)
     half = low_ref.shape[0] // 2
-    for target, pieces, rows in (
-        (away_out, piece_refs[2:], slice(half, 2 * half)),
-        (stay_out, piece_refs[:2], slice(0, half)),
+    for target, image_ref, rows in (
+        (away_out, image_refs[1], slice(half, 2 * half)),
+        (stay_out, image_refs[0], slice(0, half)),
     ):
         low, along = low_ref[rows, :], along_ref[rows, :]
         block = width // 3
         for first in range(0, width, block):
             cols = slice(first, first + block)
-            part = scale * jnp.dot(low, text_ref[:, cols], preferred_element_type=F32)
-            target[:, cols] = part - along[:, 0:1] * stacked(pieces, cols).astype(F32)
-        target[:, width:] = along
+            part = scale * jnp.dot(low, stacked(text_refs, cols), preferred_element_type=F32)
+            part = part - along[:, 0:1] * image_ref[:, cols].astype(F32)
+            target[:, cols] = part.astype(target.dtype)
+        target[:, width:] = along.astype(target.dtype)
 
 
 def merge_stats(extra, rows):
     peers = extra.shape[0] // rows
     total = jnp.sum(extra.reshape(peers, rows, EXTRA), axis=0)
     return [total[0:1, n : n + 1] + total[0:1, n + 3 : n + 4] for n in (1, 2, 3)]
-
-
-def add_kernel(stay_ref, came_ref, keep_out, send_out):
-    half = keep_out.shape[0]
-    keep_out[...] = stay_ref[:half, :] + came_ref[:half, :]
-    send_out[...] = (stay_ref[half:, :] + came_ref[half:, :]).astype(BF16)
 
 
 def join_kernel(own_rows, keep_ref, came_ref, text_back_ref, out_ref):
@@ -178,7 +189,7 @@
     out = jnp.zeros(lane.shape, F32)
     for n, value in enumerate(merge_stats(parts_ref[:, width:].astype(F32), own_rows)):
         out = jnp.where(lane == n, value / batch, out)
-    out_ref[...] = jnp.broadcast_to(out[None], out_ref.shape)
+    out_ref[...] = out
 
 
 def shape(*dims, dtype=BF16):
@@ -211,51 +222,51 @@
     text_send, text_unit, text_norm = call(
         pack_text_kernel, (shape(text_count, width), unit_shape, norm_shape), text_embed, limit=None
     )
+    swap = [(0, 1), (1, 0)]
     piece = lax.all_to_all(image_send, IMAGE_GROUP, 0, 0, tiled=True)
     text = lax.all_to_all(text_send, TEXT_GROUP, 0, 0, tiled=True)
-    swap = [(0, 1), (1, 0)]
     piece_pair = lax.ppermute(piece, PAIR, swap)
-    piece_core = lax.ppermute(piece, "core", swap)
-    piece_both = lax.ppermute(piece_pair, "core", swap)
+    text_core = lax.ppermute(text, "core", swap)
+    held = (piece, piece_pair, text, text_core)
 
     def score(a, b, c, d, *rest):
-        score_kernel(own_rows, sizes, (a, b, c, d), *rest)
+        score_kernel(own_rows, sizes, (a, b), (c, d), *rest)
 
     def image_partials(a, b, c, d, *rest):
-        image_kernel((a, b, c, d), *rest)
-
-    pieces = (piece, piece_pair, piece_core, piece_both)
+        image_kernel((a, b), (c, d), *rest)
+
     work = 2 * 4 * row_count * text_count * width
-    text_parts, low, along = call(
+    text_half = shape(text_count, wide, dtype=F32)
+    away, stay, low, along = call(
         score,
-        (shape(text_count, wide), shape(4 * row_count, text_count), shape(4 * row_count, EXTRA, dtype=F32)),
-        *pieces, text, log_scale, bias, scalars=2, flops=2 * work,
-    )
+        (text_half, text_half, shape(2 * row_count, 2 * text_count), shape(2 * row_count, EXTRA, dtype=F32)),
+        *held, log_scale, bias, scalars=2, flops=2 * work,
+    )
+    came = lax.ppermute(away, "core", swap)
+    send, keep = call(
+        image_partials,
+        (shape(row_count, wide), shape(row_count, wide, dtype=F32)),
+        *held, low, along, log_scale, scalars=1, flops=work,
+    )
+    text_parts = call(join_text_kernel, shape(text_count, wide), stay, came)
     text_back = lax.all_to_all(text_parts, TEXT_GROUP, 0, 0, tiled=True)
-    half = shape(2 * row_count, wide, dtype=F32)
-    stay, away = call(image_partials, (half, half), *pieces, text, low, along, log_scale, scalars=1, flops=work)
-    came = lax.ppermute(away, "core", swap)
-    keep, send = call(
-        add_kernel, (shape(row_count, wide, dtype=F32), shape(row_count, wide)), stay, came
-    )
     came_pair = lax.ppermute(send, PAIR, swap)
     image_parts = call(
         functools.partial(join_kernel, own_rows), shape(row_count, wide), keep, came_pair, text_back
     )
     image_back = lax.all_to_all(image_parts, IMAGE_GROUP, 0, 0, tiled=True)
     text_grad = call(finish_kernel, unit_shape, text_back, text_unit, text_norm)
-    four = sizes[PAIR] * sizes["core"]
     batch = own_rows * math.prod(sizes.values())
-    sums = call(functools.partial(stats_kernel, own_rows, batch), shape(four, 8, EXTRA, dtype=F32), image_back)
-    sums = lax.all_to_all(sums, (PAIR, "core"), 0, 0, tiled=True)
+    sums = call(functools.partial(stats_kernel, own_rows, batch), shape(8, EXTRA, dtype=F32), image_back)
+    sums_came = lax.ppermute(sums, PAIR, swap)
     image_grad = call(finish_kernel, unit_shape, image_back, image_unit, image_norm)
-    stats = jnp.sum(sums[:, 0, :3], axis=0)
+    stats = (sums + sums_came)[0, :3]
     return (image_grad, text_grad, stats)
 
 
 def solution(mesh):
     img, txt = mesh.shape["img"], mesh.shape["txt"]
-    parts = (img // 16, 2, 4, 2, 2, txt // 4, 2)
+    parts = (img // 16, 2, 2, 2, 2, 2, txt // 4, 2)
     split = Mesh(mesh.devices.reshape(parts), IMAGE_ORDER)
     image_spec, text_spec = P(IMAGE_ORDER, None), P(TEXT_ORDER, None)
     return jax.shard_map(

time: 111 us -> 113 us (1.018)
  the two profiles are of different devices: /device:TPU:1 before, /device:TPU:4 now
where the time goes in v6:
time: 113 us; the launch traced here: 112 us
  starting transfers between devices  46.4 us (41%)
  waiting for transfers between devices  35.3 us (31%)
  blocking collectives  20.1 us (18%)
  Pallas kernels  7.82 us (7%)
  between operations  2.04 us (2%)
    all_to_all x1, starting transfers between devices, per_device(): piece = lax.all_to_all(image_send, IMAGE_GROUP, 0, 0, tiled=True)  21.6 us
    all_to_all x1, blocking collectives, per_device(): image_back = lax.all_to_all(image_parts, IMAGE_GROUP, 0, 0, tiled=True)  20.1 us
    all_to_all x1, waiting for transfers between devices, per_device(): piece = lax.all_to_all(image_send, IMAGE_GROUP, 0, 0, tiled=True)  13.8 us
    ppermute x1, waiting for transfers between devices, per_device(): came_pair = lax.ppermute(send, PAIR, swap)  9.46 us
    all_to_all x1, starting transfers between devices, per_device(): text = lax.all_to_all(text_send, TEXT_GROUP, 0, 0, tiled=True)  9.04 us
    pallas_call x9, Pallas kernels, call(): pl.pallas_call(kernel, out_shape=outs, in_specs=[VMEM] * (len(args) - sca...  7.82 us
    all_to_all x1, waiting for transfers between devices, per_device(): text = lax.all_to_all(text_send, TEXT_GROUP, 0, 0, tiled=True)  7.75 us
    all_to_all x1, starting transfers between devices, per_device(): text_back = lax.all_to_all(text_parts, TEXT_GROUP, 0, 0, tiled=True)  5.5 us
  transfers between devices with their start and end apart: 8, of which 7 were waited for; matrix products, arithmetic and copies ran while one was open for 0% of the time, Pallas kernels for 3%

profile of v6, /device:TPU:4, one launch (start us, length us, event | category | flops | bytes accessed | tf_op | source)
XLA Modules:
  0.0 112.2 jit_solution(7985397402367400958)
XLA Ops:
  0.6 1.6 %shard_map.76 = (bf16[128,1280]{1,0:T(8,128)(2,1)}, f32[8,1152]{1,0:T(8,128)}, f32[8,1]{1,0:T(8,128)}) custom-call(bf16[8,1152]{1,0:T(8,128)(2,1)} %image_ref.1, s32[8]{0:T(128)} %pair_ref.1), custom_call_target="tpu_custom_call" | custom-call | bytes 73856 | tf_op jit(solution)/shard_map/pallas_call | solution.py:201
  2.3 21.6 %all-to-all-start = ((bf16[16,8,1280]{2,1,0:T(8,128)(2,1)}), bf16[16,8,1280]{2,1,0:T(8,128)(2,1)S(1)}, u32[]{:S(2)}, u32[]{:S(2)}) async-start(bf16[16,8,1280]{2,1,0:T(8,128)(2,1)} %bitcast.21), calls=%async_computation | async-start | bytes 655360 | tf_op jit(solution)/shard_map/all_to_all | solution.py:226
  23.9 1.6 %shard_map.77 = (bf16[128,1152]{1,0:T(8,128)(2,1)}, f32[8,1152]{1,0:T(8,128)}, f32[8,1]{1,0:T(8,128)}) custom-call(bf16[8,1152]{1,0:T(8,128)(2,1)} %text_ref.1), custom_call_target="tpu_custom_call" | custom-call | bytes 73728 | tf_op jit(solution)/shard_map/pallas_call | solution.py:201
  25.4 13.8 %all-to-all-done = bf16[16,8,1280]{2,1,0:T(8,128)(2,1)S(1)} async-done(((bf16[16,8,1280]{2,1,0:T(8,128)(2,1)}), bf16[16,8,1280]{2,1,0:T(8,128)(2,1)S(1)}, u32[]{:S(2)}, u32[]{:S(2)}) %all-to-all-start) | async-done | bytes 327712 | tf_op jit(solution)/shard_map/all_to_all | solution.py:226
  39.2 9.0 %all-to-all-start.1 = ((bf16[16,8,1152]{2,1,0:T(8,128)(2,1)}), bf16[16,8,1152]{2,1,0:T(8,128)(2,1)S(1)}, u32[]{:S(2)}, u32[]{:S(2)}) async-start(bf16[16,8,1152]{2,1,0:T(8,128)(2,1)} %bitcast.22), calls=%async_computation.1 | async-start | bytes 589824 | tf_op jit(solution)/shard_map/all_to_all | solution.py:227
  48.3 2.2 %collective-permute-start = (bf16[128,1280]{1,0:T(8,128)(2,1)S(1)}, bf16[128,1280]{1,0:T(8,128)(2,1)S(1)}, u32[]{:S(2)}, u32[]{:S(2)}) collective-permute-start(bf16[128,1280]{1,0:T(8,128)(2,1)S(1)} %bitcast.14), channel_id=1, source_target_pairs={{0,1},{1,0},{2,3},{3,2},{4,5},{5,4},{6,7},{7,6},{8,9},{9,8},{10,11... | collective-permute-start | bytes 983048 | tf_op jit(solution)/shard_map/ppermute | solution.py:228
  50.5 7.8 %all-to-all-done.1 = bf16[16,8,1152]{2,1,0:T(8,128)(2,1)S(1)} async-done(((bf16[16,8,1152]{2,1,0:T(8,128)(2,1)}), bf16[16,8,1152]{2,1,0:T(8,128)(2,1)S(1)}, u32[]{:S(2)}, u32[]{:S(2)}) %all-to-all-start.1) | async-done | bytes 294944 | tf_op jit(solution)/shard_map/all_to_all | solution.py:227
  58.3 1.9 %collective-permute-start.1 = (bf16[128,1152]{1,0:T(8,128)(2,1)S(1)}, bf16[128,1152]{1,0:T(8,128)(2,1)S(1)}, u32[]{:S(2)}, u32[]{:S(2)}) collective-permute-start(bf16[128,1152]{1,0:T(8,128)(2,1)S(1)} %bitcast.17), channel_id=1, source_target_pairs={{0,16},{16,0},{1,17},{17,1},{2,18},{18,2},{3,19},{19,3},{4,20},{20... | collective-permute-start | bytes 884744 | tf_op jit(solution)/shard_map/ppermute | solution.py:229
  61.5 0.3 collective-permute-done.1.d
  61.8 0.0 collective-permute-done.b
  61.8 1.3 %shard_map.78 = (f32[128,1280]{1,0:T(8,128)S(1)}, f32[128,1280]{1,0:T(8,128)S(1)}, bf16[256,256]{1,0:T(8,128)(2,1)S(1)}, f32[256,128]{1,0:T(8,128)S(1)}) custom-call(bf16[128,1280]{1,0:T(8,128)(2,1)S(1)} %bitcast.15, bf16[128,1280]{1,0:T(8,128)(2,1)S(1)} %collective-permute-done.b, bf16[128,1152]{1,0:T(8,128)(2,1)S(1)} %bitcast.18, ...), custom_call_target="tpu_custom_call" | custom-call | flops 301989888 | bytes 4980768 | tf_op jit(solution)/shard_map/pallas_call | solution.py:201
  63.1 2.2 %collective-permute-start.3 = (f32[128,1280]{1,0:T(8,128)S(1)}, f32[128,1280]{1,0:T(8,128)S(1)}, u32[]{:S(2)}, u32[]{:S(2)}) collective-permute-start(f32[128,1280]{1,0:T(8,128)S(1)} %get-tuple-element.22), channel_id=1, source_target_pairs={{0,16},{16,0},{1,17},{17,1},{2,18},{18,2},{3,19},{19,3},{4,20},{20... | collective-permute-start | bytes 1966088 | tf_op jit(solution)/shard_map/ppermute | solution.py:245
  65.2 1.8 %collective-permute-done.3.came_ref = f32[128,1280]{1,0:T(8,128)S(1)} collective-permute-done((f32[128,1280]{1,0:T(8,128)S(1)}, f32[128,1280]{1,0:T(8,128)S(1)}, u32[]{:S(2)}, u32[]{:S(2)}) %collective-permute-start.3) | collective-permute-done | bytes 655392 | tf_op jit(solution)/shard_map/ppermute | solution.py:245
  67.1 0.9 shard_map.80
  67.9 5.5 %all-to-all-start.2 = ((bf16[16,8,1280]{2,1,0:T(8,128)(2,1)}), bf16[16,8,1280]{2,1,0:T(8,128)(2,1)S(1)}, u32[]{:S(2)}, u32[]{:S(2)}) async-start(bf16[16,8,1280]{2,1,0:T(8,128)(2,1)} %bitcast.4), calls=%async_computation.2 | async-start | bytes 655360 | tf_op jit(solution)/shard_map/all_to_all | solution.py:252
  73.4 0.4 shard_map.79
  73.8 2.0 %collective-permute-start.2 = (bf16[128,1280]{1,0:T(8,128)(2,1)S(1)}, bf16[128,1280]{1,0:T(8,128)(2,1)S(1)}, u32[]{:S(2)}, u32[]{:S(2)}) collective-permute-start(bf16[128,1280]{1,0:T(8,128)(2,1)S(1)} %get-tuple-element.20), channel_id=1, source_target_pairs={{0,1},{1,0},{2,3},{3,2},{4,5},{5,4},{6,7},{7,6},{8,9},{9,8},{10,11... | collective-permute-start | bytes 983048 | tf_op jit(solution)/shard_map/ppermute | solution.py:253
  75.8 9.5 %collective-permute-done.2.came_ref = bf16[128,1280]{1,0:T(8,128)(2,1)S(1)} collective-permute-done((bf16[128,1280]{1,0:T(8,128)(2,1)S(1)}, bf16[128,1280]{1,0:T(8,128)(2,1)S(1)}, u32[]{:S(2)}, u32[]{:S(2)}) %collective-permute-start.2) | collective-permute-done | bytes 327712 | tf_op jit(solution)/shard_map/ppermute | solution.py:253
  85.3 0.3 all-to-all-done.2
  85.6 0.3 shard_map.81
  85.8 20.1 %all_to_all.44 = bf16[16,8,1280]{2,1,0:T(8,128)(2,1)S(1)} all-to-all(bf16[16,8,1280]{2,1,0:T(8,128)(2,1)S(1)} %bitcast.20), channel_id=1, replica_groups=mesh['zh'=4,'z0'=2,'x1'=2,'x0'=2,'core'=2,'xh'=2,'yh'=4,'y0'=2] {'zh','yh'}, dimensions={0} | all-to-all | bytes 655360 | tf_op jit(solution)/shard_map/all_to_all | solution.py:257
  105.9 0.0 copy-start.1
  105.9 0.0 copy-start.3
  105.9 0.2 shard_map.84
  106.1 1.9 %collective-permute-start.4 = (f32[8,128]{1,0:T(8,128)S(1)}, f32[8,128]{1,0:T(8,128)S(1)}, u32[]{:S(2)}, u32[]{:S(2)}) collective-permute-start(f32[8,128]{1,0:T(8,128)S(1)} %shard_map.84), channel_id=1, source_target_pairs={{0,1},{1,0},{2,3},{3,2},{4,5},{5,4},{6,7},{7,6},{8,9},{9,8},{10,11... | collective-permute-start | bytes 12296 | tf_op jit(solution)/shard_map/ppermute | solution.py:261
  108.1 0.0 copy-done.1
  108.1 0.0 copy-done.3
  108.1 0.0 copy-start
  108.1 0.0 copy-start.2
  108.1 0.8 shard_map.83
  108.9 0.0 copy-done
  108.9 0.0 copy-done.2
  108.9 0.8 shard_map.82
  109.7 1.9 %collective-permute-done.4 = f32[8,128]{1,0:T(8,128)S(1)} collective-permute-done((f32[8,128]{1,0:T(8,128)S(1)}, f32[8,128]{1,0:T(8,128)S(1)}, u32[]{:S(2)}, u32[]{:S(2)}) %collective-permute-start.4) | collective-permute-done | bytes 4128 | tf_op jit(solution)/shard_map/ppermute | solution.py:261
  111.7 0.5 slice_bitcast_fusion
  (1 shorter events, 0.0 us)
Async XLA Ops:
  2.3 37.0 %all-to-all-start = ((bf16[16,8,1280]{2,1,0:T(8,128)(2,1)}), bf16[16,8,1280]{2,1,0:T(8,128)(2,1)S(1)}, u32[]{:S(2)}, u32[]{:S(2)}) async-start(bf16[16,8,1280]{2,1,0:T(8,128)(2,1)} %bitcast.21), calls=%async_computation | async-start | bytes 655360 | tf_op jit(solution)/shard_map/all_to_all | solution.py:226
  39.2 19.1 %all-to-all-start.1 = ((bf16[16,8,1152]{2,1,0:T(8,128)(2,1)}), bf16[16,8,1152]{2,1,0:T(8,128)(2,1)S(1)}, u32[]{:S(2)}, u32[]{:S(2)}) async-start(bf16[16,8,1152]{2,1,0:T(8,128)(2,1)} %bitcast.22), calls=%async_computation.1 | async-start | bytes 589824 | tf_op jit(solution)/shard_map/all_to_all | solution.py:227
  48.3 13.5 %collective-permute-start = (bf16[128,1280]{1,0:T(8,128)(2,1)S(1)}, bf16[128,1280]{1,0:T(8,128)(2,1)S(1)}, u32[]{:S(2)}, u32[]{:S(2)}) collective-permute-start(bf16[128,1280]{1,0:T(8,128)(2,1)S(1)} %bitcast.14), channel_id=1, source_target_pairs={{0,1},{1,0},{2,3},{3,2},{4,5},{5,4},{6,7},{7,6},{8,9},{9,8},{10,11... | collective-permute-start | bytes 983048 | tf_op jit(solution)/shard_map/ppermute | solution.py:228
  58.3 3.5 %collective-permute-start.1 = (bf16[128,1152]{1,0:T(8,128)(2,1)S(1)}, bf16[128,1152]{1,0:T(8,128)(2,1)S(1)}, u32[]{:S(2)}, u32[]{:S(2)}) collective-permute-start(bf16[128,1152]{1,0:T(8,128)(2,1)S(1)} %bitcast.17), channel_id=1, source_target_pairs={{0,16},{16,0},{1,17},{17,1},{2,18},{18,2},{3,19},{19,3},{4,20},{20... | collective-permute-start | bytes 884744 | tf_op jit(solution)/shard_map/ppermute | solution.py:229
  63.1 4.0 %collective-permute-start.3 = (f32[128,1280]{1,0:T(8,128)S(1)}, f32[128,1280]{1,0:T(8,128)S(1)}, u32[]{:S(2)}, u32[]{:S(2)}) collective-permute-start(f32[128,1280]{1,0:T(8,128)S(1)} %get-tuple-element.22), channel_id=1, source_target_pairs={{0,16},{16,0},{1,17},{17,1},{2,18},{18,2},{3,19},{19,3},{4,20},{20... | collective-permute-start | bytes 1966088 | tf_op jit(solution)/shard_map/ppermute | solution.py:245
  67.9 17.6 %all-to-all-start.2 = ((bf16[16,8,1280]{2,1,0:T(8,128)(2,1)}), bf16[16,8,1280]{2,1,0:T(8,128)(2,1)S(1)}, u32[]{:S(2)}, u32[]{:S(2)}) async-start(bf16[16,8,1280]{2,1,0:T(8,128)(2,1)} %bitcast.4), calls=%async_computation.2 | async-start | bytes 655360 | tf_op jit(solution)/shard_map/all_to_all | solution.py:252
  73.8 11.5 %collective-permute-start.2 = (bf16[128,1280]{1,0:T(8,128)(2,1)S(1)}, bf16[128,1280]{1,0:T(8,128)(2,1)S(1)}, u32[]{:S(2)}, u32[]{:S(2)}) collective-permute-start(bf16[128,1280]{1,0:T(8,128)(2,1)S(1)} %get-tuple-element.20), channel_id=1, source_target_pairs={{0,1},{1,0},{2,3},{3,2},{4,5},{5,4},{6,7},{7,6},{8,9},{9,8},{10,11... | collective-permute-start | bytes 983048 | tf_op jit(solution)/shard_map/ppermute | solution.py:253
  105.9 2.1 %copy-start.1 = (f32[8,1152]{1,0:T(8,128)S(1)}, f32[8,1152]{1,0:T(8,128)}, u32[]{:S(2)}) copy-start(f32[8,1152]{1,0:T(8,128)} %get-tuple-element.25.unit_ref) | copy-start | bytes 110596
  105.9 2.1 %copy-start.3 = (f32[8,1]{1,0:T(8,128)S(1)}, f32[8,1]{1,0:T(8,128)}, u32[]{:S(2)}) copy-start(f32[8,1]{1,0:T(8,128)} %get-tuple-element.26.norm_ref) | copy-start | bytes 100
  106.1 5.5 %collective-permute-start.4 = (f32[8,128]{1,0:T(8,128)S(1)}, f32[8,128]{1,0:T(8,128)S(1)}, u32[]{:S(2)}, u32[]{:S(2)}) collective-permute-start(f32[8,128]{1,0:T(8,128)S(1)} %shard_map.84), channel_id=1, source_target_pairs={{0,1},{1,0},{2,3},{3,2},{4,5},{5,4},{6,7},{7,6},{8,9},{9,8},{10,11... | collective-permute-start | bytes 12296 | tf_op jit(solution)/shard_map/ppermute | solution.py:261
  108.1 0.8 copy-start
  108.1 0.8 copy-start.2

commit v7 on v6

--- a/solution.py
+++ b/solution.py
@@ -13,8 +13,8 @@
 BF16 = jnp.bfloat16
 IMAGE_ORDER = ("zh", "z0", "x1", "x0", "core", "xh", "yh", "y0")
 TEXT_ORDER = ("xh", "yh", "y0", "zh", "z0", "x1", "x0", "core")
-TEXT_GROUP = ("xh", "x1", "x0", "z0")
-IMAGE_GROUP = ("zh", "yh")
+TEXT_GROUP = ("xh", "x1", "zh")
+IMAGE_GROUP = ("x0", "z0", "yh")
 PAIR = "y0"
 VMEM = pl.BlockSpec(memory_space=pltpu.VMEM)
 SMEM = pl.BlockSpec(memory_space=pltpu.SMEM)

time: 113 us -> 114 us (level)
  the two profiles are of different devices: /device:TPU:4 before, /device:TPU:16 now
where the time goes in v7:
time: 114 us; the launch traced here: 113 us
  starting transfers between devices  47.1 us (41%)
  waiting for transfers between devices  35.7 us (31%)
  blocking collectives  20.1 us (18%)
  Pallas kernels  7.82 us (7%)
  between operations  2.05 us (2%)
    all_to_all x1, blocking collectives, per_device(): image_back = lax.all_to_all(image_parts, IMAGE_GROUP, 0, 0, tiled=True)  20.1 us
    all_to_all x1, starting transfers between devices, per_device(): text = lax.all_to_all(text_send, TEXT_GROUP, 0, 0, tiled=True)  19.6 us
    all_to_all x1, waiting for transfers between devices, per_device(): text = lax.all_to_all(text_send, TEXT_GROUP, 0, 0, tiled=True)  10.7 us
    all_to_all x1, starting transfers between devices, per_device(): piece = lax.all_to_all(image_send, IMAGE_GROUP, 0, 0, tiled=True)  10.4 us
    all_to_all x1, waiting for transfers between devices, per_device(): piece = lax.all_to_all(image_send, IMAGE_GROUP, 0, 0, tiled=True)  10.4 us
    ppermute x1, waiting for transfers between devices, per_device(): came_pair = lax.ppermute(send, PAIR, swap)  8.27 us
    pallas_call x9, Pallas kernels, call(): pl.pallas_call(kernel, out_shape=outs, in_specs=[VMEM] * (len(args) - sca...  7.82 us
    all_to_all x1, starting transfers between devices, per_device(): text_back = lax.all_to_all(text_parts, TEXT_GROUP, 0, 0, tiled=True)  4.38 us
  transfers between devices with their start and end apart: 8, of which 7 were waited for; matrix products, arithmetic and copies ran while one was open for 0% of the time, Pallas kernels for 3%

profile of v7, /device:TPU:16, one launch (start us, length us, event | category | flops | bytes accessed | tf_op | source)
XLA Modules:
  0.0 113.3 jit_solution(17644266686495455906)
XLA Ops:
  0.6 1.6 %shard_map.76 = (bf16[128,1280]{1,0:T(8,128)(2,1)}, f32[8,1152]{1,0:T(8,128)}, f32[8,1]{1,0:T(8,128)}) custom-call(bf16[8,1152]{1,0:T(8,128)(2,1)} %image_ref.1, s32[8]{0:T(128)} %pair_ref.1), custom_call_target="tpu_custom_call" | custom-call | bytes 73856 | tf_op jit(solution)/shard_map/pallas_call | solution.py:201
  2.3 10.4 %all-to-all-start = ((bf16[16,8,1280]{2,1,0:T(8,128)(2,1)}), bf16[16,8,1280]{2,1,0:T(8,128)(2,1)S(1)}, u32[]{:S(2)}, u32[]{:S(2)}) async-start(bf16[16,8,1280]{2,1,0:T(8,128)(2,1)} %bitcast.21), calls=%async_computation | async-start | bytes 655360 | tf_op jit(solution)/shard_map/all_to_all | solution.py:226
  12.7 1.6 %shard_map.77 = (bf16[128,1152]{1,0:T(8,128)(2,1)}, f32[8,1152]{1,0:T(8,128)}, f32[8,1]{1,0:T(8,128)}) custom-call(bf16[8,1152]{1,0:T(8,128)(2,1)} %text_ref.1), custom_call_target="tpu_custom_call" | custom-call | bytes 73728 | tf_op jit(solution)/shard_map/pallas_call | solution.py:201
  14.3 10.4 %all-to-all-done = bf16[16,8,1280]{2,1,0:T(8,128)(2,1)S(1)} async-done(((bf16[16,8,1280]{2,1,0:T(8,128)(2,1)}), bf16[16,8,1280]{2,1,0:T(8,128)(2,1)S(1)}, u32[]{:S(2)}, u32[]{:S(2)}) %all-to-all-start) | async-done | bytes 327712 | tf_op jit(solution)/shard_map/all_to_all | solution.py:226
  24.7 19.6 %all-to-all-start.1 = ((bf16[16,8,1152]{2,1,0:T(8,128)(2,1)}), bf16[16,8,1152]{2,1,0:T(8,128)(2,1)S(1)}, u32[]{:S(2)}, u32[]{:S(2)}) async-start(bf16[16,8,1152]{2,1,0:T(8,128)(2,1)} %bitcast.22), calls=%async_computation.1 | async-start | bytes 589824 | tf_op jit(solution)/shard_map/all_to_all | solution.py:227
  44.3 3.1 %collective-permute-start = (bf16[128,1280]{1,0:T(8,128)(2,1)S(1)}, bf16[128,1280]{1,0:T(8,128)(2,1)S(1)}, u32[]{:S(2)}, u32[]{:S(2)}) collective-permute-start(bf16[128,1280]{1,0:T(8,128)(2,1)S(1)} %bitcast.14), channel_id=1, source_target_pairs={{0,1},{1,0},{2,3},{3,2},{4,5},{5,4},{6,7},{7,6},{8,9},{9,8},{10,11... | collective-permute-start | bytes 983048 | tf_op jit(solution)/shard_map/ppermute | solution.py:228
  47.3 10.7 %all-to-all-done.1 = bf16[16,8,1152]{2,1,0:T(8,128)(2,1)S(1)} async-done(((bf16[16,8,1152]{2,1,0:T(8,128)(2,1)}), bf16[16,8,1152]{2,1,0:T(8,128)(2,1)S(1)}, u32[]{:S(2)}, u32[]{:S(2)}) %all-to-all-start.1) | async-done | bytes 294944 | tf_op jit(solution)/shard_map/all_to_all | solution.py:227
  58.0 1.9 %collective-permute-start.1 = (bf16[128,1152]{1,0:T(8,128)(2,1)S(1)}, bf16[128,1152]{1,0:T(8,128)(2,1)S(1)}, u32[]{:S(2)}, u32[]{:S(2)}) collective-permute-start(bf16[128,1152]{1,0:T(8,128)(2,1)S(1)} %bitcast.17), channel_id=1, source_target_pairs={{0,16},{16,0},{1,17},{17,1},{2,18},{18,2},{3,19},{19,3},{4,20},{20... | collective-permute-start | bytes 884744 | tf_op jit(solution)/shard_map/ppermute | solution.py:229
  61.2 0.3 collective-permute-done.1.d
  61.5 0.0 collective-permute-done.b
  61.5 1.3 %shard_map.78 = (f32[128,1280]{1,0:T(8,128)S(1)}, f32[128,1280]{1,0:T(8,128)S(1)}, bf16[256,256]{1,0:T(8,128)(2,1)S(1)}, f32[256,128]{1,0:T(8,128)S(1)}) custom-call(bf16[128,1280]{1,0:T(8,128)(2,1)S(1)} %bitcast.15, bf16[128,1280]{1,0:T(8,128)(2,1)S(1)} %collective-permute-done.b, bf16[128,1152]{1,0:T(8,128)(2,1)S(1)} %bitcast.18, ...), custom_call_target="tpu_custom_call" | custom-call | flops 301989888 | bytes 4980768 | tf_op jit(solution)/shard_map/pallas_call | solution.py:201
  62.8 2.2 %collective-permute-start.3 = (f32[128,1280]{1,0:T(8,128)S(1)}, f32[128,1280]{1,0:T(8,128)S(1)}, u32[]{:S(2)}, u32[]{:S(2)}) collective-permute-start(f32[128,1280]{1,0:T(8,128)S(1)} %get-tuple-element.22), channel_id=1, source_target_pairs={{0,16},{16,0},{1,17},{17,1},{2,18},{18,2},{3,19},{19,3},{4,20},{20... | collective-permute-start | bytes 1966088 | tf_op jit(solution)/shard_map/ppermute | solution.py:245
  65.0 1.8 %collective-permute-done.3.came_ref = f32[128,1280]{1,0:T(8,128)S(1)} collective-permute-done((f32[128,1280]{1,0:T(8,128)S(1)}, f32[128,1280]{1,0:T(8,128)S(1)}, u32[]{:S(2)}, u32[]{:S(2)}) %collective-permute-start.3) | collective-permute-done | bytes 655392 | tf_op jit(solution)/shard_map/ppermute | solution.py:245
  66.8 0.9 shard_map.80
  67.7 4.4 %all-to-all-start.2 = ((bf16[16,8,1280]{2,1,0:T(8,128)(2,1)}), bf16[16,8,1280]{2,1,0:T(8,128)(2,1)S(1)}, u32[]{:S(2)}, u32[]{:S(2)}) async-start(bf16[16,8,1280]{2,1,0:T(8,128)(2,1)} %bitcast.4), calls=%async_computation.2 | async-start | bytes 655360 | tf_op jit(solution)/shard_map/all_to_all | solution.py:252
  72.1 0.4 shard_map.79
  72.4 3.2 %collective-permute-start.2 = (bf16[128,1280]{1,0:T(8,128)(2,1)S(1)}, bf16[128,1280]{1,0:T(8,128)(2,1)S(1)}, u32[]{:S(2)}, u32[]{:S(2)}) collective-permute-start(bf16[128,1280]{1,0:T(8,128)(2,1)S(1)} %get-tuple-element.20), channel_id=1, source_target_pairs={{0,1},{1,0},{2,3},{3,2},{4,5},{5,4},{6,7},{7,6},{8,9},{9,8},{10,11... | collective-permute-start | bytes 983048 | tf_op jit(solution)/shard_map/ppermute | solution.py:253
  75.7 8.3 %collective-permute-done.2.came_ref = bf16[128,1280]{1,0:T(8,128)(2,1)S(1)} collective-permute-done((bf16[128,1280]{1,0:T(8,128)(2,1)S(1)}, bf16[128,1280]{1,0:T(8,128)(2,1)S(1)}, u32[]{:S(2)}, u32[]{:S(2)}) %collective-permute-start.2) | collective-permute-done | bytes 327712 | tf_op jit(solution)/shard_map/ppermute | solution.py:253
  83.9 2.8 %all-to-all-done.2 = bf16[16,8,1280]{2,1,0:T(8,128)(2,1)S(1)} async-done(((bf16[16,8,1280]{2,1,0:T(8,128)(2,1)}), bf16[16,8,1280]{2,1,0:T(8,128)(2,1)S(1)}, u32[]{:S(2)}, u32[]{:S(2)}) %all-to-all-start.2) | async-done | bytes 327712 | tf_op jit(solution)/shard_map/all_to_all | solution.py:252
  86.8 0.3 shard_map.81
  87.0 20.1 %all_to_all.44 = bf16[16,8,1280]{2,1,0:T(8,128)(2,1)S(1)} all-to-all(bf16[16,8,1280]{2,1,0:T(8,128)(2,1)S(1)} %bitcast.20), channel_id=1, replica_groups=mesh['zh'=4,'z0'=2,'x1'=2,'x0'=2,'core'=2,'xh'=2,'yh'=4,'y0'=2] {'x0','z..., dimensions={0} | all-to-all | bytes 655360 | tf_op jit(solution)/shard_map/all_to_all | solution.py:257
  107.1 0.0 copy-start.1
  107.1 0.0 copy-start.3
  107.1 0.2 shard_map.84
  107.3 2.4 %collective-permute-start.4 = (f32[8,128]{1,0:T(8,128)S(1)}, f32[8,128]{1,0:T(8,128)S(1)}, u32[]{:S(2)}, u32[]{:S(2)}) collective-permute-start(f32[8,128]{1,0:T(8,128)S(1)} %shard_map.84), channel_id=1, source_target_pairs={{0,1},{1,0},{2,3},{3,2},{4,5},{5,4},{6,7},{7,6},{8,9},{9,8},{10,11... | collective-permute-start | bytes 12296 | tf_op jit(solution)/shard_map/ppermute | solution.py:261
  109.7 0.0 copy-done.1
  109.8 0.0 copy-done.3
  109.8 0.0 copy-start
  109.8 0.0 copy-start.2
  109.8 0.8 shard_map.83
  110.6 0.0 copy-done
  110.6 0.0 copy-done.2
  110.6 0.8 shard_map.82
  111.4 1.4 %collective-permute-done.4 = f32[8,128]{1,0:T(8,128)S(1)} collective-permute-done((f32[8,128]{1,0:T(8,128)S(1)}, f32[8,128]{1,0:T(8,128)S(1)}, u32[]{:S(2)}, u32[]{:S(2)}) %collective-permute-start.4) | collective-permute-done | bytes 4128 | tf_op jit(solution)/shard_map/ppermute | solution.py:261
  112.8 0.5 slice_bitcast_fusion
  (1 shorter events, 0.0 us)
Async XLA Ops:
  2.3 22.4 %all-to-all-start = ((bf16[16,8,1280]{2,1,0:T(8,128)(2,1)}), bf16[16,8,1280]{2,1,0:T(8,128)(2,1)S(1)}, u32[]{:S(2)}, u32[]{:S(2)}) async-start(bf16[16,8,1280]{2,1,0:T(8,128)(2,1)} %bitcast.21), calls=%async_computation | async-start | bytes 655360 | tf_op jit(solution)/shard_map/all_to_all | solution.py:226
  24.7 33.3 %all-to-all-start.1 = ((bf16[16,8,1152]{2,1,0:T(8,128)(2,1)}), bf16[16,8,1152]{2,1,0:T(8,128)(2,1)S(1)}, u32[]{:S(2)}, u32[]{:S(2)}) async-start(bf16[16,8,1152]{2,1,0:T(8,128)(2,1)} %bitcast.22), calls=%async_computation.1 | async-start | bytes 589824 | tf_op jit(solution)/shard_map/all_to_all | solution.py:227
  44.3 17.2 %collective-permute-start = (bf16[128,1280]{1,0:T(8,128)(2,1)S(1)}, bf16[128,1280]{1,0:T(8,128)(2,1)S(1)}, u32[]{:S(2)}, u32[]{:S(2)}) collective-permute-start(bf16[128,1280]{1,0:T(8,128)(2,1)S(1)} %bitcast.14), channel_id=1, source_target_pairs={{0,1},{1,0},{2,3},{3,2},{4,5},{5,4},{6,7},{7,6},{8,9},{9,8},{10,11... | collective-permute-start | bytes 983048 | tf_op jit(solution)/shard_map/ppermute | solution.py:228
  58.0 3.5 %collective-permute-start.1 = (bf16[128,1152]{1,0:T(8,128)(2,1)S(1)}, bf16[128,1152]{1,0:T(8,128)(2,1)S(1)}, u32[]{:S(2)}, u32[]{:S(2)}) collective-permute-start(bf16[128,1152]{1,0:T(8,128)(2,1)S(1)} %bitcast.17), channel_id=1, source_target_pairs={{0,16},{16,0},{1,17},{17,1},{2,18},{18,2},{3,19},{19,3},{4,20},{20... | collective-permute-start | bytes 884744 | tf_op jit(solution)/shard_map/ppermute | solution.py:229
  62.8 4.0 %collective-permute-start.3 = (f32[128,1280]{1,0:T(8,128)S(1)}, f32[128,1280]{1,0:T(8,128)S(1)}, u32[]{:S(2)}, u32[]{:S(2)}) collective-permute-start(f32[128,1280]{1,0:T(8,128)S(1)} %get-tuple-element.22), channel_id=1, source_target_pairs={{0,16},{16,0},{1,17},{17,1},{2,18},{18,2},{3,19},{19,3},{4,20},{20... | collective-permute-start | bytes 1966088 | tf_op jit(solution)/shard_map/ppermute | solution.py:245
  67.7 19.1 %all-to-all-start.2 = ((bf16[16,8,1280]{2,1,0:T(8,128)(2,1)}), bf16[16,8,1280]{2,1,0:T(8,128)(2,1)S(1)}, u32[]{:S(2)}, u32[]{:S(2)}) async-start(bf16[16,8,1280]{2,1,0:T(8,128)(2,1)} %bitcast.4), calls=%async_computation.2 | async-start | bytes 655360 | tf_op jit(solution)/shard_map/all_to_all | solution.py:252
  72.4 11.5 %collective-permute-start.2 = (bf16[128,1280]{1,0:T(8,128)(2,1)S(1)}, bf16[128,1280]{1,0:T(8,128)(2,1)S(1)}, u32[]{:S(2)}, u32[]{:S(2)}) collective-permute-start(bf16[128,1280]{1,0:T(8,128)(2,1)S(1)} %get-tuple-element.20), channel_id=1, source_target_pairs={{0,1},{1,0},{2,3},{3,2},{4,5},{5,4},{6,7},{7,6},{8,9},{9,8},{10,11... | collective-permute-start | bytes 983048 | tf_op jit(solution)/shard_map/ppermute | solution.py:253
  107.1 2.6 %copy-start.1 = (f32[8,1152]{1,0:T(8,128)S(1)}, f32[8,1152]{1,0:T(8,128)}, u32[]{:S(2)}) copy-start(f32[8,1152]{1,0:T(8,128)} %get-tuple-element.25.unit_ref) | copy-start | bytes 110596
  107.1 2.6 %copy-start.3 = (f32[8,1]{1,0:T(8,128)S(1)}, f32[8,1]{1,0:T(8,128)}, u32[]{:S(2)}) copy-start(f32[8,1]{1,0:T(8,128)} %get-tuple-element.26.norm_ref) | copy-start | bytes 100
  107.3 5.5 %collective-permute-start.4 = (f32[8,128]{1,0:T(8,128)S(1)}, f32[8,128]{1,0:T(8,128)S(1)}, u32[]{:S(2)}, u32[]{:S(2)}) collective-permute-start(f32[8,128]{1,0:T(8,128)S(1)} %shard_map.84), channel_id=1, source_target_pairs={{0,1},{1,0},{2,3},{3,2},{4,5},{5,4},{6,7},{7,6},{8,9},{9,8},{10,11... | collective-permute-start | bytes 12296 | tf_op jit(solution)/shard_map/ppermute | solution.py:261
  109.8 0.8 copy-start
  109.8 0.8 copy-start.2

commit v8 on v7

--- a/solution.py
+++ b/solution.py
@@ -14,7 +14,9 @@
 IMAGE_ORDER = ("zh", "z0", "x1", "x0", "core", "xh", "yh", "y0")
 TEXT_ORDER = ("xh", "yh", "y0", "zh", "z0", "x1", "x0", "core")
 TEXT_GROUP = ("xh", "x1", "zh")
-IMAGE_GROUP = ("x0", "z0", "yh")
+IMAGE_GROUP = ("z0", "x0", "yh")
+GATHER_GROUP = ("x0", "yh")
+GATHER_PAIR = "z0"
 PAIR = "y0"
 VMEM = pl.BlockSpec(memory_space=pltpu.VMEM)
 SMEM = pl.BlockSpec(memory_space=pltpu.SMEM)
@@ -85,6 +87,15 @@
     return jnp.concatenate([r[:, cols] for r in piece_refs], axis=0)
 
 
+def in_order(refs, cols):
+    first = lax.axis_index(GATHER_PAIR) == 0
+    rows = []
+    for own, other in zip(refs[::2], refs[1::2]):
+        own, other = own[:, cols], other[:, cols]
+        rows += [jnp.where(first, own, other), jnp.where(first, other, own)]
+    return jnp.concatenate(rows, axis=0)
+
+
 def scale_of(log_scale_ref):
     return jnp.exp(jnp.zeros((8, 128), F32) + log_scale_ref[0])[0:1, 0:1]
 
@@ -95,9 +106,9 @@
     count, width = text_refs[0].shape
     scale = scale_of(log_scale_ref)
     column = text_columns(own_rows, sizes, count).astype(F32)
-    image = stacked(image_refs, slice(0, width))
+    image = in_order(image_refs, slice(0, width))
     text = stacked(text_refs, slice(0, width))
-    extra = stacked(image_refs, slice(width, width + EXTRA)).astype(F32)
+    extra = in_order(image_refs, slice(width, width + EXTRA)).astype(F32)
     pair = extra[:, 0:1] * 128.0 + extra[:, 1:2]
     cosine = lax.dot_general(image, text, (((1,), (1,)), ((), ())), preferred_element_type=F32)
     scaled = scale * cosine
@@ -144,16 +155,16 @@
     count, width = text_refs[0].shape
     scale = scale_of(log_scale_ref)
     half = low_ref.shape[0] // 2
-    for target, image_ref, rows in (
-        (away_out, image_refs[1], slice(half, 2 * half)),
-        (stay_out, image_refs[0], slice(0, half)),
+    for target, pieces, rows in (
+        (away_out, image_refs[2:], slice(half, 2 * half)),
+        (stay_out, image_refs[:2], slice(0, half)),
     ):
         low, along = low_ref[rows, :], along_ref[rows, :]
         block = width // 3
         for first in range(0, width, block):
             cols = slice(first, first + block)
             part = scale * jnp.dot(low, stacked(text_refs, cols), preferred_element_type=F32)
-            part = part - along[:, 0:1] * image_ref[:, cols].astype(F32)
+            part = part - along[:, 0:1] * in_order(pieces, cols).astype(F32)
             target[:, cols] = part.astype(target.dtype)
         target[:, width:] = along.astype(target.dtype)
 
@@ -215,25 +226,29 @@
     row_count = math.prod(sizes[a] for a in IMAGE_GROUP) * own_rows
     text_count = math.prod(sizes[a] for a in TEXT_GROUP) * own_rows
     unit_shape, norm_shape = shape(own_rows, width, dtype=F32), shape(own_rows, 1, dtype=F32)
+    gather_count = math.prod(sizes[a] for a in GATHER_GROUP) * own_rows
     image_send, image_unit, image_norm = call(
-        pack_image_kernel, (shape(row_count, wide), unit_shape, norm_shape),
+        pack_image_kernel, (shape(gather_count, wide), unit_shape, norm_shape),
         image_embed, pair_index, scalars=1, limit=None,
     )
     text_send, text_unit, text_norm = call(
         pack_text_kernel, (shape(text_count, width), unit_shape, norm_shape), text_embed, limit=None
     )
     swap = [(0, 1), (1, 0)]
-    piece = lax.all_to_all(image_send, IMAGE_GROUP, 0, 0, tiled=True)
+    piece = lax.all_to_all(image_send, GATHER_GROUP, 0, 0, tiled=True)
     text = lax.all_to_all(text_send, TEXT_GROUP, 0, 0, tiled=True)
+    piece_near = lax.ppermute(piece, GATHER_PAIR, swap)
     piece_pair = lax.ppermute(piece, PAIR, swap)
+    piece_both = lax.ppermute(piece_near, PAIR, swap)
+    text, piece_pair, piece_both = lax.optimization_barrier((text, piece_pair, piece_both))
     text_core = lax.ppermute(text, "core", swap)
-    held = (piece, piece_pair, text, text_core)
-
-    def score(a, b, c, d, *rest):
-        score_kernel(own_rows, sizes, (a, b), (c, d), *rest)
-
-    def image_partials(a, b, c, d, *rest):
-        image_kernel((a, b), (c, d), *rest)
+    held = (piece, piece_near, piece_pair, piece_both, text, text_core)
+
+    def score(*refs):
+        score_kernel(own_rows, sizes, refs[:4], refs[4:6], *refs[6:])
+
+    def image_partials(*refs):
+        image_kernel(refs[:4], refs[4:6], *refs[6:])
 
     work = 2 * 4 * row_count * text_count * width
     text_half = shape(text_count, wide, dtype=F32)

time: 114 us -> 120 us (1.053)
  starting transfers between devices: 47.1 us -> 59.3 us
  waiting for transfers between devices: 35.7 us -> 30.4 us
    all_to_all x1, waiting for transfers between devices: 10.7 us -> 0.01 us  [per_device(): text = lax.all_to_all(text_send, TEXT_GROUP, 0, 0, tiled=True)]
    ppermute x0 -> x2, waiting for transfers between devices: none -> 8.35 us  [the longest x1 4.56 us: per_device(): piece_near = lax.ppermute(piece, GATHER_PAIR, swap)]
    ppermute x0 -> x2, starting transfers between devices: none -> 8.2 us  [the longest x1 4.82 us: per_device(): piece_near = lax.ppermute(piece, GATHER_PAIR, swap)]
    all_to_all x1, starting transfers between devices: 4.38 us -> 10.7 us  [per_device(): text_back = lax.all_to_all(text_parts, TEXT_GROUP, 0, 0, tiled=True)]
    all_to_all x1, starting transfers between devices: 10.4 us -> 7.58 us  [per_device(): piece = lax.all_to_all(image_send, GATHER_GROUP, 0, 0, tiled=True)]
    all_to_all x1, waiting for transfers between devices: 10.4 us -> 7.63 us  [per_device(): piece = lax.all_to_all(image_send, GATHER_GROUP, 0, 0, tiled=True)]
  transfers between devices with their start and end apart: 8 -> 10, of which waited for: 7 -> 8; matrix products, arithmetic and copies ran while one was open for 0% -> 0% of each run, Pallas kernels for 3% -> 3%
where the time goes in v8:
time: 120 us; the launch traced here: 119 us
  starting transfers between devices  59.3 us (49%)
  waiting for transfers between devices  30.4 us (25%)
  blocking collectives  19.2 us (16%)
  Pallas kernels  7.75 us (6%)
  between operations  2.08 us (2%)
    all_to_all x1, starting transfers between devices, per_device(): text = lax.all_to_all(text_send, TEXT_GROUP, 0, 0, tiled=True)  20 us
    all_to_all x1, blocking collectives, per_device(): image_back = lax.all_to_all(image_parts, IMAGE_GROUP, 0, 0, tiled=True)  19.2 us
    all_to_all x1, starting transfers between devices, per_device(): text_back = lax.all_to_all(text_parts, TEXT_GROUP, 0, 0, tiled=True)  10.7 us
    ppermute x1, waiting for transfers between devices, per_device(): came_pair = lax.ppermute(send, PAIR, swap)  7.83 us
    pallas_call x9, Pallas kernels, call(): pl.pallas_call(kernel, out_shape=outs, in_specs=[VMEM] * (len(args) - sca...  7.75 us
    all_to_all x1, waiting for transfers between devices, per_device(): piece = lax.all_to_all(image_send, GATHER_GROUP, 0, 0, tiled=True)  7.63 us
    all_to_all x1, starting transfers between devices, per_device(): piece = lax.all_to_all(image_send, GATHER_GROUP, 0, 0, tiled=True)  7.58 us
    ppermute x1, starting transfers between devices, per_device(): piece_near = lax.ppermute(piece, GATHER_PAIR, swap)  4.82 us
  transfers between devices with their start and end apart: 10, of which 8 were waited for; matrix products, arithmetic and copies ran while one was open for 0% of the time, Pallas kernels for 3%

profile of v8, /device:TPU:16, one launch (start us, length us, event | category | flops | bytes accessed | tf_op | source)
XLA Modules:
  0.0 119.2 jit_solution(9260693016661124892)
XLA Ops:
  0.6 1.6 %shard_map.76 = (bf16[64,1280]{1,0:T(8,128)(2,1)}, f32[8,1152]{1,0:T(8,128)}, f32[8,1]{1,0:T(8,128)}) custom-call(bf16[8,1152]{1,0:T(8,128)(2,1)} %image_ref.1, s32[8]{0:T(128)} %pair_ref.1), custom_call_target="tpu_custom_call" | custom-call | bytes 73856 | tf_op jit(solution)/shard_map/pallas_call | solution.py:212
  2.2 7.6 %all-to-all-start = ((bf16[8,8,1280]{2,1,0:T(8,128)(2,1)}), bf16[8,8,1280]{2,1,0:T(8,128)(2,1)S(1)}, u32[]{:S(2)}, u32[]{:S(2)}) async-start(bf16[8,8,1280]{2,1,0:T(8,128)(2,1)} %bitcast.23), calls=%async_computation | async-start | bytes 327680 | tf_op jit(solution)/shard_map/all_to_all | solution.py:238
  9.8 1.6 %shard_map.77 = (bf16[128,1152]{1,0:T(8,128)(2,1)}, f32[8,1152]{1,0:T(8,128)}, f32[8,1]{1,0:T(8,128)}) custom-call(bf16[8,1152]{1,0:T(8,128)(2,1)} %text_ref.1), custom_call_target="tpu_custom_call" | custom-call | bytes 73728 | tf_op jit(solution)/shard_map/pallas_call | solution.py:212
  11.4 7.6 %all-to-all-done = bf16[8,8,1280]{2,1,0:T(8,128)(2,1)S(1)} async-done(((bf16[8,8,1280]{2,1,0:T(8,128)(2,1)}), bf16[8,8,1280]{2,1,0:T(8,128)(2,1)S(1)}, u32[]{:S(2)}, u32[]{:S(2)}) %all-to-all-start) | async-done | bytes 163872 | tf_op jit(solution)/shard_map/all_to_all | solution.py:238
  19.0 20.0 %all-to-all-start.1 = ((bf16[16,8,1152]{2,1,0:T(8,128)(2,1)}), bf16[16,8,1152]{2,1,0:T(8,128)(2,1)S(1)}, u32[]{:S(2)}, u32[]{:S(2)}) async-start(bf16[16,8,1152]{2,1,0:T(8,128)(2,1)} %bitcast.22), calls=%async_computation.1 | async-start | bytes 589824 | tf_op jit(solution)/shard_map/all_to_all | solution.py:239
  38.9 4.8 %collective-permute-start = (bf16[64,1280]{1,0:T(8,128)(2,1)S(1)}, bf16[64,1280]{1,0:T(8,128)(2,1)S(1)}, u32[]{:S(2)}, u32[]{:S(2)}) collective-permute-start(bf16[64,1280]{1,0:T(8,128)(2,1)S(1)} %bitcast.17), channel_id=1, source_target_pairs={{0,128},{128,0},{1,129},{129,1},{2,130},{130,2},{3,131},{131,3},{4... | collective-permute-start | bytes 491528 | tf_op jit(solution)/shard_map/ppermute | solution.py:240
  43.8 3.1 %collective-permute-start.1 = (bf16[64,1280]{1,0:T(8,128)(2,1)S(1)}, bf16[64,1280]{1,0:T(8,128)(2,1)S(1)}, u32[]{:S(2)}, u32[]{:S(2)}) collective-permute-start(bf16[64,1280]{1,0:T(8,128)(2,1)S(1)} %bitcast.18), channel_id=1, source_target_pairs={{0,1},{1,0},{2,3},{3,2},{4,5},{5,4},{6,7},{7,6},{8,9},{9,8},{10,11... | collective-permute-start | bytes 491528 | tf_op jit(solution)/shard_map/ppermute | solution.py:241
  46.9 4.6 %collective-permute-done.refs_1_ = bf16[64,1280]{1,0:T(8,128)(2,1)S(1)} collective-permute-done((bf16[64,1280]{1,0:T(8,128)(2,1)S(1)}, bf16[64,1280]{1,0:T(8,128)(2,1)S(1)}, u32[]{:S(2)}, u32[]{:S(2)}) %collective-permute-start) | collective-permute-done | bytes 163872 | tf_op jit(solution)/shard_map/ppermute | solution.py:240
  51.5 3.4 %collective-permute-start.2 = (bf16[64,1280]{1,0:T(8,128)(2,1)S(1)}, bf16[64,1280]{1,0:T(8,128)(2,1)S(1)}, u32[]{:S(2)}, u32[]{:S(2)}) collective-permute-start(bf16[64,1280]{1,0:T(8,128)(2,1)S(1)} %collective-permute-done.refs_1_), channel_id=1, source_target_pairs={{0,1},{1,0},{2,3},{3,2},{4,5},{5,4},{6,7},{7,6},{8,9},{9,8},{10,11... | collective-permute-start | bytes 491528 | tf_op jit(solution)/shard_map/ppermute | solution.py:242
  54.9 0.0 collective-permute-done.1.refs_2_
  54.9 0.0 all-to-all-done.1
  54.9 3.8 %collective-permute-done.2.refs_3_ = bf16[64,1280]{1,0:T(8,128)(2,1)S(1)} collective-permute-done((bf16[64,1280]{1,0:T(8,128)(2,1)S(1)}, bf16[64,1280]{1,0:T(8,128)(2,1)S(1)}, u32[]{:S(2)}, u32[]{:S(2)}) %collective-permute-start.2) | collective-permute-done | bytes 163872 | tf_op jit(solution)/shard_map/ppermute | solution.py:242
  58.7 1.9 %collective-permute-start.3 = (bf16[128,1152]{1,0:T(8,128)(2,1)S(1)}, bf16[128,1152]{1,0:T(8,128)(2,1)S(1)}, u32[]{:S(2)}, u32[]{:S(2)}) collective-permute-start(bf16[128,1152]{1,0:T(8,128)(2,1)S(1)} %bitcast.14), channel_id=1, source_target_pairs={{0,16},{16,0},{1,17},{17,1},{2,18},{18,2},{3,19},{19,3},{4,20},{20... | collective-permute-start | bytes 884744 | tf_op jit(solution)/shard_map/ppermute | solution.py:244
  61.9 0.3 collective-permute-done.3.refs_5_
  62.2 1.3 %shard_map.78 = (f32[128,1280]{1,0:T(8,128)S(1)}, f32[128,1280]{1,0:T(8,128)S(1)}, bf16[256,256]{1,0:T(8,128)(2,1)S(1)}, f32[256,128]{1,0:T(8,128)S(1)}) custom-call(bf16[64,1280]{1,0:T(8,128)(2,1)S(1)} %bitcast.19, bf16[64,1280]{1,0:T(8,128)(2,1)S(1)} %collective-permute-done.refs_1_, bf16[64,1280]{1,0:T(8,128)(2,1)S(1)} %collective-permute-done.1.refs_2_, ...), custom_call_target="tpu_custom_call" | custom-call | flops 301989888 | bytes 4980768 | tf_op jit(solution)/shard_map/pallas_call | solution.py:212
  63.5 2.2 %collective-permute-start.5 = (f32[128,1280]{1,0:T(8,128)S(1)}, f32[128,1280]{1,0:T(8,128)S(1)}, u32[]{:S(2)}, u32[]{:S(2)}) collective-permute-start(f32[128,1280]{1,0:T(8,128)S(1)} %get-tuple-element.28), channel_id=1, source_target_pairs={{0,16},{16,0},{1,17},{17,1},{2,18},{18,2},{3,19},{19,3},{4,20},{20... | collective-permute-start | bytes 1966088 | tf_op jit(solution)/shard_map/ppermute | solution.py:260
  65.6 1.8 %collective-permute-done.5.came_ref = f32[128,1280]{1,0:T(8,128)S(1)} collective-permute-done((f32[128,1280]{1,0:T(8,128)S(1)}, f32[128,1280]{1,0:T(8,128)S(1)}, u32[]{:S(2)}, u32[]{:S(2)}) %collective-permute-start.5) | collective-permute-done | bytes 655392 | tf_op jit(solution)/shard_map/ppermute | solution.py:260
  67.5 0.9 shard_map.80
  68.4 10.7 %all-to-all-start.2 = ((bf16[16,8,1280]{2,1,0:T(8,128)(2,1)}), bf16[16,8,1280]{2,1,0:T(8,128)(2,1)S(1)}, u32[]{:S(2)}, u32[]{:S(2)}) async-start(bf16[16,8,1280]{2,1,0:T(8,128)(2,1)} %bitcast.4), calls=%async_computation.2 | async-start | bytes 655360 | tf_op jit(solution)/shard_map/all_to_all | solution.py:267
  79.0 0.4 shard_map.79
  79.4 3.6 %collective-permute-start.4 = (bf16[128,1280]{1,0:T(8,128)(2,1)S(1)}, bf16[128,1280]{1,0:T(8,128)(2,1)S(1)}, u32[]{:S(2)}, u32[]{:S(2)}) collective-permute-start(bf16[128,1280]{1,0:T(8,128)(2,1)S(1)} %get-tuple-element.26), channel_id=1, source_target_pairs={{0,1},{1,0},{2,3},{3,2},{4,5},{5,4},{6,7},{7,6},{8,9},{9,8},{10,11... | collective-permute-start | bytes 983048 | tf_op jit(solution)/shard_map/ppermute | solution.py:268
  83.1 7.8 %collective-permute-done.4.came_ref = bf16[128,1280]{1,0:T(8,128)(2,1)S(1)} collective-permute-done((bf16[128,1280]{1,0:T(8,128)(2,1)S(1)}, bf16[128,1280]{1,0:T(8,128)(2,1)S(1)}, u32[]{:S(2)}, u32[]{:S(2)}) %collective-permute-start.4) | collective-permute-done | bytes 327712 | tf_op jit(solution)/shard_map/ppermute | solution.py:268
  90.9 2.7 %all-to-all-done.2 = bf16[16,8,1280]{2,1,0:T(8,128)(2,1)S(1)} async-done(((bf16[16,8,1280]{2,1,0:T(8,128)(2,1)}), bf16[16,8,1280]{2,1,0:T(8,128)(2,1)S(1)}, u32[]{:S(2)}, u32[]{:S(2)}) %all-to-all-start.2) | async-done | bytes 327712 | tf_op jit(solution)/shard_map/all_to_all | solution.py:267
  93.6 0.3 shard_map.81
  93.8 19.2 %all_to_all.45 = bf16[16,8,1280]{2,1,0:T(8,128)(2,1)S(1)} all-to-all(bf16[16,8,1280]{2,1,0:T(8,128)(2,1)S(1)} %bitcast.21), channel_id=1, replica_groups=mesh['zh'=4,'z0'=2,'x1'=2,'x0'=2,'core'=2,'xh'=2,'yh'=4,'y0'=2] {'z0','x..., dimensions={0} | all-to-all | bytes 655360 | tf_op jit(solution)/shard_map/all_to_all | solution.py:272
  113.0 0.0 copy-start.1
  113.0 0.0 copy-start.3
  113.0 0.2 shard_map.84
  113.2 2.1 %collective-permute-start.6 = (f32[8,128]{1,0:T(8,128)S(1)}, f32[8,128]{1,0:T(8,128)S(1)}, u32[]{:S(2)}, u32[]{:S(2)}) collective-permute-start(f32[8,128]{1,0:T(8,128)S(1)} %shard_map.84), channel_id=1, source_target_pairs={{0,1},{1,0},{2,3},{3,2},{4,5},{5,4},{6,7},{7,6},{8,9},{9,8},{10,11... | collective-permute-start | bytes 12296 | tf_op jit(solution)/shard_map/ppermute | solution.py:276
  115.3 0.0 copy-done.1
  115.3 0.0 copy-done.3
  115.3 0.0 copy-start
  115.3 0.0 copy-start.2
  115.3 0.8 shard_map.83
  116.1 0.0 copy-done
  116.1 0.0 copy-done.2
  116.1 0.8 shard_map.82
  116.9 1.8 %collective-permute-done.6 = f32[8,128]{1,0:T(8,128)S(1)} collective-permute-done((f32[8,128]{1,0:T(8,128)S(1)}, f32[8,128]{1,0:T(8,128)S(1)}, u32[]{:S(2)}, u32[]{:S(2)}) %collective-permute-start.6) | collective-permute-done | bytes 4128 | tf_op jit(solution)/shard_map/ppermute | solution.py:276
  118.7 0.5 slice_bitcast_fusion
  (1 shorter events, 0.0 us)
Async XLA Ops:
  2.2 16.8 %all-to-all-start = ((bf16[8,8,1280]{2,1,0:T(8,128)(2,1)}), bf16[8,8,1280]{2,1,0:T(8,128)(2,1)S(1)}, u32[]{:S(2)}, u32[]{:S(2)}) async-start(bf16[8,8,1280]{2,1,0:T(8,128)(2,1)} %bitcast.23), calls=%async_computation | async-start | bytes 327680 | tf_op jit(solution)/shard_map/all_to_all | solution.py:238
  19.0 35.9 %all-to-all-start.1 = ((bf16[16,8,1152]{2,1,0:T(8,128)(2,1)}), bf16[16,8,1152]{2,1,0:T(8,128)(2,1)S(1)}, u32[]{:S(2)}, u32[]{:S(2)}) async-start(bf16[16,8,1152]{2,1,0:T(8,128)(2,1)} %bitcast.22), calls=%async_computation.1 | async-start | bytes 589824 | tf_op jit(solution)/shard_map/all_to_all | solution.py:239
  38.9 12.5 %collective-permute-start = (bf16[64,1280]{1,0:T(8,128)(2,1)S(1)}, bf16[64,1280]{1,0:T(8,128)(2,1)S(1)}, u32[]{:S(2)}, u32[]{:S(2)}) collective-permute-start(bf16[64,1280]{1,0:T(8,128)(2,1)S(1)} %bitcast.17), channel_id=1, source_target_pairs={{0,128},{128,0},{1,129},{129,1},{2,130},{130,2},{3,131},{131,3},{4... | collective-permute-start | bytes 491528 | tf_op jit(solution)/shard_map/ppermute | solution.py:240
  43.8 11.1 %collective-permute-start.1 = (bf16[64,1280]{1,0:T(8,128)(2,1)S(1)}, bf16[64,1280]{1,0:T(8,128)(2,1)S(1)}, u32[]{:S(2)}, u32[]{:S(2)}) collective-permute-start(bf16[64,1280]{1,0:T(8,128)(2,1)S(1)} %bitcast.18), channel_id=1, source_target_pairs={{0,1},{1,0},{2,3},{3,2},{4,5},{5,4},{6,7},{7,6},{8,9},{9,8},{10,11... | collective-permute-start | bytes 491528 | tf_op jit(solution)/shard_map/ppermute | solution.py:241
  51.5 7.2 %collective-permute-start.2 = (bf16[64,1280]{1,0:T(8,128)(2,1)S(1)}, bf16[64,1280]{1,0:T(8,128)(2,1)S(1)}, u32[]{:S(2)}, u32[]{:S(2)}) collective-permute-start(bf16[64,1280]{1,0:T(8,128)(2,1)S(1)} %collective-permute-done.refs_1_), channel_id=1, source_target_pairs={{0,1},{1,0},{2,3},{3,2},{4,5},{5,4},{6,7},{7,6},{8,9},{9,8},{10,11... | collective-permute-start | bytes 491528 | tf_op jit(solution)/shard_map/ppermute | solution.py:242
  58.7 3.5 %collective-permute-start.3 = (bf16[128,1152]{1,0:T(8,128)(2,1)S(1)}, bf16[128,1152]{1,0:T(8,128)(2,1)S(1)}, u32[]{:S(2)}, u32[]{:S(2)}) collective-permute-start(bf16[128,1152]{1,0:T(8,128)(2,1)S(1)} %bitcast.14), channel_id=1, source_target_pairs={{0,16},{16,0},{1,17},{17,1},{2,18},{18,2},{3,19},{19,3},{4,20},{20... | collective-permute-start | bytes 884744 | tf_op jit(solution)/shard_map/ppermute | solution.py:244
  63.5 4.0 %collective-permute-start.5 = (f32[128,1280]{1,0:T(8,128)S(1)}, f32[128,1280]{1,0:T(8,128)S(1)}, u32[]{:S(2)}, u32[]{:S(2)}) collective-permute-start(f32[128,1280]{1,0:T(8,128)S(1)} %get-tuple-element.28), channel_id=1, source_target_pairs={{0,16},{16,0},{1,17},{17,1},{2,18},{18,2},{3,19},{19,3},{4,20},{20... | collective-permute-start | bytes 1966088 | tf_op jit(solution)/shard_map/ppermute | solution.py:260
  68.4 25.2 %all-to-all-start.2 = ((bf16[16,8,1280]{2,1,0:T(8,128)(2,1)}), bf16[16,8,1280]{2,1,0:T(8,128)(2,1)S(1)}, u32[]{:S(2)}, u32[]{:S(2)}) async-start(bf16[16,8,1280]{2,1,0:T(8,128)(2,1)} %bitcast.4), calls=%async_computation.2 | async-start | bytes 655360 | tf_op jit(solution)/shard_map/all_to_all | solution.py:267
  79.4 11.5 %collective-permute-start.4 = (bf16[128,1280]{1,0:T(8,128)(2,1)S(1)}, bf16[128,1280]{1,0:T(8,128)(2,1)S(1)}, u32[]{:S(2)}, u32[]{:S(2)}) collective-permute-start(bf16[128,1280]{1,0:T(8,128)(2,1)S(1)} %get-tuple-element.26), channel_id=1, source_target_pairs={{0,1},{1,0},{2,3},{3,2},{4,5},{5,4},{6,7},{7,6},{8,9},{9,8},{10,11... | collective-permute-start | bytes 983048 | tf_op jit(solution)/shard_map/ppermute | solution.py:268
  113.0 2.3 %copy-start.1 = (f32[8,1152]{1,0:T(8,128)S(1)}, f32[8,1152]{1,0:T(8,128)}, u32[]{:S(2)}) copy-start(f32[8,1152]{1,0:T(8,128)} %get-tuple-element.31.unit_ref) | copy-start | bytes 110596
  113.0 2.3 %copy-start.3 = (f32[8,1]{1,0:T(8,128)S(1)}, f32[8,1]{1,0:T(8,128)}, u32[]{:S(2)}) copy-start(f32[8,1]{1,0:T(8,128)} %get-tuple-element.32.norm_ref) | copy-start | bytes 100
  113.2 5.5 %collective-permute-start.6 = (f32[8,128]{1,0:T(8,128)S(1)}, f32[8,128]{1,0:T(8,128)S(1)}, u32[]{:S(2)}, u32[]{:S(2)}) collective-permute-start(f32[8,128]{1,0:T(8,128)S(1)} %shard_map.84), channel_id=1, source_target_pairs={{0,1},{1,0},{2,3},{3,2},{4,5},{5,4},{6,7},{7,6},{8,9},{9,8},{10,11... | collective-permute-start | bytes 12296 | tf_op jit(solution)/shard_map/ppermute | solution.py:276
  115.3 0.8 copy-start
  115.3 0.8 copy-start.2

commit v9 on v5

--- a/solution.py
+++ b/solution.py
@@ -11,11 +11,10 @@
 EXTRA = 128
 F32 = jnp.float32
 BF16 = jnp.bfloat16
-IMAGE_ORDER = ("zh", "z0", "xl", "core", "xh", "yh", "y0")
-TEXT_ORDER = ("xh", "yh", "y0", "zh", "z0", "xl", "core")
+IMAGE_ORDER = ("z", "xl", "core", "xh", "yh", "y0")
+TEXT_ORDER = ("xh", "yh", "y0", "z", "xl", "core")
 TEXT_GROUP = ("xh", "xl", "yh")
-IMAGE_GROUP = ("zh", "y0")
-PAIR = "z0"
+IMAGE_GROUP = ("z", "y0")
 VMEM = pl.BlockSpec(memory_space=pltpu.VMEM)
 SMEM = pl.BlockSpec(memory_space=pltpu.SMEM)
 
@@ -69,7 +68,7 @@
 def text_columns(own_rows, sizes, count):
     place = lax.broadcasted_iota(jnp.int32, (1, count), 1)
     peer, row = place // own_rows, place % own_rows
-    index = {a: lax.axis_index(a) for a in IMAGE_GROUP + (PAIR, "core")}
+    index = {a: lax.axis_index(a) for a in IMAGE_GROUP + ("core",)}
     for a in reversed(TEXT_GROUP):
         index[a] = peer % sizes[a]
         peer = peer // sizes[a]
@@ -129,8 +128,8 @@
     scale = scale_of(log_scale_ref)
     half = low_ref.shape[0] // 2
     for target, pieces, rows in (
-        (away_out, piece_refs[2:], slice(half, 2 * half)),
-        (stay_out, piece_refs[:2], slice(0, half)),
+        (away_out, piece_refs[1:], slice(half, 2 * half)),
+        (stay_out, piece_refs[:1], slice(0, half)),
     ):
         low, along = low_ref[rows, :], along_ref[rows, :]
         block = width // 3
@@ -147,19 +146,13 @@
     return [total[0:1, n : n + 1] + total[0:1, n + 3 : n + 4] for n in (1, 2, 3)]
 
 
-def add_kernel(stay_ref, came_ref, keep_out, send_out):
-    half = keep_out.shape[0]
-    keep_out[...] = stay_ref[:half, :] + came_ref[:half, :]
-    send_out[...] = (stay_ref[half:, :] + came_ref[half:, :]).astype(BF16)
-
-
 def join_kernel(own_rows, keep_ref, came_ref, text_back_ref, out_ref):
     width = keep_ref.shape[1] - EXTRA
-    out_ref[:, :width] = (keep_ref[:, :width] + came_ref[:, :width].astype(F32)).astype(BF16)
+    out_ref[:, :width] = (keep_ref[:, :width] + came_ref[:, :width]).astype(BF16)
     lane = lanes(keep_ref.shape[0])
     stats = merge_stats(text_back_ref[:, width:].astype(F32), own_rows)
     stats = split_stats(lane, 1, [jnp.broadcast_to(t, lane.shape) for t in stats])
-    along = keep_ref[:, width:] + came_ref[:, width:].astype(F32)
+    along = keep_ref[:, width:] + came_ref[:, width:]
     out_ref[:, width:] = jnp.where(lane == 0, along, stats).astype(BF16)
 
 
@@ -178,7 +171,7 @@
     out = jnp.zeros(lane.shape, F32)
     for n, value in enumerate(merge_stats(parts_ref[:, width:].astype(F32), own_rows)):
         out = jnp.where(lane == n, value / batch, out)
-    out_ref[...] = jnp.broadcast_to(out[None], out_ref.shape)
+    out_ref[...] = out
 
 
 def shape(*dims, dtype=BF16):
@@ -211,51 +204,42 @@
     text_send, text_unit, text_norm = call(
         pack_text_kernel, (shape(text_count, width), unit_shape, norm_shape), text_embed, limit=None
     )
+    swap = [(0, 1), (1, 0)]
     piece = lax.all_to_all(image_send, IMAGE_GROUP, 0, 0, tiled=True)
     text = lax.all_to_all(text_send, TEXT_GROUP, 0, 0, tiled=True)
-    swap = [(0, 1), (1, 0)]
-    piece_pair = lax.ppermute(piece, PAIR, swap)
     piece_core = lax.ppermute(piece, "core", swap)
-    piece_both = lax.ppermute(piece_pair, "core", swap)
-
-    def score(a, b, c, d, *rest):
-        score_kernel(own_rows, sizes, (a, b, c, d), *rest)
-
-    def image_partials(a, b, c, d, *rest):
-        image_kernel((a, b, c, d), *rest)
-
-    pieces = (piece, piece_pair, piece_core, piece_both)
-    work = 2 * 4 * row_count * text_count * width
+
+    def score(*refs):
+        score_kernel(own_rows, sizes, refs[:2], *refs[2:])
+
+    def image_partials(*refs):
+        image_kernel(refs[:2], *refs[2:])
+
+    pieces = (piece, piece_core)
+    work = 2 * 2 * row_count * text_count * width
     text_parts, low, along = call(
         score,
-        (shape(text_count, wide), shape(4 * row_count, text_count), shape(4 * row_count, EXTRA, dtype=F32)),
+        (shape(text_count, wide), shape(2 * row_count, text_count), shape(2 * row_count, EXTRA, dtype=F32)),
         *pieces, text, log_scale, bias, scalars=2, flops=2 * work,
     )
     text_back = lax.all_to_all(text_parts, TEXT_GROUP, 0, 0, tiled=True)
-    half = shape(2 * row_count, wide, dtype=F32)
-    stay, away = call(image_partials, (half, half), *pieces, text, low, along, log_scale, scalars=1, flops=work)
+    half = shape(row_count, wide, dtype=F32)
+    keep, away = call(image_partials, (half, half), *pieces, text, low, along, log_scale, scalars=1, flops=work)
     came = lax.ppermute(away, "core", swap)
-    keep, send = call(
-        add_kernel, (shape(row_count, wide, dtype=F32), shape(row_count, wide)), stay, came
-    )
-    came_pair = lax.ppermute(send, PAIR, swap)
-    image_parts = call(
-        functools.partial(join_kernel, own_rows), shape(row_count, wide), keep, came_pair, text_back
-    )
+    image_parts = call(functools.partial(join_kernel, own_rows), shape(row_count, wide), keep, came, text_back)
     image_back = lax.all_to_all(image_parts, IMAGE_GROUP, 0, 0, tiled=True)
     text_grad = call(finish_kernel, unit_shape, text_back, text_unit, text_norm)
-    four = sizes[PAIR] * sizes["core"]
     batch = own_rows * math.prod(sizes.values())
-    sums = call(functools.partial(stats_kernel, own_rows, batch), shape(four, 8, EXTRA, dtype=F32), image_back)
-    sums = lax.all_to_all(sums, (PAIR, "core"), 0, 0, tiled=True)
+    sums = call(functools.partial(stats_kernel, own_rows, batch), shape(8, EXTRA, dtype=F32), image_back)
+    sums_came = lax.ppermute(sums, "core", swap)
     image_grad = call(finish_kernel, unit_shape, image_back, image_unit, image_norm)
-    stats = jnp.sum(sums[:, 0, :3], axis=0)
+    stats = (sums + sums_came)[0, :3]
     return (image_grad, text_grad, stats)
 
 
 def solution(mesh):
     img, txt = mesh.shape["img"], mesh.shape["txt"]
-    parts = (img // 16, 2, 4, 2, 2, txt // 4, 2)
+    parts = (img // 8, 4, 2, 2, txt // 4, 2)
     split = Mesh(mesh.devices.reshape(parts), IMAGE_ORDER)
     image_spec, text_spec = P(IMAGE_ORDER, None), P(TEXT_ORDER, None)
     return jax.shard_map(

time: 111 us -> 114 us (1.027)
  starting transfers between devices: 65 us -> 52.6 us
  waiting for transfers between devices: 21.2 us -> 33.5 us
  blocking collectives: 13 us -> 16.6 us
    all_to_all x1, waiting for transfers between devices: 3.42 us -> 11.4 us  [per_device(): text_back = lax.all_to_all(text_parts, TEXT_GROUP, 0, 0, tiled=True)]
    all_to_all x1 -> x0, starting transfers between devices: 7.82 us -> none  [per_device(): sums = lax.all_to_all(sums, (PAIR, 'core'), 0, 0, tiled=True)]
    all_to_all x1, waiting for transfers between devices: 3.91 us -> 10.8 us  [per_device(): text = lax.all_to_all(text_send, TEXT_GROUP, 0, 0, tiled=True)]
    ppermute x3 -> x1, starting transfers between devices: 11.8 us -> 5.6 us  [per_device(): sums_came = lax.ppermute(sums, 'core', swap)]
    ppermute x3 -> x1, waiting for transfers between devices: 4.26 us -> 0.01 us  [per_device(): sums_came = lax.ppermute(sums, 'core', swap)]
    all_to_all x1, blocking collectives: 13 us -> 16.6 us  [per_device(): image_back = lax.all_to_all(image_parts, IMAGE_GROUP, 0, 0, tiled=True)]
    all_to_all x1, waiting for transfers between devices: 6.45 us -> 9.51 us  [per_device(): piece = lax.all_to_all(image_send, IMAGE_GROUP, 0, 0, tiled=True)]
    all_to_all x1 -> x0, waiting for transfers between devices: 1.5 us -> none  [per_device(): sums = lax.all_to_all(sums, (PAIR, 'core'), 0, 0, tiled=True)]
  transfers between devices with their start and end apart: 9 -> 6, of which waited for: 6 -> 4; matrix products, arithmetic and copies ran while one was open for 0% -> 0% of each run, Pallas kernels for 3% -> 3%
where the time goes in v9:
time: 114 us; the launch traced here: 113 us
  starting transfers between devices  52.6 us (46%)
  waiting for transfers between devices  33.5 us (29%)
  blocking collectives  16.6 us (15%)
  Pallas kernels  7.87 us (7%)
  between operations  2.04 us (2%)
    all_to_all x1, starting transfers between devices, per_device(): piece = lax.all_to_all(image_send, IMAGE_GROUP, 0, 0, tiled=True)  18.5 us
    all_to_all x1, blocking collectives, per_device(): image_back = lax.all_to_all(image_parts, IMAGE_GROUP, 0, 0, tiled=True)  16.6 us
    all_to_all x1, starting transfers between devices, per_device(): text = lax.all_to_all(text_send, TEXT_GROUP, 0, 0, tiled=True)  11.7 us
    all_to_all x1, waiting for transfers between devices, per_device(): text_back = lax.all_to_all(text_parts, TEXT_GROUP, 0, 0, tiled=True)  11.4 us
    all_to_all x1, waiting for transfers between devices, per_device(): text = lax.all_to_all(text_send, TEXT_GROUP, 0, 0, tiled=True)  10.8 us
    all_to_all x1, waiting for transfers between devices, per_device(): piece = lax.all_to_all(image_send, IMAGE_GROUP, 0, 0, tiled=True)  9.51 us
    pallas_call x8, Pallas kernels, call(): pl.pallas_call(kernel, out_shape=outs, in_specs=[VMEM] * (len(args) - sca...  7.87 us
    all_to_all x1, starting transfers between devices, per_device(): text_back = lax.all_to_all(text_parts, TEXT_GROUP, 0, 0, tiled=True)  7.54 us
  transfers between devices with their start and end apart: 6, of which 4 were waited for; matrix products, arithmetic and copies ran while one was open for 0% of the time, Pallas kernels for 3%

profile of v9, /device:TPU:1, one launch (start us, length us, event | category | flops | bytes accessed | tf_op | source)
XLA Modules:
  0.0 113.1 jit_solution(9504547169755906683)
XLA Ops:
  0.6 1.6 %shard_map.76 = (bf16[128,1280]{1,0:T(8,128)(2,1)}, f32[8,1152]{1,0:T(8,128)}, f32[8,1]{1,0:T(8,128)}) custom-call(bf16[8,1152]{1,0:T(8,128)(2,1)} %image_ref.1, s32[8]{0:T(128)} %pair_ref.1), custom_call_target="tpu_custom_call" | custom-call | bytes 73856 | tf_op jit(solution)/shard_map/pallas_call | solution.py:183
  2.3 18.5 %all-to-all-start = ((bf16[16,8,1280]{2,1,0:T(8,128)(2,1)}), bf16[16,8,1280]{2,1,0:T(8,128)(2,1)S(1)}, u32[]{:S(2)}, u32[]{:S(2)}) async-start(bf16[16,8,1280]{2,1,0:T(8,128)(2,1)} %bitcast.21), calls=%async_computation | async-start | bytes 655360 | tf_op jit(solution)/shard_map/all_to_all | solution.py:208
  20.7 1.7 %shard_map.77 = (bf16[256,1152]{1,0:T(8,128)(2,1)}, f32[8,1152]{1,0:T(8,128)}, f32[8,1]{1,0:T(8,128)}) custom-call(bf16[8,1152]{1,0:T(8,128)(2,1)} %text_ref.1), custom_call_target="tpu_custom_call" | custom-call | bytes 73728 | tf_op jit(solution)/shard_map/pallas_call | solution.py:183
  22.4 9.5 %all-to-all-done = bf16[16,8,1280]{2,1,0:T(8,128)(2,1)S(1)} async-done(((bf16[16,8,1280]{2,1,0:T(8,128)(2,1)}), bf16[16,8,1280]{2,1,0:T(8,128)(2,1)S(1)}, u32[]{:S(2)}, u32[]{:S(2)}) %all-to-all-start) | async-done | bytes 327712 | tf_op jit(solution)/shard_map/all_to_all | solution.py:208
  31.9 11.7 %all-to-all-start.1 = ((bf16[32,8,1152]{2,1,0:T(8,128)(2,1)}), bf16[32,8,1152]{2,1,0:T(8,128)(2,1)S(1)}, u32[]{:S(2)}, u32[]{:S(2)}) async-start(bf16[32,8,1152]{2,1,0:T(8,128)(2,1)} %bitcast.20), calls=%async_computation.1 | async-start | bytes 1179648 | tf_op jit(solution)/shard_map/all_to_all | solution.py:209
  43.6 4.6 %collective-permute-start = (bf16[128,1280]{1,0:T(8,128)(2,1)S(1)}, bf16[128,1280]{1,0:T(8,128)(2,1)S(1)}, u32[]{:S(2)}, u32[]{:S(2)}) collective-permute-start(bf16[128,1280]{1,0:T(8,128)(2,1)S(1)} %bitcast.16), channel_id=1, source_target_pairs={{0,16},{16,0},{1,17},{17,1},{2,18},{18,2},{3,19},{19,3},{4,20},{20... | collective-permute-start | bytes 983048 | tf_op jit(solution)/shard_map/ppermute | solution.py:210
  49.6 0.0 collective-permute-done.refs_1_
  49.6 10.8 %all-to-all-done.1 = bf16[32,8,1152]{2,1,0:T(8,128)(2,1)S(1)} async-done(((bf16[32,8,1152]{2,1,0:T(8,128)(2,1)}), bf16[32,8,1152]{2,1,0:T(8,128)(2,1)S(1)}, u32[]{:S(2)}, u32[]{:S(2)}) %all-to-all-start.1) | async-done | bytes 589856 | tf_op jit(solution)/shard_map/all_to_all | solution.py:209
  60.4 2.2 %shard_map.78 = (bf16[256,1280]{1,0:T(8,128)(2,1)}, bf16[256,256]{1,0:T(8,128)(2,1)S(1)}, f32[256,128]{1,0:T(8,128)S(1)}) custom-call(bf16[128,1280]{1,0:T(8,128)(2,1)S(1)} %bitcast.17, bf16[128,1280]{1,0:T(8,128)(2,1)S(1)} %collective-permute-done.refs_1_, bf16[256,1152]{1,0:T(8,128)(2,1)S(1)} %bitcast.12, f32[1]{0:T(128)S(6)} %copy.8.refs_3_.refs_5_, ...), custom_call_target="tpu_custom_call" | custom-call | flops 301989888 | bytes 4980768 | tf_op jit(solution)/shard_map/pallas_call | solution.py:183
  62.6 7.5 %all-to-all-start.2 = ((bf16[32,8,1280]{2,1,0:T(8,128)(2,1)}), bf16[32,8,1280]{2,1,0:T(8,128)(2,1)S(1)}, u32[]{:S(2)}, u32[]{:S(2)}) async-start(bf16[32,8,1280]{2,1,0:T(8,128)(2,1)} %bitcast.4), calls=%async_computation.2 | async-start | bytes 1310720 | tf_op jit(solution)/shard_map/all_to_all | solution.py:225
  70.1 0.4 shard_map.79
  70.5 4.7 %collective-permute-start.1 = (f32[128,1280]{1,0:T(8,128)S(1)}, f32[128,1280]{1,0:T(8,128)S(1)}, u32[]{:S(2)}, u32[]{:S(2)}) collective-permute-start(f32[128,1280]{1,0:T(8,128)S(1)} %get-tuple-element.19), channel_id=1, source_target_pairs={{0,16},{16,0},{1,17},{17,1},{2,18},{18,2},{3,19},{19,3},{4,20},{20... | collective-permute-start | bytes 1966088 | tf_op jit(solution)/shard_map/ppermute | solution.py:228
  75.2 1.7 %collective-permute-done.1.came_ref = f32[128,1280]{1,0:T(8,128)S(1)} collective-permute-done((f32[128,1280]{1,0:T(8,128)S(1)}, f32[128,1280]{1,0:T(8,128)S(1)}, u32[]{:S(2)}, u32[]{:S(2)}) %collective-permute-start.1) | collective-permute-done | bytes 655392 | tf_op jit(solution)/shard_map/ppermute | solution.py:228
  76.9 11.4 %all-to-all-done.2 = bf16[32,8,1280]{2,1,0:T(8,128)(2,1)S(1)} async-done(((bf16[32,8,1280]{2,1,0:T(8,128)(2,1)}), bf16[32,8,1280]{2,1,0:T(8,128)(2,1)S(1)}, u32[]{:S(2)}, u32[]{:S(2)}) %all-to-all-start.2) | async-done | bytes 655392 | tf_op jit(solution)/shard_map/all_to_all | solution.py:225
  88.3 0.2 shard_map.80
  88.5 16.6 %all_to_all.44 = bf16[16,8,1280]{2,1,0:T(8,128)(2,1)S(1)} all-to-all(bf16[16,8,1280]{2,1,0:T(8,128)(2,1)S(1)} %bitcast.19), channel_id=1, replica_groups=mesh['z'=8,'xl'=4,'core'=2,'xh'=2,'yh'=4,'y0'=2] {'z','y0'}, dimensions={0} | all-to-all | bytes 655360 | tf_op jit(solution)/shard_map/all_to_all | solution.py:230
  105.1 0.0 copy-start.1
  105.1 0.0 copy-start.3
  105.1 0.2 shard_map.83
  105.3 5.6 %collective-permute-start.2 = (f32[8,128]{1,0:T(8,128)S(1)}, f32[8,128]{1,0:T(8,128)S(1)}, u32[]{:S(2)}, u32[]{:S(2)}) collective-permute-start(f32[8,128]{1,0:T(8,128)S(1)} %shard_map.83), channel_id=1, source_target_pairs={{0,16},{16,0},{1,17},{17,1},{2,18},{18,2},{3,19},{19,3},{4,20},{20... | collective-permute-start | bytes 12296 | tf_op jit(solution)/shard_map/ppermute | solution.py:234
  110.9 0.0 copy-done.1
  110.9 0.0 copy-done.3
  111.0 0.0 copy-start
  111.0 0.0 copy-start.2
  111.0 0.8 shard_map.82
  111.8 0.0 copy-done
  111.8 0.0 copy-done.2
  111.8 0.8 shard_map.81
  112.6 0.0 collective-permute-done.2
  112.6 0.5 slice_bitcast_fusion
  (1 shorter events, 0.0 us)
Async XLA Ops:
  2.3 29.7 %all-to-all-start = ((bf16[16,8,1280]{2,1,0:T(8,128)(2,1)}), bf16[16,8,1280]{2,1,0:T(8,128)(2,1)S(1)}, u32[]{:S(2)}, u32[]{:S(2)}) async-start(bf16[16,8,1280]{2,1,0:T(8,128)(2,1)} %bitcast.21), calls=%async_computation | async-start | bytes 655360 | tf_op jit(solution)/shard_map/all_to_all | solution.py:208
  31.9 28.5 %all-to-all-start.1 = ((bf16[32,8,1152]{2,1,0:T(8,128)(2,1)}), bf16[32,8,1152]{2,1,0:T(8,128)(2,1)S(1)}, u32[]{:S(2)}, u32[]{:S(2)}) async-start(bf16[32,8,1152]{2,1,0:T(8,128)(2,1)} %bitcast.20), calls=%async_computation.1 | async-start | bytes 1179648 | tf_op jit(solution)/shard_map/all_to_all | solution.py:209
  43.6 5.9 %collective-permute-start = (bf16[128,1280]{1,0:T(8,128)(2,1)S(1)}, bf16[128,1280]{1,0:T(8,128)(2,1)S(1)}, u32[]{:S(2)}, u32[]{:S(2)}) collective-permute-start(bf16[128,1280]{1,0:T(8,128)(2,1)S(1)} %bitcast.16), channel_id=1, source_target_pairs={{0,16},{16,0},{1,17},{17,1},{2,18},{18,2},{3,19},{19,3},{4,20},{20... | collective-permute-start | bytes 983048 | tf_op jit(solution)/shard_map/ppermute | solution.py:210
  62.6 25.7 %all-to-all-start.2 = ((bf16[32,8,1280]{2,1,0:T(8,128)(2,1)}), bf16[32,8,1280]{2,1,0:T(8,128)(2,1)S(1)}, u32[]{:S(2)}, u32[]{:S(2)}) async-start(bf16[32,8,1280]{2,1,0:T(8,128)(2,1)} %bitcast.4), calls=%async_computation.2 | async-start | bytes 1310720 | tf_op jit(solution)/shard_map/all_to_all | solution.py:225
  70.5 6.4 %collective-permute-start.1 = (f32[128,1280]{1,0:T(8,128)S(1)}, f32[128,1280]{1,0:T(8,128)S(1)}, u32[]{:S(2)}, u32[]{:S(2)}) collective-permute-start(f32[128,1280]{1,0:T(8,128)S(1)} %get-tuple-element.19), channel_id=1, source_target_pairs={{0,16},{16,0},{1,17},{17,1},{2,18},{18,2},{3,19},{19,3},{4,20},{20... | collective-permute-start | bytes 1966088 | tf_op jit(solution)/shard_map/ppermute | solution.py:228
  105.1 5.8 %copy-start.1 = (f32[8,1152]{1,0:T(8,128)S(1)}, f32[8,1152]{1,0:T(8,128)}, u32[]{:S(2)}) copy-start(f32[8,1152]{1,0:T(8,128)} %get-tuple-element.23.unit_ref) | copy-start | bytes 110596
  105.1 5.8 %copy-start.3 = (f32[8,1]{1,0:T(8,128)S(1)}, f32[8,1]{1,0:T(8,128)}, u32[]{:S(2)}) copy-start(f32[8,1]{1,0:T(8,128)} %get-tuple-element.24.norm_ref) | copy-start | bytes 100
  105.3 7.3 %collective-permute-start.2 = (f32[8,128]{1,0:T(8,128)S(1)}, f32[8,128]{1,0:T(8,128)S(1)}, u32[]{:S(2)}, u32[]{:S(2)}) collective-permute-start(f32[8,128]{1,0:T(8,128)S(1)} %shard_map.83), channel_id=1, source_target_pairs={{0,16},{16,0},{1,17},{17,1},{2,18},{18,2},{3,19},{19,3},{4,20},{20... | collective-permute-start | bytes 12296 | tf_op jit(solution)/shard_map/ppermute | solution.py:234
  111.0 0.8 copy-start
  111.0 0.8 copy-start.2

commit v10 on v5

--- a/solution.py
+++ b/solution.py
@@ -11,11 +11,11 @@
 EXTRA = 128
 F32 = jnp.float32
 BF16 = jnp.bfloat16
-IMAGE_ORDER = ("zh", "z0", "xl", "core", "xh", "yh", "y0")
-TEXT_ORDER = ("xh", "yh", "y0", "zh", "z0", "xl", "core")
-TEXT_GROUP = ("xh", "xl", "yh")
-IMAGE_GROUP = ("zh", "y0")
-PAIR = "z0"
+IMAGE_ORDER = ("zh", "z0", "x1", "x0", "core", "xh", "y")
+TEXT_ORDER = ("xh", "y", "zh", "z0", "x1", "x0", "core")
+TEXT_GROUP = ("y", "zh")
+IMAGE_GROUP = ("z0", "xh", "x1")
+PAIR = "x0"
 VMEM = pl.BlockSpec(memory_space=pltpu.VMEM)
 SMEM = pl.BlockSpec(memory_space=pltpu.SMEM)
 
@@ -255,7 +255,7 @@
 
 def solution(mesh):
     img, txt = mesh.shape["img"], mesh.shape["txt"]
-    parts = (img // 16, 2, 4, 2, 2, txt // 4, 2)
+    parts = (img // 16, 2, 2, 2, 2, 2, txt // 2)
     split = Mesh(mesh.devices.reshape(parts), IMAGE_ORDER)
     image_spec, text_spec = P(IMAGE_ORDER, None), P(TEXT_ORDER, None)
     return jax.shard_map(

time: 111 us -> 113 us (1.018)
  waiting for transfers between devices: 21.2 us -> 22.8 us
    all_to_all x1, starting transfers between devices: 11.7 us -> 20.8 us  [per_device(): text = lax.all_to_all(text_send, TEXT_GROUP, 0, 0, tiled=True)]
    all_to_all x1, starting transfers between devices: 17.4 us -> 10 us  [per_device(): piece = lax.all_to_all(image_send, IMAGE_GROUP, 0, 0, tiled=True)]
    ppermute x1, starting transfers between devices: 4.62 us -> 2.66 us  [per_device(): came_pair = lax.ppermute(send, PAIR, swap)]
    all_to_all x1, waiting for transfers between devices: 3.42 us -> 5.31 us  [per_device(): text_back = lax.all_to_all(text_parts, TEXT_GROUP, 0, 0, tiled=True)]
    ppermute x1, starting transfers between devices: 3.9 us -> 2.66 us  [per_device(): piece_pair = lax.ppermute(piece, PAIR, swap)]
where the time goes in v10:
time: 113 us; the launch traced here: 112 us
  starting transfers between devices  64.7 us (57%)
  waiting for transfers between devices  22.8 us (20%)
  blocking collectives  13.4 us (12%)
  Pallas kernels  8.46 us (7%)
  between operations  2.04 us (2%)
    all_to_all x1, starting transfers between devices, per_device(): text = lax.all_to_all(text_send, TEXT_GROUP, 0, 0, tiled=True)  20.8 us
    all_to_all x1, blocking collectives, per_device(): image_back = lax.all_to_all(image_parts, IMAGE_GROUP, 0, 0, tiled=True)  13.4 us
    all_to_all x1, starting transfers between devices, per_device(): piece = lax.all_to_all(image_send, IMAGE_GROUP, 0, 0, tiled=True)  10 us
    all_to_all x1, starting transfers between devices, per_device(): text_back = lax.all_to_all(text_parts, TEXT_GROUP, 0, 0, tiled=True)  8.5 us
    pallas_call x9, Pallas kernels, call(): pl.pallas_call(kernel, out_shape=outs, in_specs=[VMEM] * (len(args) - sca...  8.46 us
    all_to_all x1, starting transfers between devices, per_device(): sums = lax.all_to_all(sums, (PAIR, 'core'), 0, 0, tiled=True)  7.35 us
    all_to_all x1, waiting for transfers between devices, per_device(): piece = lax.all_to_all(image_send, IMAGE_GROUP, 0, 0, tiled=True)  6.22 us
    ppermute x1, starting transfers between devices, per_device(): piece_core = lax.ppermute(piece, 'core', swap)  5.35 us
  transfers between devices with their start and end apart: 9, of which 6 were waited for; matrix products, arithmetic and copies ran while one was open for 0% of the time, Pallas kernels for 3%

profile of v10, /device:TPU:1, one launch (start us, length us, event | category | flops | bytes accessed | tf_op | source)
XLA Modules:
  0.0 111.9 jit_solution(8170119474257643878)
XLA Ops:
  0.6 1.6 %shard_map.76 = (bf16[64,1280]{1,0:T(8,128)(2,1)}, f32[8,1152]{1,0:T(8,128)}, f32[8,1]{1,0:T(8,128)}) custom-call(bf16[8,1152]{1,0:T(8,128)(2,1)} %image_ref.1, s32[8]{0:T(128)} %pair_ref.1), custom_call_target="tpu_custom_call" | custom-call | bytes 73856 | tf_op jit(solution)/shard_map/pallas_call | solution.py:190
  2.2 10.0 %all-to-all-start = ((bf16[8,8,1280]{2,1,0:T(8,128)(2,1)}), bf16[8,8,1280]{2,1,0:T(8,128)(2,1)S(1)}, u32[]{:S(2)}, u32[]{:S(2)}) async-start(bf16[8,8,1280]{2,1,0:T(8,128)(2,1)} %bitcast.20), calls=%async_computation | async-start | bytes 327680 | tf_op jit(solution)/shard_map/all_to_all | solution.py:214
  12.2 1.7 %shard_map.77 = (bf16[256,1152]{1,0:T(8,128)(2,1)}, f32[8,1152]{1,0:T(8,128)}, f32[8,1]{1,0:T(8,128)}) custom-call(bf16[8,1152]{1,0:T(8,128)(2,1)} %text_ref.1), custom_call_target="tpu_custom_call" | custom-call | bytes 73728 | tf_op jit(solution)/shard_map/pallas_call | solution.py:190
  13.9 6.2 %all-to-all-done = bf16[8,8,1280]{2,1,0:T(8,128)(2,1)S(1)} async-done(((bf16[8,8,1280]{2,1,0:T(8,128)(2,1)}), bf16[8,8,1280]{2,1,0:T(8,128)(2,1)S(1)}, u32[]{:S(2)}, u32[]{:S(2)}) %all-to-all-start) | async-done | bytes 163872 | tf_op jit(solution)/shard_map/all_to_all | solution.py:214
  20.1 20.8 %all-to-all-start.1 = ((bf16[32,8,1152]{2,1,0:T(8,128)(2,1)}), bf16[32,8,1152]{2,1,0:T(8,128)(2,1)S(1)}, u32[]{:S(2)}, u32[]{:S(2)}) async-start(bf16[32,8,1152]{2,1,0:T(8,128)(2,1)} %bitcast.19), calls=%async_computation.1 | async-start | bytes 1179648 | tf_op jit(solution)/shard_map/all_to_all | solution.py:215
  40.9 2.7 %collective-permute-start = (bf16[64,1280]{1,0:T(8,128)(2,1)S(1)}, bf16[64,1280]{1,0:T(8,128)(2,1)S(1)}, u32[]{:S(2)}, u32[]{:S(2)}) collective-permute-start(bf16[64,1280]{1,0:T(8,128)(2,1)S(1)} %bitcast.14), channel_id=1, source_target_pairs={{0,32},{32,0},{1,33},{33,1},{2,34},{34,2},{3,35},{35,3},{4,36},{36... | collective-permute-start | bytes 491528 | tf_op jit(solution)/shard_map/ppermute | solution.py:217
  43.6 5.3 %collective-permute-start.1 = (bf16[64,1280]{1,0:T(8,128)(2,1)S(1)}, bf16[64,1280]{1,0:T(8,128)(2,1)S(1)}, u32[]{:S(2)}, u32[]{:S(2)}) collective-permute-start(bf16[64,1280]{1,0:T(8,128)(2,1)S(1)} %bitcast.15), channel_id=1, source_target_pairs={{0,16},{16,0},{1,17},{17,1},{2,18},{18,2},{3,19},{19,3},{4,20},{20... | collective-permute-start | bytes 491528 | tf_op jit(solution)/shard_map/ppermute | solution.py:218
  48.9 0.0 collective-permute-done.b
  48.9 4.0 %collective-permute-start.2 = (bf16[64,1280]{1,0:T(8,128)(2,1)S(1)}, bf16[64,1280]{1,0:T(8,128)(2,1)S(1)}, u32[]{:S(2)}, u32[]{:S(2)}) collective-permute-start(bf16[64,1280]{1,0:T(8,128)(2,1)S(1)} %collective-permute-done.b), channel_id=1, source_target_pairs={{0,16},{16,0},{1,17},{17,1},{2,18},{18,2},{3,19},{19,3},{4,20},{20... | collective-permute-start | bytes 491528 | tf_op jit(solution)/shard_map/ppermute | solution.py:219
  54.2 0.0 collective-permute-done.1.c
  54.2 0.0 collective-permute-done.2.d
  54.2 3.4 %all-to-all-done.1 = bf16[32,8,1152]{2,1,0:T(8,128)(2,1)S(1)} async-done(((bf16[32,8,1152]{2,1,0:T(8,128)(2,1)}), bf16[32,8,1152]{2,1,0:T(8,128)(2,1)S(1)}, u32[]{:S(2)}, u32[]{:S(2)}) %all-to-all-start.1) | async-done | bytes 589856 | tf_op jit(solution)/shard_map/all_to_all | solution.py:215
  57.7 2.2 %shard_map.78 = (bf16[256,1280]{1,0:T(8,128)(2,1)}, bf16[256,256]{1,0:T(8,128)(2,1)S(1)}, f32[256,128]{1,0:T(8,128)S(1)}) custom-call(bf16[64,1280]{1,0:T(8,128)(2,1)S(1)} %bitcast.16, bf16[64,1280]{1,0:T(8,128)(2,1)S(1)} %collective-permute-done.b, bf16[64,1280]{1,0:T(8,128)(2,1)S(1)} %collective-permute-done.1.c, ...), custom_call_target="tpu_custom_call" | custom-call | flops 301989888 | bytes 4980768 | tf_op jit(solution)/shard_map/pallas_call | solution.py:190
  59.8 8.5 %all-to-all-start.2 = ((bf16[32,8,1280]{2,1,0:T(8,128)(2,1)}), bf16[32,8,1280]{2,1,0:T(8,128)(2,1)S(1)}, u32[]{:S(2)}, u32[]{:S(2)}) async-start(bf16[32,8,1280]{2,1,0:T(8,128)(2,1)} %bitcast.4), calls=%async_computation.2 | async-start | bytes 1310720 | tf_op jit(solution)/shard_map/all_to_all | solution.py:234
  68.3 0.4 shard_map.79
  68.7 3.5 %collective-permute-start.3 = (f32[128,1280]{1,0:T(8,128)S(1)}, f32[128,1280]{1,0:T(8,128)S(1)}, u32[]{:S(2)}, u32[]{:S(2)}) collective-permute-start(f32[128,1280]{1,0:T(8,128)S(1)} %get-tuple-element.21), channel_id=1, source_target_pairs={{0,16},{16,0},{1,17},{17,1},{2,18},{18,2},{3,19},{19,3},{4,20},{20... | collective-permute-start | bytes 1966088 | tf_op jit(solution)/shard_map/ppermute | solution.py:237
  72.2 1.7 %collective-permute-done.3.came_ref = f32[128,1280]{1,0:T(8,128)S(1)} collective-permute-done((f32[128,1280]{1,0:T(8,128)S(1)}, f32[128,1280]{1,0:T(8,128)S(1)}, u32[]{:S(2)}, u32[]{:S(2)}) %collective-permute-start.3) | collective-permute-done | bytes 655392 | tf_op jit(solution)/shard_map/ppermute | solution.py:237
  73.9 0.1 shard_map.80
  73.9 2.7 %collective-permute-start.4 = (bf16[64,1280]{1,0:T(8,128)(2,1)S(1)}, bf16[64,1280]{1,0:T(8,128)(2,1)S(1)}, u32[]{:S(2)}, u32[]{:S(2)}) collective-permute-start(bf16[64,1280]{1,0:T(8,128)(2,1)S(1)} %get-tuple-element.23), channel_id=1, source_target_pairs={{0,32},{32,0},{1,33},{33,1},{2,34},{34,2},{3,35},{35,3},{4,36},{36... | collective-permute-start | bytes 491528 | tf_op jit(solution)/shard_map/ppermute | solution.py:241
  76.6 4.6 %collective-permute-done.4.came_ref = bf16[64,1280]{1,0:T(8,128)(2,1)S(1)} collective-permute-done((bf16[64,1280]{1,0:T(8,128)(2,1)S(1)}, bf16[64,1280]{1,0:T(8,128)(2,1)S(1)}, u32[]{:S(2)}, u32[]{:S(2)}) %collective-permute-start.4) | collective-permute-done | bytes 163872 | tf_op jit(solution)/shard_map/ppermute | solution.py:241
  81.2 5.3 %all-to-all-done.2 = bf16[32,8,1280]{2,1,0:T(8,128)(2,1)S(1)} async-done(((bf16[32,8,1280]{2,1,0:T(8,128)(2,1)}), bf16[32,8,1280]{2,1,0:T(8,128)(2,1)S(1)}, u32[]{:S(2)}, u32[]{:S(2)}) %all-to-all-start.2) | async-done | bytes 655392 | tf_op jit(solution)/shard_map/all_to_all | solution.py:234
  86.5 0.2 shard_map.81
  86.8 13.4 %all_to_all.49 = bf16[8,8,1280]{2,1,0:T(8,128)(2,1)S(1)} all-to-all(bf16[8,8,1280]{2,1,0:T(8,128)(2,1)S(1)} %bitcast.18), channel_id=1, replica_groups=mesh['zh'=4,'z0'=2,'x1'=2,'x0'=2,'core'=2,'xh'=2,'y'=8] {'z0','xh','x1'}, dimensions={0} | all-to-all | bytes 327680 | tf_op jit(solution)/shard_map/all_to_all | solution.py:245
  100.1 0.0 copy-start
  100.1 0.8 shard_map.84
  100.9 0.0 copy-start.3
  100.9 7.4 %all-to-all-start.4 = ((f32[4,8,128]{2,1,0:T(8,128)}), f32[4,8,128]{2,1,0:T(8,128)S(1)}, u32[]{:S(2)}, u32[]{:S(2)}) async-start(f32[4,8,128]{2,1,0:T(8,128)} %shard_map.84), calls=%async_computation.4 | async-start | bytes 32768 | tf_op jit(solution)/shard_map/all_to_all | solution.py:250
  108.3 0.0 copy-done
  108.3 0.0 copy-done.3
  108.3 0.0 copy-start.1
  108.3 0.0 copy-start.2
  108.3 0.8 shard_map.83
  109.1 0.0 copy-done.1
  109.1 0.0 copy-done.2
  109.1 0.8 shard_map.82
  109.9 1.5 %all-to-all-done.4 = f32[4,8,128]{2,1,0:T(8,128)S(1)} async-done(((f32[4,8,128]{2,1,0:T(8,128)}), f32[4,8,128]{2,1,0:T(8,128)S(1)}, u32[]{:S(2)}, u32[]{:S(2)}) %all-to-all-start.4) | async-done | bytes 16416 | tf_op jit(solution)/shard_map/all_to_all | solution.py:250
  111.4 0.5 slice_reduce_fusion
Async XLA Ops:
  2.2 17.9 %all-to-all-start = ((bf16[8,8,1280]{2,1,0:T(8,128)(2,1)}), bf16[8,8,1280]{2,1,0:T(8,128)(2,1)S(1)}, u32[]{:S(2)}, u32[]{:S(2)}) async-start(bf16[8,8,1280]{2,1,0:T(8,128)(2,1)} %bitcast.20), calls=%async_computation | async-start | bytes 327680 | tf_op jit(solution)/shard_map/all_to_all | solution.py:214
  20.1 37.5 %all-to-all-start.1 = ((bf16[32,8,1152]{2,1,0:T(8,128)(2,1)}), bf16[32,8,1152]{2,1,0:T(8,128)(2,1)S(1)}, u32[]{:S(2)}, u32[]{:S(2)}) async-start(bf16[32,8,1152]{2,1,0:T(8,128)(2,1)} %bitcast.19), calls=%async_computation.1 | async-start | bytes 1179648 | tf_op jit(solution)/shard_map/all_to_all | solution.py:215
  40.9 8.0 %collective-permute-start = (bf16[64,1280]{1,0:T(8,128)(2,1)S(1)}, bf16[64,1280]{1,0:T(8,128)(2,1)S(1)}, u32[]{:S(2)}, u32[]{:S(2)}) collective-permute-start(bf16[64,1280]{1,0:T(8,128)(2,1)S(1)} %bitcast.14), channel_id=1, source_target_pairs={{0,32},{32,0},{1,33},{33,1},{2,34},{34,2},{3,35},{35,3},{4,36},{36... | collective-permute-start | bytes 491528 | tf_op jit(solution)/shard_map/ppermute | solution.py:217
  43.6 10.7 %collective-permute-start.1 = (bf16[64,1280]{1,0:T(8,128)(2,1)S(1)}, bf16[64,1280]{1,0:T(8,128)(2,1)S(1)}, u32[]{:S(2)}, u32[]{:S(2)}) collective-permute-start(bf16[64,1280]{1,0:T(8,128)(2,1)S(1)} %bitcast.15), channel_id=1, source_target_pairs={{0,16},{16,0},{1,17},{17,1},{2,18},{18,2},{3,19},{19,3},{4,20},{20... | collective-permute-start | bytes 491528 | tf_op jit(solution)/shard_map/ppermute | solution.py:218
  48.9 5.3 %collective-permute-start.2 = (bf16[64,1280]{1,0:T(8,128)(2,1)S(1)}, bf16[64,1280]{1,0:T(8,128)(2,1)S(1)}, u32[]{:S(2)}, u32[]{:S(2)}) collective-permute-start(bf16[64,1280]{1,0:T(8,128)(2,1)S(1)} %collective-permute-done.b), channel_id=1, source_target_pairs={{0,16},{16,0},{1,17},{17,1},{2,18},{18,2},{3,19},{19,3},{4,20},{20... | collective-permute-start | bytes 491528 | tf_op jit(solution)/shard_map/ppermute | solution.py:219
  59.8 26.7 %all-to-all-start.2 = ((bf16[32,8,1280]{2,1,0:T(8,128)(2,1)}), bf16[32,8,1280]{2,1,0:T(8,128)(2,1)S(1)}, u32[]{:S(2)}, u32[]{:S(2)}) async-start(bf16[32,8,1280]{2,1,0:T(8,128)(2,1)} %bitcast.4), calls=%async_computation.2 | async-start | bytes 1310720 | tf_op jit(solution)/shard_map/all_to_all | solution.py:234
  68.7 5.2 %collective-permute-start.3 = (f32[128,1280]{1,0:T(8,128)S(1)}, f32[128,1280]{1,0:T(8,128)S(1)}, u32[]{:S(2)}, u32[]{:S(2)}) collective-permute-start(f32[128,1280]{1,0:T(8,128)S(1)} %get-tuple-element.21), channel_id=1, source_target_pairs={{0,16},{16,0},{1,17},{17,1},{2,18},{18,2},{3,19},{19,3},{4,20},{20... | collective-permute-start | bytes 1966088 | tf_op jit(solution)/shard_map/ppermute | solution.py:237
  73.9 7.3 %collective-permute-start.4 = (bf16[64,1280]{1,0:T(8,128)(2,1)S(1)}, bf16[64,1280]{1,0:T(8,128)(2,1)S(1)}, u32[]{:S(2)}, u32[]{:S(2)}) collective-permute-start(bf16[64,1280]{1,0:T(8,128)(2,1)S(1)} %get-tuple-element.23), channel_id=1, source_target_pairs={{0,32},{32,0},{1,33},{33,1},{2,34},{34,2},{3,35},{35,3},{4,36},{36... | collective-permute-start | bytes 491528 | tf_op jit(solution)/shard_map/ppermute | solution.py:241
  100.1 8.1 %copy-start = (f32[8,1152]{1,0:T(8,128)S(1)}, f32[8,1152]{1,0:T(8,128)}, u32[]{:S(2)}) copy-start(f32[8,1152]{1,0:T(8,128)} %get-tuple-element.27.unit_ref) | copy-start | bytes 110596
  100.9 7.4 %copy-start.3 = (f32[8,1]{1,0:T(8,128)S(1)}, f32[8,1]{1,0:T(8,128)}, u32[]{:S(2)}) copy-start(f32[8,1]{1,0:T(8,128)} %get-tuple-element.28.norm_ref) | copy-start | bytes 100
  100.9 10.5 %all-to-all-start.4 = ((f32[4,8,128]{2,1,0:T(8,128)}), f32[4,8,128]{2,1,0:T(8,128)S(1)}, u32[]{:S(2)}, u32[]{:S(2)}) async-start(f32[4,8,128]{2,1,0:T(8,128)} %shard_map.84), calls=%async_computation.4 | async-start | bytes 32768 | tf_op jit(solution)/shard_map/all_to_all | solution.py:250
  108.3 0.8 copy-start.1
  108.3 0.8 copy-start.2

commit v11 on v5

--- a/solution.py
+++ b/solution.py
@@ -11,11 +11,11 @@
 EXTRA = 128
 F32 = jnp.float32
 BF16 = jnp.bfloat16
-IMAGE_ORDER = ("zh", "z0", "xl", "core", "xh", "yh", "y0")
-TEXT_ORDER = ("xh", "yh", "y0", "zh", "z0", "xl", "core")
+IMAGE_ORDER = ("zh", "zl", "xl", "core", "xh", "yh", "y0")
+TEXT_ORDER = ("xh", "yh", "y0", "zh", "zl", "xl", "core")
 TEXT_GROUP = ("xh", "xl", "yh")
-IMAGE_GROUP = ("zh", "y0")
-PAIR = "z0"
+IMAGE_GROUP = ("zl", "y0")
+PAIR = "zh"
 VMEM = pl.BlockSpec(memory_space=pltpu.VMEM)
 SMEM = pl.BlockSpec(memory_space=pltpu.SMEM)
 
@@ -255,7 +255,7 @@
 
 def solution(mesh):
     img, txt = mesh.shape["img"], mesh.shape["txt"]
-    parts = (img // 16, 2, 4, 2, 2, txt // 4, 2)
+    parts = (2, img // 16, 4, 2, 2, txt // 4, 2)
     split = Mesh(mesh.devices.reshape(parts), IMAGE_ORDER)
     image_spec, text_spec = P(IMAGE_ORDER, None), P(TEXT_ORDER, None)
     return jax.shard_map(

time: 111 us -> 118 us (1.063)
  starting transfers between devices: 65 us -> 75.4 us
  blocking collectives: 13 us -> 8.94 us
    ppermute x1, starting transfers between devices: 3.9 us -> 11.6 us  [per_device(): piece_pair = lax.ppermute(piece, PAIR, swap)]
    all_to_all x1, starting transfers between devices: 17.4 us -> 11.7 us  [per_device(): piece = lax.all_to_all(image_send, IMAGE_GROUP, 0, 0, tiled=True)]
    all_to_all x1, blocking collectives: 13 us -> 8.94 us  [per_device(): image_back = lax.all_to_all(image_parts, IMAGE_GROUP, 0, 0, tiled=True)]
    all_to_all x1, waiting for transfers between devices: 1.5 us -> 5.41 us  [per_device(): sums = lax.all_to_all(sums, (PAIR, 'core'), 0, 0, tiled=True)]
    all_to_all x1, waiting for transfers between devices: 3.91 us -> 0.01 us  [per_device(): text = lax.all_to_all(text_send, TEXT_GROUP, 0, 0, tiled=True)]
    all_to_all x1, starting transfers between devices: 8.01 us -> 11.9 us  [per_device(): text_back = lax.all_to_all(text_parts, TEXT_GROUP, 0, 0, tiled=True)]
    ppermute x1, waiting for transfers between devices: 4.26 us -> 7.6 us  [per_device(): came_pair = lax.ppermute(send, PAIR, swap)]
    all_to_all x1, starting transfers between devices: 7.82 us -> 10.2 us  [per_device(): sums = lax.all_to_all(sums, (PAIR, 'core'), 0, 0, tiled=True)]
  transfers between devices with their start and end apart: 9 -> 9, of which waited for: 6 -> 5; matrix products, arithmetic and copies ran while one was open for 0% -> 0% of each run, Pallas kernels for 3% -> 3%
where the time goes in v11:
time: 118 us; the launch traced here: 117 us
  starting transfers between devices  75.4 us (64%)
  waiting for transfers between devices  21.3 us (18%)
  blocking collectives  8.94 us (8%)
  Pallas kernels  8.46 us (7%)
  between operations  2.05 us (2%)
    all_to_all x1, starting transfers between devices, per_device(): text_back = lax.all_to_all(text_parts, TEXT_GROUP, 0, 0, tiled=True)  11.9 us
    all_to_all x1, starting transfers between devices, per_device(): text = lax.all_to_all(text_send, TEXT_GROUP, 0, 0, tiled=True)  11.9 us
    all_to_all x1, starting transfers between devices, per_device(): piece = lax.all_to_all(image_send, IMAGE_GROUP, 0, 0, tiled=True)  11.7 us
    ppermute x1, starting transfers between devices, per_device(): piece_pair = lax.ppermute(piece, PAIR, swap)  11.6 us
    all_to_all x1, starting transfers between devices, per_device(): sums = lax.all_to_all(sums, (PAIR, 'core'), 0, 0, tiled=True)  10.2 us
    all_to_all x1, blocking collectives, per_device(): image_back = lax.all_to_all(image_parts, IMAGE_GROUP, 0, 0, tiled=True)  8.94 us
    pallas_call x9, Pallas kernels, call(): pl.pallas_call(kernel, out_shape=outs, in_specs=[VMEM] * (len(args) - sca...  8.46 us
    ppermute x1, waiting for transfers between devices, per_device(): came_pair = lax.ppermute(send, PAIR, swap)  7.6 us
  transfers between devices with their start and end apart: 9, of which 5 were waited for; matrix products, arithmetic and copies ran while one was open for 0% of the time, Pallas kernels for 3%

profile of v11, /device:TPU:1, one launch (start us, length us, event | category | flops | bytes accessed | tf_op | source)
XLA Modules:
  0.0 116.7 jit_solution(3379661674963121697)
XLA Ops:
  0.6 1.6 %shard_map.76 = (bf16[64,1280]{1,0:T(8,128)(2,1)}, f32[8,1152]{1,0:T(8,128)}, f32[8,1]{1,0:T(8,128)}) custom-call(bf16[8,1152]{1,0:T(8,128)(2,1)} %image_ref.1, s32[8]{0:T(128)} %pair_ref.1), custom_call_target="tpu_custom_call" | custom-call | bytes 73856 | tf_op jit(solution)/shard_map/pallas_call | solution.py:190
  2.2 11.7 %all-to-all-start = ((bf16[8,8,1280]{2,1,0:T(8,128)(2,1)}), bf16[8,8,1280]{2,1,0:T(8,128)(2,1)S(1)}, u32[]{:S(2)}, u32[]{:S(2)}) async-start(bf16[8,8,1280]{2,1,0:T(8,128)(2,1)} %bitcast.20), calls=%async_computation | async-start | bytes 327680 | tf_op jit(solution)/shard_map/all_to_all | solution.py:214
  13.9 1.7 %shard_map.77 = (bf16[256,1152]{1,0:T(8,128)(2,1)}, f32[8,1152]{1,0:T(8,128)}, f32[8,1]{1,0:T(8,128)}) custom-call(bf16[8,1152]{1,0:T(8,128)(2,1)} %text_ref.1), custom_call_target="tpu_custom_call" | custom-call | bytes 73728 | tf_op jit(solution)/shard_map/pallas_call | solution.py:190
  15.6 4.5 %all-to-all-done = bf16[8,8,1280]{2,1,0:T(8,128)(2,1)S(1)} async-done(((bf16[8,8,1280]{2,1,0:T(8,128)(2,1)}), bf16[8,8,1280]{2,1,0:T(8,128)(2,1)S(1)}, u32[]{:S(2)}, u32[]{:S(2)}) %all-to-all-start) | async-done | bytes 163872 | tf_op jit(solution)/shard_map/all_to_all | solution.py:214
  20.1 11.9 %all-to-all-start.1 = ((bf16[32,8,1152]{2,1,0:T(8,128)(2,1)}), bf16[32,8,1152]{2,1,0:T(8,128)(2,1)S(1)}, u32[]{:S(2)}, u32[]{:S(2)}) async-start(bf16[32,8,1152]{2,1,0:T(8,128)(2,1)} %bitcast.19), calls=%async_computation.1 | async-start | bytes 1179648 | tf_op jit(solution)/shard_map/all_to_all | solution.py:215
  31.9 11.6 %collective-permute-start = (bf16[64,1280]{1,0:T(8,128)(2,1)S(1)}, bf16[64,1280]{1,0:T(8,128)(2,1)S(1)}, u32[]{:S(2)}, u32[]{:S(2)}) collective-permute-start(bf16[64,1280]{1,0:T(8,128)(2,1)S(1)} %bitcast.14), channel_id=1, source_target_pairs={{0,512},{512,0},{1,513},{513,1},{2,514},{514,2},{3,515},{515,3},{4... | collective-permute-start | bytes 491528 | tf_op jit(solution)/shard_map/ppermute | solution.py:217
  43.5 4.5 %collective-permute-start.1 = (bf16[64,1280]{1,0:T(8,128)(2,1)S(1)}, bf16[64,1280]{1,0:T(8,128)(2,1)S(1)}, u32[]{:S(2)}, u32[]{:S(2)}) collective-permute-start(bf16[64,1280]{1,0:T(8,128)(2,1)S(1)} %bitcast.15), channel_id=1, source_target_pairs={{0,16},{16,0},{1,17},{17,1},{2,18},{18,2},{3,19},{19,3},{4,20},{20... | collective-permute-start | bytes 491528 | tf_op jit(solution)/shard_map/ppermute | solution.py:218
  48.0 0.0 collective-permute-done.b
  48.0 5.1 %collective-permute-start.2 = (bf16[64,1280]{1,0:T(8,128)(2,1)S(1)}, bf16[64,1280]{1,0:T(8,128)(2,1)S(1)}, u32[]{:S(2)}, u32[]{:S(2)}) collective-permute-start(bf16[64,1280]{1,0:T(8,128)(2,1)S(1)} %collective-permute-done.b), channel_id=1, source_target_pairs={{0,16},{16,0},{1,17},{17,1},{2,18},{18,2},{3,19},{19,3},{4,20},{20... | collective-permute-start | bytes 491528 | tf_op jit(solution)/shard_map/ppermute | solution.py:219
  54.5 0.0 collective-permute-done.1.c
  54.5 0.0 collective-permute-done.2.d
  54.5 0.0 all-to-all-done.1
  54.5 2.2 %shard_map.78 = (bf16[256,1280]{1,0:T(8,128)(2,1)}, bf16[256,256]{1,0:T(8,128)(2,1)S(1)}, f32[256,128]{1,0:T(8,128)S(1)}) custom-call(bf16[64,1280]{1,0:T(8,128)(2,1)S(1)} %bitcast.16, bf16[64,1280]{1,0:T(8,128)(2,1)S(1)} %collective-permute-done.b, bf16[64,1280]{1,0:T(8,128)(2,1)S(1)} %collective-permute-done.1.c, ...), custom_call_target="tpu_custom_call" | custom-call | flops 301989888 | bytes 4980768 | tf_op jit(solution)/shard_map/pallas_call | solution.py:190
  56.7 11.9 %all-to-all-start.2 = ((bf16[32,8,1280]{2,1,0:T(8,128)(2,1)}), bf16[32,8,1280]{2,1,0:T(8,128)(2,1)S(1)}, u32[]{:S(2)}, u32[]{:S(2)}) async-start(bf16[32,8,1280]{2,1,0:T(8,128)(2,1)} %bitcast.4), calls=%async_computation.2 | async-start | bytes 1310720 | tf_op jit(solution)/shard_map/all_to_all | solution.py:234
  68.6 0.4 shard_map.79
  68.9 2.2 %collective-permute-start.3 = (f32[128,1280]{1,0:T(8,128)S(1)}, f32[128,1280]{1,0:T(8,128)S(1)}, u32[]{:S(2)}, u32[]{:S(2)}) collective-permute-start(f32[128,1280]{1,0:T(8,128)S(1)} %get-tuple-element.21), channel_id=1, source_target_pairs={{0,16},{16,0},{1,17},{17,1},{2,18},{18,2},{3,19},{19,3},{4,20},{20... | collective-permute-start | bytes 1966088 | tf_op jit(solution)/shard_map/ppermute | solution.py:237
  71.2 1.7 %collective-permute-done.3.came_ref = f32[128,1280]{1,0:T(8,128)S(1)} collective-permute-done((f32[128,1280]{1,0:T(8,128)S(1)}, f32[128,1280]{1,0:T(8,128)S(1)}, u32[]{:S(2)}, u32[]{:S(2)}) %collective-permute-start.3) | collective-permute-done | bytes 655392 | tf_op jit(solution)/shard_map/ppermute | solution.py:237
  72.9 0.1 shard_map.80
  73.0 6.3 %collective-permute-start.4 = (bf16[64,1280]{1,0:T(8,128)(2,1)S(1)}, bf16[64,1280]{1,0:T(8,128)(2,1)S(1)}, u32[]{:S(2)}, u32[]{:S(2)}) collective-permute-start(bf16[64,1280]{1,0:T(8,128)(2,1)S(1)} %get-tuple-element.23), channel_id=1, source_target_pairs={{0,512},{512,0},{1,513},{513,1},{2,514},{514,2},{3,515},{515,3},{4... | collective-permute-start | bytes 491528 | tf_op jit(solution)/shard_map/ppermute | solution.py:241
  79.3 7.6 %collective-permute-done.4.came_ref = bf16[64,1280]{1,0:T(8,128)(2,1)S(1)} collective-permute-done((bf16[64,1280]{1,0:T(8,128)(2,1)S(1)}, bf16[64,1280]{1,0:T(8,128)(2,1)S(1)}, u32[]{:S(2)}, u32[]{:S(2)}) %collective-permute-start.4) | collective-permute-done | bytes 163872 | tf_op jit(solution)/shard_map/ppermute | solution.py:241
  86.9 2.0 %all-to-all-done.2 = bf16[32,8,1280]{2,1,0:T(8,128)(2,1)S(1)} async-done(((bf16[32,8,1280]{2,1,0:T(8,128)(2,1)}), bf16[32,8,1280]{2,1,0:T(8,128)(2,1)S(1)}, u32[]{:S(2)}, u32[]{:S(2)}) %all-to-all-start.2) | async-done | bytes 655392 | tf_op jit(solution)/shard_map/all_to_all | solution.py:234
  88.9 0.2 shard_map.81
  89.2 8.9 %all_to_all.49 = bf16[8,8,1280]{2,1,0:T(8,128)(2,1)S(1)} all-to-all(bf16[8,8,1280]{2,1,0:T(8,128)(2,1)S(1)} %bitcast.18), channel_id=1, replica_groups=mesh['zh'=2,'zl'=4,'xl'=4,'core'=2,'xh'=2,'yh'=4,'y0'=2] {'zl','y0'}, dimensions={0} | all-to-all | bytes 327680 | tf_op jit(solution)/shard_map/all_to_all | solution.py:245
  98.1 0.0 copy-start
  98.1 0.8 shard_map.84
  98.9 0.0 copy-start.3
  98.9 10.2 %all-to-all-start.4 = ((f32[4,8,128]{2,1,0:T(8,128)}), f32[4,8,128]{2,1,0:T(8,128)S(1)}, u32[]{:S(2)}, u32[]{:S(2)}) async-start(f32[4,8,128]{2,1,0:T(8,128)} %shard_map.84), calls=%async_computation.4 | async-start | bytes 32768 | tf_op jit(solution)/shard_map/all_to_all | solution.py:250
  109.1 0.0 copy-done
  109.1 0.0 copy-done.3
  109.1 0.0 copy-start.1
  109.1 0.0 copy-start.2
  109.1 0.8 shard_map.83
  110.0 0.0 copy-done.1
  110.0 0.0 copy-done.2
  110.0 0.8 shard_map.82
  110.7 5.4 %all-to-all-done.4 = f32[4,8,128]{2,1,0:T(8,128)S(1)} async-done(((f32[4,8,128]{2,1,0:T(8,128)}), f32[4,8,128]{2,1,0:T(8,128)S(1)}, u32[]{:S(2)}, u32[]{:S(2)}) %all-to-all-start.4) | async-done | bytes 16416 | tf_op jit(solution)/shard_map/all_to_all | solution.py:250
  116.2 0.5 slice_reduce_fusion
Async XLA Ops:
  2.2 17.9 %all-to-all-start = ((bf16[8,8,1280]{2,1,0:T(8,128)(2,1)}), bf16[8,8,1280]{2,1,0:T(8,128)(2,1)S(1)}, u32[]{:S(2)}, u32[]{:S(2)}) async-start(bf16[8,8,1280]{2,1,0:T(8,128)(2,1)} %bitcast.20), calls=%async_computation | async-start | bytes 327680 | tf_op jit(solution)/shard_map/all_to_all | solution.py:214
  20.1 34.4 %all-to-all-start.1 = ((bf16[32,8,1152]{2,1,0:T(8,128)(2,1)}), bf16[32,8,1152]{2,1,0:T(8,128)(2,1)S(1)}, u32[]{:S(2)}, u32[]{:S(2)}) async-start(bf16[32,8,1152]{2,1,0:T(8,128)(2,1)} %bitcast.19), calls=%async_computation.1 | async-start | bytes 1179648 | tf_op jit(solution)/shard_map/all_to_all | solution.py:215
  31.9 16.1 %collective-permute-start = (bf16[64,1280]{1,0:T(8,128)(2,1)S(1)}, bf16[64,1280]{1,0:T(8,128)(2,1)S(1)}, u32[]{:S(2)}, u32[]{:S(2)}) collective-permute-start(bf16[64,1280]{1,0:T(8,128)(2,1)S(1)} %bitcast.14), channel_id=1, source_target_pairs={{0,512},{512,0},{1,513},{513,1},{2,514},{514,2},{3,515},{515,3},{4... | collective-permute-start | bytes 491528 | tf_op jit(solution)/shard_map/ppermute | solution.py:217
  43.5 10.9 %collective-permute-start.1 = (bf16[64,1280]{1,0:T(8,128)(2,1)S(1)}, bf16[64,1280]{1,0:T(8,128)(2,1)S(1)}, u32[]{:S(2)}, u32[]{:S(2)}) collective-permute-start(bf16[64,1280]{1,0:T(8,128)(2,1)S(1)} %bitcast.15), channel_id=1, source_target_pairs={{0,16},{16,0},{1,17},{17,1},{2,18},{18,2},{3,19},{19,3},{4,20},{20... | collective-permute-start | bytes 491528 | tf_op jit(solution)/shard_map/ppermute | solution.py:218
  48.0 6.4 %collective-permute-start.2 = (bf16[64,1280]{1,0:T(8,128)(2,1)S(1)}, bf16[64,1280]{1,0:T(8,128)(2,1)S(1)}, u32[]{:S(2)}, u32[]{:S(2)}) collective-permute-start(bf16[64,1280]{1,0:T(8,128)(2,1)S(1)} %collective-permute-done.b), channel_id=1, source_target_pairs={{0,16},{16,0},{1,17},{17,1},{2,18},{18,2},{3,19},{19,3},{4,20},{20... | collective-permute-start | bytes 491528 | tf_op jit(solution)/shard_map/ppermute | solution.py:219
  56.7 32.3 %all-to-all-start.2 = ((bf16[32,8,1280]{2,1,0:T(8,128)(2,1)}), bf16[32,8,1280]{2,1,0:T(8,128)(2,1)S(1)}, u32[]{:S(2)}, u32[]{:S(2)}) async-start(bf16[32,8,1280]{2,1,0:T(8,128)(2,1)} %bitcast.4), calls=%async_computation.2 | async-start | bytes 1310720 | tf_op jit(solution)/shard_map/all_to_all | solution.py:234
  68.9 4.0 %collective-permute-start.3 = (f32[128,1280]{1,0:T(8,128)S(1)}, f32[128,1280]{1,0:T(8,128)S(1)}, u32[]{:S(2)}, u32[]{:S(2)}) collective-permute-start(f32[128,1280]{1,0:T(8,128)S(1)} %get-tuple-element.21), channel_id=1, source_target_pairs={{0,16},{16,0},{1,17},{17,1},{2,18},{18,2},{3,19},{19,3},{4,20},{20... | collective-permute-start | bytes 1966088 | tf_op jit(solution)/shard_map/ppermute | solution.py:237
  73.0 13.9 %collective-permute-start.4 = (bf16[64,1280]{1,0:T(8,128)(2,1)S(1)}, bf16[64,1280]{1,0:T(8,128)(2,1)S(1)}, u32[]{:S(2)}, u32[]{:S(2)}) collective-permute-start(bf16[64,1280]{1,0:T(8,128)(2,1)S(1)} %get-tuple-element.23), channel_id=1, source_target_pairs={{0,512},{512,0},{1,513},{513,1},{2,514},{514,2},{3,515},{515,3},{4... | collective-permute-start | bytes 491528 | tf_op jit(solution)/shard_map/ppermute | solution.py:241
  98.1 11.0 %copy-start = (f32[8,1152]{1,0:T(8,128)S(1)}, f32[8,1152]{1,0:T(8,128)}, u32[]{:S(2)}) copy-start(f32[8,1152]{1,0:T(8,128)} %get-tuple-element.27.unit_ref) | copy-start | bytes 110596
  98.9 10.2 %copy-start.3 = (f32[8,1]{1,0:T(8,128)S(1)}, f32[8,1]{1,0:T(8,128)}, u32[]{:S(2)}) copy-start(f32[8,1]{1,0:T(8,128)} %get-tuple-element.28.norm_ref) | copy-start | bytes 100
  98.9 17.3 %all-to-all-start.4 = ((f32[4,8,128]{2,1,0:T(8,128)}), f32[4,8,128]{2,1,0:T(8,128)S(1)}, u32[]{:S(2)}, u32[]{:S(2)}) async-start(f32[4,8,128]{2,1,0:T(8,128)} %shard_map.84), calls=%async_computation.4 | async-start | bytes 32768 | tf_op jit(solution)/shard_map/all_to_all | solution.py:250
  109.1 0.8 copy-start.1
  109.1 0.8 copy-start.2

commit v12 on v5

--- a/solution.py
+++ b/solution.py
@@ -87,7 +87,13 @@
     return jnp.exp(jnp.zeros((8, 128), F32) + log_scale_ref[0])[0:1, 0:1]
 
 
-def score_kernel(own_rows, sizes, piece_refs, text_ref, log_scale_ref, bias_ref, text_out, low_out, along_out):
+def score_kernel(own_rows, sizes, piece_refs, text_ref, log_scale_ref, bias_ref, text_out, low_out, along_out, text_made, sems):
+    copies = []
+
+    def send(cols):
+        copies.append(pltpu.make_async_copy(text_made.at[:, cols], text_out.at[:, cols], sems.at[len(copies)]))
+        copies[-1].start()
+
     text = text_ref[...]
     count, width = text.shape
     scale = scale_of(log_scale_ref)
@@ -114,14 +120,18 @@
     along_text = jnp.broadcast_to(jnp.sum(product, axis=0, keepdims=True), (128, count)).T
     along_text = along_text.astype(BF16).astype(F32)
     low_turned = dlogit.T.astype(BF16)
+    lane = lanes(count)
+    stats = split_stats(lane, 1, [jnp.broadcast_to(t, lane.shape) for t in totals])
+    text_made[:, width:] = jnp.where(lane == 0, along_text, stats).astype(BF16)
+    send(slice(width, width + EXTRA))
     block = width // 3
     for first in range(0, width, block):
         cols = slice(first, first + block)
         part = scale * jnp.dot(low_turned, image[:, cols], preferred_element_type=F32)
-        text_out[:, cols] = (part - along_text[:, 0:1] * text[:, cols].astype(F32)).astype(BF16)
-    lane = lanes(count)
-    stats = split_stats(lane, 1, [jnp.broadcast_to(t, lane.shape) for t in totals])
-    text_out[:, width:] = jnp.where(lane == 0, along_text, stats).astype(BF16)
+        text_made[:, cols] = (part - along_text[:, 0:1] * text[:, cols].astype(F32)).astype(BF16)
+        send(cols)
+    for copy in copies:
+        copy.wait()
 
 
 def image_kernel(piece_refs, text_ref, low_ref, along_ref, log_scale_ref, stay_out, away_out):
@@ -185,13 +195,14 @@
     return jax.ShapeDtypeStruct(dims, dtype)
 
 
-def call(kernel, outs, *args, scalars=0, flops=0, limit=40 * 1024 * 1024):
+def call(kernel, outs, *args, scalars=0, flops=0, limit=40 * 1024 * 1024, out_specs=None, scratch=()):
     size = sum(a.size * a.dtype.itemsize for a in args)
     return pl.pallas_call(
         kernel,
         out_shape=outs,
         in_specs=[VMEM] * (len(args) - scalars) + [SMEM] * scalars,
-        out_specs=jax.tree.map(lambda _: VMEM, outs),
+        out_specs=out_specs or jax.tree.map(lambda _: VMEM, outs),
+        scratch_shapes=list(scratch),
         cost_estimate=pl.CostEstimate(flops=flops, bytes_accessed=4 * size, transcendentals=0),
         compiler_params=pltpu.CompilerParams(vmem_limit_bytes=limit),
     )(*args)
@@ -230,6 +241,8 @@
         score,
         (shape(text_count, wide), shape(4 * row_count, text_count), shape(4 * row_count, EXTRA, dtype=F32)),
         *pieces, text, log_scale, bias, scalars=2, flops=2 * work,
+        out_specs=(pl.BlockSpec(memory_space=pl.ANY), VMEM, VMEM),
+        scratch=[pltpu.VMEM((text_count, wide), BF16), pltpu.SemaphoreType.DMA((4,))],
     )
     text_back = lax.all_to_all(text_parts, TEXT_GROUP, 0, 0, tiled=True)
     half = shape(2 * row_count, wide, dtype=F32)

time: 111 us -> 111 us (level)
  no operation moved by 1% of the time
where the time goes in v12:
time: 111 us; the launch traced here: 110 us
  starting transfers between devices  65 us (59%)
  waiting for transfers between devices  21.2 us (19%)
  blocking collectives  13 us (12%)
  Pallas kernels  8.37 us (8%)
  between operations  2.05 us (2%)
    all_to_all x1, starting transfers between devices, per_device(): piece = lax.all_to_all(image_send, IMAGE_GROUP, 0, 0, tiled=True)  17.4 us
    all_to_all x1, blocking collectives, per_device(): image_back = lax.all_to_all(image_parts, IMAGE_GROUP, 0, 0, tiled=True)  13 us
    all_to_all x1, starting transfers between devices, per_device(): text = lax.all_to_all(text_send, TEXT_GROUP, 0, 0, tiled=True)  11.7 us
    pallas_call x9, Pallas kernels, call(): pl.pallas_call(kernel, out_shape=outs, in_specs=[VMEM] * (len(args) - sca...  8.37 us
    all_to_all x1, starting transfers between devices, per_device(): text_back = lax.all_to_all(text_parts, TEXT_GROUP, 0, 0, tiled=True)  8.02 us
    all_to_all x1, starting transfers between devices, per_device(): sums = lax.all_to_all(sums, (PAIR, 'core'), 0, 0, tiled=True)  7.82 us
    all_to_all x1, waiting for transfers between devices, per_device(): piece = lax.all_to_all(image_send, IMAGE_GROUP, 0, 0, tiled=True)  6.45 us
    ppermute x1, starting transfers between devices, per_device(): came_pair = lax.ppermute(send, PAIR, swap)  4.62 us
  transfers between devices with their start and end apart: 9, of which 6 were waited for; matrix products, arithmetic and copies ran while one was open for 0% of the time, Pallas kernels for 3%

profile of v12, /device:TPU:1, one launch (start us, length us, event | category | flops | bytes accessed | tf_op | source)
XLA Modules:
  0.0 110.2 jit_solution(3071048624757482256)
XLA Ops:
  0.6 1.6 %shard_map.76 = (bf16[64,1280]{1,0:T(8,128)(2,1)}, f32[8,1152]{1,0:T(8,128)}, f32[8,1]{1,0:T(8,128)}) custom-call(bf16[8,1152]{1,0:T(8,128)(2,1)} %image_ref.1, s32[8]{0:T(128)} %pair_ref.1), custom_call_target="tpu_custom_call" | custom-call | bytes 73856 | tf_op jit(solution)/shard_map/pallas_call | solution.py:200
  2.2 17.4 %all-to-all-start = ((bf16[8,8,1280]{2,1,0:T(8,128)(2,1)}), bf16[8,8,1280]{2,1,0:T(8,128)(2,1)S(1)}, u32[]{:S(2)}, u32[]{:S(2)}) async-start(bf16[8,8,1280]{2,1,0:T(8,128)(2,1)} %bitcast.20), calls=%async_computation | async-start | bytes 327680 | tf_op jit(solution)/shard_map/all_to_all | solution.py:225
  19.6 1.7 %shard_map.77 = (bf16[256,1152]{1,0:T(8,128)(2,1)}, f32[8,1152]{1,0:T(8,128)}, f32[8,1]{1,0:T(8,128)}) custom-call(bf16[8,1152]{1,0:T(8,128)(2,1)} %text_ref.1), custom_call_target="tpu_custom_call" | custom-call | bytes 73728 | tf_op jit(solution)/shard_map/pallas_call | solution.py:200
  21.3 6.4 %all-to-all-done = bf16[8,8,1280]{2,1,0:T(8,128)(2,1)S(1)} async-done(((bf16[8,8,1280]{2,1,0:T(8,128)(2,1)}), bf16[8,8,1280]{2,1,0:T(8,128)(2,1)S(1)}, u32[]{:S(2)}, u32[]{:S(2)}) %all-to-all-start) | async-done | bytes 163872 | tf_op jit(solution)/shard_map/all_to_all | solution.py:225
  27.8 11.7 %all-to-all-start.1 = ((bf16[32,8,1152]{2,1,0:T(8,128)(2,1)}), bf16[32,8,1152]{2,1,0:T(8,128)(2,1)S(1)}, u32[]{:S(2)}, u32[]{:S(2)}) async-start(bf16[32,8,1152]{2,1,0:T(8,128)(2,1)} %bitcast.19), calls=%async_computation.1 | async-start | bytes 1179648 | tf_op jit(solution)/shard_map/all_to_all | solution.py:226
  39.5 3.9 %collective-permute-start = (bf16[64,1280]{1,0:T(8,128)(2,1)S(1)}, bf16[64,1280]{1,0:T(8,128)(2,1)S(1)}, u32[]{:S(2)}, u32[]{:S(2)}) collective-permute-start(bf16[64,1280]{1,0:T(8,128)(2,1)S(1)} %bitcast.14), channel_id=1, source_target_pairs={{0,128},{128,0},{1,129},{129,1},{2,130},{130,2},{3,131},{131,3},{4... | collective-permute-start | bytes 491528 | tf_op jit(solution)/shard_map/ppermute | solution.py:228
  43.4 4.5 %collective-permute-start.1 = (bf16[64,1280]{1,0:T(8,128)(2,1)S(1)}, bf16[64,1280]{1,0:T(8,128)(2,1)S(1)}, u32[]{:S(2)}, u32[]{:S(2)}) collective-permute-start(bf16[64,1280]{1,0:T(8,128)(2,1)S(1)} %bitcast.15), channel_id=1, source_target_pairs={{0,16},{16,0},{1,17},{17,1},{2,18},{18,2},{3,19},{19,3},{4,20},{20... | collective-permute-start | bytes 491528 | tf_op jit(solution)/shard_map/ppermute | solution.py:229
  48.0 0.0 collective-permute-done.b
  48.0 3.3 %collective-permute-start.2 = (bf16[64,1280]{1,0:T(8,128)(2,1)S(1)}, bf16[64,1280]{1,0:T(8,128)(2,1)S(1)}, u32[]{:S(2)}, u32[]{:S(2)}) collective-permute-start(bf16[64,1280]{1,0:T(8,128)(2,1)S(1)} %collective-permute-done.b), channel_id=1, source_target_pairs={{0,16},{16,0},{1,17},{17,1},{2,18},{18,2},{3,19},{19,3},{4,20},{20... | collective-permute-start | bytes 491528 | tf_op jit(solution)/shard_map/ppermute | solution.py:230
  52.5 0.0 collective-permute-done.1.c
  52.5 0.0 collective-permute-done.2.d
  52.5 3.9 %all-to-all-done.1 = bf16[32,8,1152]{2,1,0:T(8,128)(2,1)S(1)} async-done(((bf16[32,8,1152]{2,1,0:T(8,128)(2,1)}), bf16[32,8,1152]{2,1,0:T(8,128)(2,1)S(1)}, u32[]{:S(2)}, u32[]{:S(2)}) %all-to-all-start.1) | async-done | bytes 589856 | tf_op jit(solution)/shard_map/all_to_all | solution.py:226
  56.4 2.1 %shard_map.78 = (bf16[256,1280]{1,0:T(8,128)(2,1)}, bf16[256,256]{1,0:T(8,128)(2,1)S(1)}, f32[256,128]{1,0:T(8,128)S(1)}) custom-call(bf16[64,1280]{1,0:T(8,128)(2,1)S(1)} %bitcast.16, bf16[64,1280]{1,0:T(8,128)(2,1)S(1)} %collective-permute-done.b, bf16[64,1280]{1,0:T(8,128)(2,1)S(1)} %collective-permute-done.1.c, ...), custom_call_target="tpu_custom_call" | custom-call | flops 301989888 | bytes 4980768 | tf_op jit(solution)/shard_map/pallas_call | solution.py:200
  58.5 8.0 %all-to-all-start.2 = ((bf16[32,8,1280]{2,1,0:T(8,128)(2,1)}), bf16[32,8,1280]{2,1,0:T(8,128)(2,1)S(1)}, u32[]{:S(2)}, u32[]{:S(2)}) async-start(bf16[32,8,1280]{2,1,0:T(8,128)(2,1)} %bitcast.4), calls=%async_computation.2 | async-start | bytes 1310720 | tf_op jit(solution)/shard_map/all_to_all | solution.py:247
  66.6 0.4 shard_map.79
  66.9 3.7 %collective-permute-start.3 = (f32[128,1280]{1,0:T(8,128)S(1)}, f32[128,1280]{1,0:T(8,128)S(1)}, u32[]{:S(2)}, u32[]{:S(2)}) collective-permute-start(f32[128,1280]{1,0:T(8,128)S(1)} %get-tuple-element.21), channel_id=1, source_target_pairs={{0,16},{16,0},{1,17},{17,1},{2,18},{18,2},{3,19},{19,3},{4,20},{20... | collective-permute-start | bytes 1966088 | tf_op jit(solution)/shard_map/ppermute | solution.py:250
  70.6 1.7 %collective-permute-done.3.came_ref = f32[128,1280]{1,0:T(8,128)S(1)} collective-permute-done((f32[128,1280]{1,0:T(8,128)S(1)}, f32[128,1280]{1,0:T(8,128)S(1)}, u32[]{:S(2)}, u32[]{:S(2)}) %collective-permute-start.3) | collective-permute-done | bytes 655392 | tf_op jit(solution)/shard_map/ppermute | solution.py:250
  72.3 0.1 shard_map.80
  72.4 4.6 %collective-permute-start.4 = (bf16[64,1280]{1,0:T(8,128)(2,1)S(1)}, bf16[64,1280]{1,0:T(8,128)(2,1)S(1)}, u32[]{:S(2)}, u32[]{:S(2)}) collective-permute-start(bf16[64,1280]{1,0:T(8,128)(2,1)S(1)} %get-tuple-element.23), channel_id=1, source_target_pairs={{0,128},{128,0},{1,129},{129,1},{2,130},{130,2},{3,131},{131,3},{4... | collective-permute-start | bytes 491528 | tf_op jit(solution)/shard_map/ppermute | solution.py:254
  77.0 4.3 %collective-permute-done.4.came_ref = bf16[64,1280]{1,0:T(8,128)(2,1)S(1)} collective-permute-done((bf16[64,1280]{1,0:T(8,128)(2,1)S(1)}, bf16[64,1280]{1,0:T(8,128)(2,1)S(1)}, u32[]{:S(2)}, u32[]{:S(2)}) %collective-permute-start.4) | collective-permute-done | bytes 163872 | tf_op jit(solution)/shard_map/ppermute | solution.py:254
  81.3 3.4 %all-to-all-done.2 = bf16[32,8,1280]{2,1,0:T(8,128)(2,1)S(1)} async-done(((bf16[32,8,1280]{2,1,0:T(8,128)(2,1)}), bf16[32,8,1280]{2,1,0:T(8,128)(2,1)S(1)}, u32[]{:S(2)}, u32[]{:S(2)}) %all-to-all-start.2) | async-done | bytes 655392 | tf_op jit(solution)/shard_map/all_to_all | solution.py:247
  84.7 0.2 shard_map.81
  84.9 13.0 %all_to_all.49 = bf16[8,8,1280]{2,1,0:T(8,128)(2,1)S(1)} all-to-all(bf16[8,8,1280]{2,1,0:T(8,128)(2,1)S(1)} %bitcast.18), channel_id=1, replica_groups=mesh['zh'=4,'z0'=2,'xl'=4,'core'=2,'xh'=2,'yh'=4,'y0'=2] {'zh','y0'}, dimensions={0} | all-to-all | bytes 327680 | tf_op jit(solution)/shard_map/all_to_all | solution.py:258
  97.9 0.0 copy-start
  97.9 0.8 shard_map.84
  98.7 0.0 copy-start.3
  98.7 7.8 %all-to-all-start.4 = ((f32[4,8,128]{2,1,0:T(8,128)}), f32[4,8,128]{2,1,0:T(8,128)S(1)}, u32[]{:S(2)}, u32[]{:S(2)}) async-start(f32[4,8,128]{2,1,0:T(8,128)} %shard_map.84), calls=%async_computation.4 | async-start | bytes 32768 | tf_op jit(solution)/shard_map/all_to_all | solution.py:263
  106.5 0.0 copy-done
  106.5 0.0 copy-done.3
  106.5 0.0 copy-start.1
  106.5 0.0 copy-start.2
  106.5 0.8 shard_map.83
  107.3 0.0 copy-done.1
  107.4 0.0 copy-done.2
  107.4 0.8 shard_map.82
  108.1 1.5 %all-to-all-done.4 = f32[4,8,128]{2,1,0:T(8,128)S(1)} async-done(((f32[4,8,128]{2,1,0:T(8,128)}), f32[4,8,128]{2,1,0:T(8,128)S(1)}, u32[]{:S(2)}, u32[]{:S(2)}) %all-to-all-start.4) | async-done | bytes 16416 | tf_op jit(solution)/shard_map/all_to_all | solution.py:263
  109.6 0.5 slice_reduce_fusion
Async XLA Ops:
  2.2 25.6 %all-to-all-start = ((bf16[8,8,1280]{2,1,0:T(8,128)(2,1)}), bf16[8,8,1280]{2,1,0:T(8,128)(2,1)S(1)}, u32[]{:S(2)}, u32[]{:S(2)}) async-start(bf16[8,8,1280]{2,1,0:T(8,128)(2,1)} %bitcast.20), calls=%async_computation | async-start | bytes 327680 | tf_op jit(solution)/shard_map/all_to_all | solution.py:225
  27.8 28.7 %all-to-all-start.1 = ((bf16[32,8,1152]{2,1,0:T(8,128)(2,1)}), bf16[32,8,1152]{2,1,0:T(8,128)(2,1)S(1)}, u32[]{:S(2)}, u32[]{:S(2)}) async-start(bf16[32,8,1152]{2,1,0:T(8,128)(2,1)} %bitcast.19), calls=%async_computation.1 | async-start | bytes 1179648 | tf_op jit(solution)/shard_map/all_to_all | solution.py:226
  39.5 8.5 %collective-permute-start = (bf16[64,1280]{1,0:T(8,128)(2,1)S(1)}, bf16[64,1280]{1,0:T(8,128)(2,1)S(1)}, u32[]{:S(2)}, u32[]{:S(2)}) collective-permute-start(bf16[64,1280]{1,0:T(8,128)(2,1)S(1)} %bitcast.14), channel_id=1, source_target_pairs={{0,128},{128,0},{1,129},{129,1},{2,130},{130,2},{3,131},{131,3},{4... | collective-permute-start | bytes 491528 | tf_op jit(solution)/shard_map/ppermute | solution.py:228
  43.4 9.1 %collective-permute-start.1 = (bf16[64,1280]{1,0:T(8,128)(2,1)S(1)}, bf16[64,1280]{1,0:T(8,128)(2,1)S(1)}, u32[]{:S(2)}, u32[]{:S(2)}) collective-permute-start(bf16[64,1280]{1,0:T(8,128)(2,1)S(1)} %bitcast.15), channel_id=1, source_target_pairs={{0,16},{16,0},{1,17},{17,1},{2,18},{18,2},{3,19},{19,3},{4,20},{20... | collective-permute-start | bytes 491528 | tf_op jit(solution)/shard_map/ppermute | solution.py:229
  48.0 4.6 %collective-permute-start.2 = (bf16[64,1280]{1,0:T(8,128)(2,1)S(1)}, bf16[64,1280]{1,0:T(8,128)(2,1)S(1)}, u32[]{:S(2)}, u32[]{:S(2)}) collective-permute-start(bf16[64,1280]{1,0:T(8,128)(2,1)S(1)} %collective-permute-done.b), channel_id=1, source_target_pairs={{0,16},{16,0},{1,17},{17,1},{2,18},{18,2},{3,19},{19,3},{4,20},{20... | collective-permute-start | bytes 491528 | tf_op jit(solution)/shard_map/ppermute | solution.py:230
  58.5 26.2 %all-to-all-start.2 = ((bf16[32,8,1280]{2,1,0:T(8,128)(2,1)}), bf16[32,8,1280]{2,1,0:T(8,128)(2,1)S(1)}, u32[]{:S(2)}, u32[]{:S(2)}) async-start(bf16[32,8,1280]{2,1,0:T(8,128)(2,1)} %bitcast.4), calls=%async_computation.2 | async-start | bytes 1310720 | tf_op jit(solution)/shard_map/all_to_all | solution.py:247
  66.9 5.4 %collective-permute-start.3 = (f32[128,1280]{1,0:T(8,128)S(1)}, f32[128,1280]{1,0:T(8,128)S(1)}, u32[]{:S(2)}, u32[]{:S(2)}) collective-permute-start(f32[128,1280]{1,0:T(8,128)S(1)} %get-tuple-element.21), channel_id=1, source_target_pairs={{0,16},{16,0},{1,17},{17,1},{2,18},{18,2},{3,19},{19,3},{4,20},{20... | collective-permute-start | bytes 1966088 | tf_op jit(solution)/shard_map/ppermute | solution.py:250
  72.4 8.9 %collective-permute-start.4 = (bf16[64,1280]{1,0:T(8,128)(2,1)S(1)}, bf16[64,1280]{1,0:T(8,128)(2,1)S(1)}, u32[]{:S(2)}, u32[]{:S(2)}) collective-permute-start(bf16[64,1280]{1,0:T(8,128)(2,1)S(1)} %get-tuple-element.23), channel_id=1, source_target_pairs={{0,128},{128,0},{1,129},{129,1},{2,130},{130,2},{3,131},{131,3},{4... | collective-permute-start | bytes 491528 | tf_op jit(solution)/shard_map/ppermute | solution.py:254
  97.9 8.6 %copy-start = (f32[8,1152]{1,0:T(8,128)S(1)}, f32[8,1152]{1,0:T(8,128)}, u32[]{:S(2)}) copy-start(f32[8,1152]{1,0:T(8,128)} %get-tuple-element.27.unit_ref) | copy-start | bytes 110596
  98.7 7.8 %copy-start.3 = (f32[8,1]{1,0:T(8,128)S(1)}, f32[8,1]{1,0:T(8,128)}, u32[]{:S(2)}) copy-start(f32[8,1]{1,0:T(8,128)} %get-tuple-element.28.norm_ref) | copy-start | bytes 100
  98.7 10.9 %all-to-all-start.4 = ((f32[4,8,128]{2,1,0:T(8,128)}), f32[4,8,128]{2,1,0:T(8,128)S(1)}, u32[]{:S(2)}, u32[]{:S(2)}) async-start(f32[4,8,128]{2,1,0:T(8,128)} %shard_map.84), calls=%async_computation.4 | async-start | bytes 32768 | tf_op jit(solution)/shard_map/all_to_all | solution.py:263
  106.5 0.8 copy-start.1
  106.5 0.8 copy-start.2

commit v13 on v4

--- a/solution.py
+++ b/solution.py
@@ -13,9 +13,9 @@
 BF16 = jnp.bfloat16
 IMAGE_ORDER = ("zh", "z0", "xl", "core", "xh", "yh", "y0")
 TEXT_ORDER = ("xh", "yh", "y0", "zh", "z0", "xl", "core")
-TEXT_GROUP = ("xh", "xl", "yh")
-IMAGE_GROUP = ("zh", "y0")
-PAIR = "z0"
+TEXT_GROUP = ("xh", "xl", "zh")
+IMAGE_GROUP = ("z0", "yh")
+PAIR = "y0"
 VMEM = pl.BlockSpec(memory_space=pltpu.VMEM)
 SMEM = pl.BlockSpec(memory_space=pltpu.SMEM)
 

time: 112 us -> 113 us (level)
  starting transfers between devices: 47.5 us -> 54.2 us
  blocking collectives: 38.6 us -> 32.4 us
    all_to_all x1, starting transfers between devices: 11.7 us -> 19.9 us  [per_device(): text = lax.all_to_all(text_send, TEXT_GROUP, 0, 0, tiled=True)]
    all_to_all x1, blocking collectives: 25.6 us -> 18.7 us  [per_device(): piece = lax.all_to_all(image_send, IMAGE_GROUP, 0, 0, tiled=True)]
    ppermute x1, starting transfers between devices: 4.62 us -> 2.07 us  [per_device(): came_pair = lax.ppermute(send, PAIR, swap)]
  transfers between devices with their start and end apart: 8 -> 8, of which waited for: 5 -> 5; matrix products, arithmetic and copies ran while one was open for 0% -> 0% of each run, Pallas kernels for 2% -> 1%
where the time goes in v13:
time: 113 us; the launch traced here: 112 us
  starting transfers between devices  54.2 us (48%)
  blocking collectives  32.4 us (29%)
  waiting for transfers between devices  16.3 us (14%)
  Pallas kernels  6.77 us (6%)
  between operations  2.04 us (2%)
    all_to_all x1, starting transfers between devices, per_device(): text = lax.all_to_all(text_send, TEXT_GROUP, 0, 0, tiled=True)  19.9 us
    all_to_all x1, blocking collectives, per_device(): piece = lax.all_to_all(image_send, IMAGE_GROUP, 0, 0, tiled=True)  18.7 us
    all_to_all x1, blocking collectives, per_device(): image_back = lax.all_to_all(image_parts, IMAGE_GROUP, 0, 0, tiled=True)  13.7 us
    ppermute x1, waiting for transfers between devices, per_device(): came_pair = lax.ppermute(send, PAIR, swap)  8.74 us
    all_to_all x1, starting transfers between devices, per_device(): text_back = lax.all_to_all(text_parts, TEXT_GROUP, 0, 0, tiled=True)  8.67 us
    all_to_all x1, starting transfers between devices, per_device(): sums = lax.all_to_all(sums, (PAIR, 'core'), 0, 0, tiled=True)  7.26 us
    pallas_call x7, Pallas kernels, call(): pl.pallas_call(kernel, out_shape=outs, in_specs=[VMEM] * (len(args) - sca...  6.77 us
    ppermute x1, starting transfers between devices, per_device(): piece_core = lax.ppermute(piece, 'core', swap)  5.46 us
  transfers between devices with their start and end apart: 8, of which 5 were waited for; matrix products, arithmetic and copies ran while one was open for 0% of the time, Pallas kernels for 1%

profile of v13, /device:TPU:1, one launch (start us, length us, event | category | flops | bytes accessed | tf_op | source)
XLA Modules:
  0.0 112.3 jit_solution(12535765212829297020)
XLA Ops:
  0.6 1.8 %shard_map.76 = (bf16[64,1280]{1,0:T(8,128)(2,1)}, bf16[256,1152]{1,0:T(8,128)(2,1)}, f32[8,1152]{1,0:T(8,128)}, f32[8,1]{1,0:T(8,128)}, f32[8,1152]{1,0:T(8,128)}, /*index=5*/f32[8,1]{1,0:T(8,128)}) custom-call(bf16[8,1152]{1,0:T(8,128)(2,1)} %image_ref.1, bf16[8,1152]{1,0:T(8,128)(2,1)} %text_ref.1, s32[8]{0:T(128)} %pair_ref.1), custom_call_target="tpu_custom_call" | custom-call | bytes 147584 | tf_op jit(solution)/shard_map/pallas_call | solution.py:167
  2.5 18.7 %all_to_all.49 = bf16[8,8,1280]{2,1,0:T(8,128)(2,1)S(1)} all-to-all(bf16[8,8,1280]{2,1,0:T(8,128)(2,1)} %bitcast.18), channel_id=1, replica_groups=mesh['zh'=4,'z0'=2,'xl'=4,'core'=2,'xh'=2,'yh'=4,'y0'=2] {'z0','yh'}, dimensions={0} | all-to-all | bytes 327680 | tf_op jit(solution)/shard_map/all_to_all | solution.py:190
  21.2 19.9 %all-to-all-start.1 = ((bf16[32,8,1152]{2,1,0:T(8,128)(2,1)}), bf16[32,8,1152]{2,1,0:T(8,128)(2,1)S(1)}, u32[]{:S(2)}, u32[]{:S(2)}) async-start(bf16[32,8,1152]{2,1,0:T(8,128)(2,1)} %bitcast.17), calls=%async_computation.1 | async-start | bytes 1179648 | tf_op jit(solution)/shard_map/all_to_all | solution.py:191
  41.1 2.9 %collective-permute-start = (bf16[64,1280]{1,0:T(8,128)(2,1)S(1)}, bf16[64,1280]{1,0:T(8,128)(2,1)S(1)}, u32[]{:S(2)}, u32[]{:S(2)}) collective-permute-start(bf16[64,1280]{1,0:T(8,128)(2,1)S(1)} %bitcast.14), channel_id=1, source_target_pairs={{0,1},{1,0},{2,3},{3,2},{4,5},{5,4},{6,7},{7,6},{8,9},{9,8},{10,11... | collective-permute-start | bytes 491528 | tf_op jit(solution)/shard_map/ppermute | solution.py:192
  44.0 5.5 %collective-permute-start.1 = (bf16[64,1280]{1,0:T(8,128)(2,1)S(1)}, bf16[64,1280]{1,0:T(8,128)(2,1)S(1)}, u32[]{:S(2)}, u32[]{:S(2)}) collective-permute-start(bf16[64,1280]{1,0:T(8,128)(2,1)S(1)} %bitcast.15), channel_id=1, source_target_pairs={{0,16},{16,0},{1,17},{17,1},{2,18},{18,2},{3,19},{19,3},{4,20},{20... | collective-permute-start | bytes 491528 | tf_op jit(solution)/shard_map/ppermute | solution.py:193
  49.5 0.0 collective-permute-done.b
  49.5 3.7 %collective-permute-start.2 = (bf16[64,1280]{1,0:T(8,128)(2,1)S(1)}, bf16[64,1280]{1,0:T(8,128)(2,1)S(1)}, u32[]{:S(2)}, u32[]{:S(2)}) collective-permute-start(bf16[64,1280]{1,0:T(8,128)(2,1)S(1)} %collective-permute-done.b), channel_id=1, source_target_pairs={{0,16},{16,0},{1,17},{17,1},{2,18},{18,2},{3,19},{19,3},{4,20},{20... | collective-permute-start | bytes 491528 | tf_op jit(solution)/shard_map/ppermute | solution.py:194
  54.5 0.0 collective-permute-done.1.c
  54.5 0.0 collective-permute-done.2.d
  54.5 3.2 %all-to-all-done.1 = bf16[32,8,1152]{2,1,0:T(8,128)(2,1)S(1)} async-done(((bf16[32,8,1152]{2,1,0:T(8,128)(2,1)}), bf16[32,8,1152]{2,1,0:T(8,128)(2,1)S(1)}, u32[]{:S(2)}, u32[]{:S(2)}) %all-to-all-start.1) | async-done | bytes 589856 | tf_op jit(solution)/shard_map/all_to_all | solution.py:191
  57.7 2.3 %shard_map.77 = (bf16[256,1280]{1,0:T(8,128)(2,1)}, f32[128,1280]{1,0:T(8,128)S(1)}, f32[128,1280]{1,0:T(8,128)S(1)}) custom-call(bf16[64,1280]{1,0:T(8,128)(2,1)S(1)} %bitcast.16, bf16[64,1280]{1,0:T(8,128)(2,1)S(1)} %collective-permute-done.b, bf16[64,1280]{1,0:T(8,128)(2,1)S(1)} %collective-permute-done.1.c, ...), custom_call_target="tpu_custom_call" | custom-call | flops 452984832 | bytes 4980768 | tf_op jit(solution)/shard_map/pallas_call | solution.py:167
  60.0 8.7 %all-to-all-start.2 = ((bf16[32,8,1280]{2,1,0:T(8,128)(2,1)}), bf16[32,8,1280]{2,1,0:T(8,128)(2,1)S(1)}, u32[]{:S(2)}, u32[]{:S(2)}) async-start(bf16[32,8,1280]{2,1,0:T(8,128)(2,1)} %bitcast.4), calls=%async_computation.2 | async-start | bytes 1310720 | tf_op jit(solution)/shard_map/all_to_all | solution.py:205
  68.7 4.2 %collective-permute-start.3 = (f32[128,1280]{1,0:T(8,128)S(1)}, f32[128,1280]{1,0:T(8,128)S(1)}, u32[]{:S(2)}, u32[]{:S(2)}) collective-permute-start(f32[128,1280]{1,0:T(8,128)S(1)} %get-tuple-element.17), channel_id=1, source_target_pairs={{0,16},{16,0},{1,17},{17,1},{2,18},{18,2},{3,19},{19,3},{4,20},{20... | collective-permute-start | bytes 1966088 | tf_op jit(solution)/shard_map/ppermute | solution.py:206
  72.9 1.7 %collective-permute-done.3.came_ref = f32[128,1280]{1,0:T(8,128)S(1)} collective-permute-done((f32[128,1280]{1,0:T(8,128)S(1)}, f32[128,1280]{1,0:T(8,128)S(1)}, u32[]{:S(2)}, u32[]{:S(2)}) %collective-permute-start.3) | collective-permute-done | bytes 655392 | tf_op jit(solution)/shard_map/ppermute | solution.py:206
  74.6 0.1 shard_map.78
  74.7 2.1 %collective-permute-start.4 = (f32[64,1280]{1,0:T(8,128)S(1)}, f32[64,1280]{1,0:T(8,128)S(1)}, u32[]{:S(2)}, u32[]{:S(2)}) collective-permute-start(f32[64,1280]{1,0:T(8,128)S(1)} %get-tuple-element.19), channel_id=1, source_target_pairs={{0,1},{1,0},{2,3},{3,2},{4,5},{5,4},{6,7},{7,6},{8,9},{9,8},{10,11... | collective-permute-start | bytes 983048 | tf_op jit(solution)/shard_map/ppermute | solution.py:209
  76.8 8.7 %collective-permute-done.4.came_ref = f32[64,1280]{1,0:T(8,128)S(1)} collective-permute-done((f32[64,1280]{1,0:T(8,128)S(1)}, f32[64,1280]{1,0:T(8,128)S(1)}, u32[]{:S(2)}, u32[]{:S(2)}) %collective-permute-start.4) | collective-permute-done | bytes 327712 | tf_op jit(solution)/shard_map/ppermute | solution.py:209
  85.5 1.1 all-to-all-done.2
  86.6 0.2 shard_map.79
  86.8 13.7 %all_to_all.50 = bf16[8,8,1280]{2,1,0:T(8,128)(2,1)S(1)} all-to-all(bf16[8,8,1280]{2,1,0:T(8,128)(2,1)S(1)} %bitcast.12), channel_id=1, replica_groups=mesh['zh'=4,'z0'=2,'xl'=4,'core'=2,'xh'=2,'yh'=4,'y0'=2] {'z0','yh'}, dimensions={0} | all-to-all | bytes 327680 | tf_op jit(solution)/shard_map/all_to_all | solution.py:213
  100.6 0.0 copy-start
  100.6 0.8 shard_map.82
  101.3 0.0 copy-start.3
  101.3 7.3 %all-to-all-start.4 = ((f32[4,8,128]{2,1,0:T(8,128)}), f32[4,8,128]{2,1,0:T(8,128)S(1)}, u32[]{:S(2)}, u32[]{:S(2)}) async-start(f32[4,8,128]{2,1,0:T(8,128)} %shard_map.82), calls=%async_computation.4 | async-start | bytes 32768 | tf_op jit(solution)/shard_map/all_to_all | solution.py:217
  108.6 0.0 copy-done
  108.6 0.0 copy-done.3
  108.6 0.0 copy-start.1
  108.6 0.0 copy-start.2
  108.6 0.8 shard_map.81
  109.4 0.0 copy-done.1
  109.4 0.0 copy-done.2
  109.4 0.8 shard_map.80
  110.2 1.5 %all-to-all-done.4 = f32[4,8,128]{2,1,0:T(8,128)S(1)} async-done(((f32[4,8,128]{2,1,0:T(8,128)}), f32[4,8,128]{2,1,0:T(8,128)S(1)}, u32[]{:S(2)}, u32[]{:S(2)}) %all-to-all-start.4) | async-done | bytes 16416 | tf_op jit(solution)/shard_map/all_to_all | solution.py:217
  111.8 0.5 broadcast_multiply_fusion
  (1 shorter events, 0.0 us)
Async XLA Ops:
  21.2 36.5 %all-to-all-start.1 = ((bf16[32,8,1152]{2,1,0:T(8,128)(2,1)}), bf16[32,8,1152]{2,1,0:T(8,128)(2,1)S(1)}, u32[]{:S(2)}, u32[]{:S(2)}) async-start(bf16[32,8,1152]{2,1,0:T(8,128)(2,1)} %bitcast.17), calls=%async_computation.1 | async-start | bytes 1179648 | tf_op jit(solution)/shard_map/all_to_all | solution.py:191
  41.1 8.4 %collective-permute-start = (bf16[64,1280]{1,0:T(8,128)(2,1)S(1)}, bf16[64,1280]{1,0:T(8,128)(2,1)S(1)}, u32[]{:S(2)}, u32[]{:S(2)}) collective-permute-start(bf16[64,1280]{1,0:T(8,128)(2,1)S(1)} %bitcast.14), channel_id=1, source_target_pairs={{0,1},{1,0},{2,3},{3,2},{4,5},{5,4},{6,7},{7,6},{8,9},{9,8},{10,11... | collective-permute-start | bytes 491528 | tf_op jit(solution)/shard_map/ppermute | solution.py:192
  44.0 10.5 %collective-permute-start.1 = (bf16[64,1280]{1,0:T(8,128)(2,1)S(1)}, bf16[64,1280]{1,0:T(8,128)(2,1)S(1)}, u32[]{:S(2)}, u32[]{:S(2)}) collective-permute-start(bf16[64,1280]{1,0:T(8,128)(2,1)S(1)} %bitcast.15), channel_id=1, source_target_pairs={{0,16},{16,0},{1,17},{17,1},{2,18},{18,2},{3,19},{19,3},{4,20},{20... | collective-permute-start | bytes 491528 | tf_op jit(solution)/shard_map/ppermute | solution.py:193
  49.5 5.0 %collective-permute-start.2 = (bf16[64,1280]{1,0:T(8,128)(2,1)S(1)}, bf16[64,1280]{1,0:T(8,128)(2,1)S(1)}, u32[]{:S(2)}, u32[]{:S(2)}) collective-permute-start(bf16[64,1280]{1,0:T(8,128)(2,1)S(1)} %collective-permute-done.b), channel_id=1, source_target_pairs={{0,16},{16,0},{1,17},{17,1},{2,18},{18,2},{3,19},{19,3},{4,20},{20... | collective-permute-start | bytes 491528 | tf_op jit(solution)/shard_map/ppermute | solution.py:194
  60.0 26.6 %all-to-all-start.2 = ((bf16[32,8,1280]{2,1,0:T(8,128)(2,1)}), bf16[32,8,1280]{2,1,0:T(8,128)(2,1)S(1)}, u32[]{:S(2)}, u32[]{:S(2)}) async-start(bf16[32,8,1280]{2,1,0:T(8,128)(2,1)} %bitcast.4), calls=%async_computation.2 | async-start | bytes 1310720 | tf_op jit(solution)/shard_map/all_to_all | solution.py:205
  68.7 6.0 %collective-permute-start.3 = (f32[128,1280]{1,0:T(8,128)S(1)}, f32[128,1280]{1,0:T(8,128)S(1)}, u32[]{:S(2)}, u32[]{:S(2)}) collective-permute-start(f32[128,1280]{1,0:T(8,128)S(1)} %get-tuple-element.17), channel_id=1, source_target_pairs={{0,16},{16,0},{1,17},{17,1},{2,18},{18,2},{3,19},{19,3},{4,20},{20... | collective-permute-start | bytes 1966088 | tf_op jit(solution)/shard_map/ppermute | solution.py:206
  74.7 10.8 %collective-permute-start.4 = (f32[64,1280]{1,0:T(8,128)S(1)}, f32[64,1280]{1,0:T(8,128)S(1)}, u32[]{:S(2)}, u32[]{:S(2)}) collective-permute-start(f32[64,1280]{1,0:T(8,128)S(1)} %get-tuple-element.19), channel_id=1, source_target_pairs={{0,1},{1,0},{2,3},{3,2},{4,5},{5,4},{6,7},{7,6},{8,9},{9,8},{10,11... | collective-permute-start | bytes 983048 | tf_op jit(solution)/shard_map/ppermute | solution.py:209
  100.6 8.0 %copy-start = (f32[8,1152]{1,0:T(8,128)S(1)}, f32[8,1152]{1,0:T(8,128)}, u32[]{:S(2)}) copy-start(f32[8,1152]{1,0:T(8,128)} %get-tuple-element.23.unit_ref) | copy-start | bytes 110596
  101.3 7.3 %copy-start.3 = (f32[8,1]{1,0:T(8,128)S(1)}, f32[8,1]{1,0:T(8,128)}, u32[]{:S(2)}) copy-start(f32[8,1]{1,0:T(8,128)} %get-tuple-element.24.norm_ref) | copy-start | bytes 100
  101.3 10.4 %all-to-all-start.4 = ((f32[4,8,128]{2,1,0:T(8,128)}), f32[4,8,128]{2,1,0:T(8,128)S(1)}, u32[]{:S(2)}, u32[]{:S(2)}) async-start(f32[4,8,128]{2,1,0:T(8,128)} %shard_map.82), calls=%async_computation.4 | async-start | bytes 32768 | tf_op jit(solution)/shard_map/all_to_all | solution.py:217
  108.6 0.8 copy-start.1
  108.6 0.8 copy-start.2

commit v14 on v4

--- a/solution.py
+++ b/solution.py
@@ -149,13 +149,13 @@
     grad_out[...] = (grad - unit * jnp.sum(unit * grad, axis=1, keepdims=True)) / norm_ref[...]
 
 
-def stats_kernel(own_rows, parts_ref, out_ref):
+def stats_kernel(own_rows, batch, parts_ref, out_ref):
     width = parts_ref.shape[1] - EXTRA
     lane = lanes(8)
     out = jnp.zeros(lane.shape, F32)
     for n, value in enumerate(merge_stats(parts_ref[:, width:].astype(F32), own_rows)):
-        out = jnp.where(lane == n, value, out)
-    out_ref[...] = jnp.broadcast_to(out[None], out_ref.shape)
+        out = jnp.where(lane == n, value / batch, out)
+    out_ref[...] = out
 
 
 def shape(*dims, dtype=BF16):
@@ -212,12 +212,15 @@
     )
     image_back = lax.all_to_all(image_parts, IMAGE_GROUP, 0, 0, tiled=True)
     text_grad = call(finish_kernel, unit_shape, text_back, text_unit, text_norm)
-    four = sizes[PAIR] * sizes["core"]
-    sums = call(functools.partial(stats_kernel, own_rows), shape(four, 8, EXTRA, dtype=F32), image_back)
-    sums = lax.all_to_all(sums, (PAIR, "core"), 0, 0, tiled=True)
+    batch = own_rows * math.prod(sizes.values())
+    sums = call(functools.partial(stats_kernel, own_rows, batch), shape(8, EXTRA, dtype=F32), image_back)
+    others = (
+        lax.ppermute(sums, "core", swap),
+        lax.ppermute(sums, PAIR, swap),
+        lax.ppermute(sums, (PAIR, "core"), [(0, 3), (1, 2), (2, 1), (3, 0)]),
+    )
     image_grad = call(finish_kernel, unit_shape, image_back, image_unit, image_norm)
-    batch = own_rows * math.prod(sizes.values())
-    stats = jnp.sum(sums[:, 0, :3], axis=0) / batch
+    stats = ((sums + others[0]) + (others[1] + others[2]))[0, :3]
     return (image_grad, text_grad, stats)
 
 

time: 112 us -> 113 us (level)
  starting transfers between devices: 47.5 us -> 51.5 us
  waiting for transfers between devices: 15.2 us -> 13.7 us
    ppermute x0 -> x3, starting transfers between devices: none -> 11.7 us  [the longest x1 7.52 us: per_device(): lax.ppermute(sums, (PAIR, 'core'), [(0, 3), (1, 2), (2, 1), (3, 0)])]
    all_to_all x1 -> x0, starting transfers between devices: 7.81 us -> none  [per_device(): sums = lax.all_to_all(sums, (PAIR, 'core'), 0, 0, tiled=True)]
    all_to_all x1 -> x0, waiting for transfers between devices: 1.5 us -> none  [per_device(): sums = lax.all_to_all(sums, (PAIR, 'core'), 0, 0, tiled=True)]
  transfers between devices with their start and end apart: 8 -> 10, of which waited for: 5 -> 4; matrix products, arithmetic and copies ran while one was open for 0% -> 0% of each run, Pallas kernels for 2% -> 1%
where the time goes in v14:
time: 113 us; the launch traced here: 112 us
  starting transfers between devices  51.5 us (46%)
  blocking collectives  38.6 us (34%)
  waiting for transfers between devices  13.7 us (12%)
  Pallas kernels  6.17 us (5%)
  between operations  2.1 us (2%)
    all_to_all x1, blocking collectives, per_device(): piece = lax.all_to_all(image_send, IMAGE_GROUP, 0, 0, tiled=True)  25.6 us
    all_to_all x1, blocking collectives, per_device(): image_back = lax.all_to_all(image_parts, IMAGE_GROUP, 0, 0, tiled=True)  13 us
    all_to_all x1, starting transfers between devices, per_device(): text = lax.all_to_all(text_send, TEXT_GROUP, 0, 0, tiled=True)  11.7 us
    all_to_all x1, starting transfers between devices, per_device(): text_back = lax.all_to_all(text_parts, TEXT_GROUP, 0, 0, tiled=True)  8.01 us
    ppermute x1, waiting for transfers between devices, per_device(): came_pair = lax.ppermute(send, PAIR, swap)  7.77 us
    ppermute x1, starting transfers between devices, per_device(): lax.ppermute(sums, (PAIR, 'core'), [(0, 3), (1, 2), (2, 1), (3, 0)])  7.52 us
    pallas_call x7, Pallas kernels, call(): pl.pallas_call(kernel, out_shape=outs, in_specs=[VMEM] * (len(args) - sca...  6.17 us
    ppermute x1, starting transfers between devices, per_device(): came_pair = lax.ppermute(send, PAIR, swap)  4.62 us
  transfers between devices with their start and end apart: 10, of which 4 were waited for; matrix products, arithmetic and copies ran while one was open for 0% of the time, Pallas kernels for 1%

profile of v14, /device:TPU:1, one launch (start us, length us, event | category | flops | bytes accessed | tf_op | source)
XLA Modules:
  0.0 112.5 jit_solution(5033655924501813199)
XLA Ops:
  0.6 1.8 %shard_map.76 = (bf16[64,1280]{1,0:T(8,128)(2,1)}, bf16[256,1152]{1,0:T(8,128)(2,1)}, f32[8,1152]{1,0:T(8,128)}, f32[8,1]{1,0:T(8,128)}, f32[8,1152]{1,0:T(8,128)}, /*index=5*/f32[8,1]{1,0:T(8,128)}) custom-call(bf16[8,1152]{1,0:T(8,128)(2,1)} %image_ref.1, bf16[8,1152]{1,0:T(8,128)(2,1)} %text_ref.1, s32[8]{0:T(128)} %pair_ref.1), custom_call_target="tpu_custom_call" | custom-call | bytes 147584 | tf_op jit(solution)/shard_map/pallas_call | solution.py:167
  2.5 25.6 %all_to_all.44 = bf16[8,8,1280]{2,1,0:T(8,128)(2,1)S(1)} all-to-all(bf16[8,8,1280]{2,1,0:T(8,128)(2,1)} %bitcast.20), channel_id=1, replica_groups=mesh['zh'=4,'z0'=2,'xl'=4,'core'=2,'xh'=2,'yh'=4,'y0'=2] {'zh','y0'}, dimensions={0} | all-to-all | bytes 327680 | tf_op jit(solution)/shard_map/all_to_all | solution.py:190
  28.0 11.7 %all-to-all-start.1 = ((bf16[32,8,1152]{2,1,0:T(8,128)(2,1)}), bf16[32,8,1152]{2,1,0:T(8,128)(2,1)S(1)}, u32[]{:S(2)}, u32[]{:S(2)}) async-start(bf16[32,8,1152]{2,1,0:T(8,128)(2,1)} %bitcast.19), calls=%async_computation.1 | async-start | bytes 1179648 | tf_op jit(solution)/shard_map/all_to_all | solution.py:191
  39.7 3.9 %collective-permute-start = (bf16[64,1280]{1,0:T(8,128)(2,1)S(1)}, bf16[64,1280]{1,0:T(8,128)(2,1)S(1)}, u32[]{:S(2)}, u32[]{:S(2)}) collective-permute-start(bf16[64,1280]{1,0:T(8,128)(2,1)S(1)} %bitcast.16), channel_id=1, source_target_pairs={{0,128},{128,0},{1,129},{129,1},{2,130},{130,2},{3,131},{131,3},{4... | collective-permute-start | bytes 491528 | tf_op jit(solution)/shard_map/ppermute | solution.py:192
  43.6 4.5 %collective-permute-start.1 = (bf16[64,1280]{1,0:T(8,128)(2,1)S(1)}, bf16[64,1280]{1,0:T(8,128)(2,1)S(1)}, u32[]{:S(2)}, u32[]{:S(2)}) collective-permute-start(bf16[64,1280]{1,0:T(8,128)(2,1)S(1)} %bitcast.17), channel_id=1, source_target_pairs={{0,16},{16,0},{1,17},{17,1},{2,18},{18,2},{3,19},{19,3},{4,20},{20... | collective-permute-start | bytes 491528 | tf_op jit(solution)/shard_map/ppermute | solution.py:193
  48.2 0.0 collective-permute-done.b
  48.2 3.3 %collective-permute-start.2 = (bf16[64,1280]{1,0:T(8,128)(2,1)S(1)}, bf16[64,1280]{1,0:T(8,128)(2,1)S(1)}, u32[]{:S(2)}, u32[]{:S(2)}) collective-permute-start(bf16[64,1280]{1,0:T(8,128)(2,1)S(1)} %collective-permute-done.b), channel_id=1, source_target_pairs={{0,16},{16,0},{1,17},{17,1},{2,18},{18,2},{3,19},{19,3},{4,20},{20... | collective-permute-start | bytes 491528 | tf_op jit(solution)/shard_map/ppermute | solution.py:194
  52.8 0.0 collective-permute-done.1.c
  52.8 0.0 collective-permute-done.2.d
  52.8 3.9 %all-to-all-done.1 = bf16[32,8,1152]{2,1,0:T(8,128)(2,1)S(1)} async-done(((bf16[32,8,1152]{2,1,0:T(8,128)(2,1)}), bf16[32,8,1152]{2,1,0:T(8,128)(2,1)S(1)}, u32[]{:S(2)}, u32[]{:S(2)}) %all-to-all-start.1) | async-done | bytes 589856 | tf_op jit(solution)/shard_map/all_to_all | solution.py:191
  56.7 2.3 %shard_map.77 = (bf16[256,1280]{1,0:T(8,128)(2,1)}, f32[128,1280]{1,0:T(8,128)S(1)}, f32[128,1280]{1,0:T(8,128)S(1)}) custom-call(bf16[64,1280]{1,0:T(8,128)(2,1)S(1)} %bitcast.18, bf16[64,1280]{1,0:T(8,128)(2,1)S(1)} %collective-permute-done.b, bf16[64,1280]{1,0:T(8,128)(2,1)S(1)} %collective-permute-done.1.c, ...), custom_call_target="tpu_custom_call" | custom-call | flops 452984832 | bytes 4980768 | tf_op jit(solution)/shard_map/pallas_call | solution.py:167
  59.0 8.0 %all-to-all-start.2 = ((bf16[32,8,1280]{2,1,0:T(8,128)(2,1)}), bf16[32,8,1280]{2,1,0:T(8,128)(2,1)S(1)}, u32[]{:S(2)}, u32[]{:S(2)}) async-start(bf16[32,8,1280]{2,1,0:T(8,128)(2,1)} %bitcast.4), calls=%async_computation.2 | async-start | bytes 1310720 | tf_op jit(solution)/shard_map/all_to_all | solution.py:205
  67.0 3.7 %collective-permute-start.3 = (f32[128,1280]{1,0:T(8,128)S(1)}, f32[128,1280]{1,0:T(8,128)S(1)}, u32[]{:S(2)}, u32[]{:S(2)}) collective-permute-start(f32[128,1280]{1,0:T(8,128)S(1)} %get-tuple-element.17), channel_id=1, source_target_pairs={{0,16},{16,0},{1,17},{17,1},{2,18},{18,2},{3,19},{19,3},{4,20},{20... | collective-permute-start | bytes 1966088 | tf_op jit(solution)/shard_map/ppermute | solution.py:206
  70.7 1.7 %collective-permute-done.3.came_ref = f32[128,1280]{1,0:T(8,128)S(1)} collective-permute-done((f32[128,1280]{1,0:T(8,128)S(1)}, f32[128,1280]{1,0:T(8,128)S(1)}, u32[]{:S(2)}, u32[]{:S(2)}) %collective-permute-start.3) | collective-permute-done | bytes 655392 | tf_op jit(solution)/shard_map/ppermute | solution.py:206
  72.4 0.1 shard_map.78
  72.5 4.6 %collective-permute-start.4 = (f32[64,1280]{1,0:T(8,128)S(1)}, f32[64,1280]{1,0:T(8,128)S(1)}, u32[]{:S(2)}, u32[]{:S(2)}) collective-permute-start(f32[64,1280]{1,0:T(8,128)S(1)} %get-tuple-element.19), channel_id=1, source_target_pairs={{0,128},{128,0},{1,129},{129,1},{2,130},{130,2},{3,131},{131,3},{4... | collective-permute-start | bytes 983048 | tf_op jit(solution)/shard_map/ppermute | solution.py:209
  77.1 7.8 %collective-permute-done.4.came_ref = f32[64,1280]{1,0:T(8,128)S(1)} collective-permute-done((f32[64,1280]{1,0:T(8,128)S(1)}, f32[64,1280]{1,0:T(8,128)S(1)}, u32[]{:S(2)}, u32[]{:S(2)}) %collective-permute-start.4) | collective-permute-done | bytes 327712 | tf_op jit(solution)/shard_map/ppermute | solution.py:209
  84.9 0.3 all-to-all-done.2
  85.1 0.2 shard_map.79
  85.3 13.0 %all_to_all.45 = bf16[8,8,1280]{2,1,0:T(8,128)(2,1)S(1)} all-to-all(bf16[8,8,1280]{2,1,0:T(8,128)(2,1)S(1)} %bitcast.14), channel_id=1, replica_groups=mesh['zh'=4,'z0'=2,'xl'=4,'core'=2,'xh'=2,'yh'=4,'y0'=2] {'zh','y0'}, dimensions={0} | all-to-all | bytes 327680 | tf_op jit(solution)/shard_map/all_to_all | solution.py:213
  98.3 0.0 copy-start
  98.3 0.0 copy-start.3
  98.3 0.2 shard_map.82
  98.5 7.5 %collective-permute-start.7 = (f32[8,128]{1,0:T(8,128)S(1)}, f32[8,128]{1,0:T(8,128)S(1)}, u32[]{:S(2)}, u32[]{:S(2)}) collective-permute-start(f32[8,128]{1,0:T(8,128)S(1)} %shard_map.82), channel_id=1, source_target_pairs={{0,144},{16,128},{128,16},{144,0},{1,145},{17,129},{129,17},{145,1... | collective-permute-start | bytes 12296 | tf_op jit(solution)/shard_map/ppermute | solution.py:220
  106.1 2.1 %collective-permute-start.6 = (f32[8,128]{1,0:T(8,128)S(1)}, f32[8,128]{1,0:T(8,128)S(1)}, u32[]{:S(2)}, u32[]{:S(2)}) collective-permute-start(f32[8,128]{1,0:T(8,128)S(1)} %shard_map.82), channel_id=1, source_target_pairs={{0,128},{128,0},{1,129},{129,1},{2,130},{130,2},{3,131},{131,3},{4... | collective-permute-start | bytes 12296 | tf_op jit(solution)/shard_map/ppermute | solution.py:219
  108.2 2.1 %collective-permute-start.5 = (f32[8,128]{1,0:T(8,128)S(1)}, f32[8,128]{1,0:T(8,128)S(1)}, u32[]{:S(2)}, u32[]{:S(2)}) collective-permute-start(f32[8,128]{1,0:T(8,128)S(1)} %shard_map.82), channel_id=1, source_target_pairs={{0,16},{16,0},{1,17},{17,1},{2,18},{18,2},{3,19},{19,3},{4,20},{20... | collective-permute-start | bytes 12296 | tf_op jit(solution)/shard_map/ppermute | solution.py:218
  110.3 0.0 copy-done
  110.3 0.0 copy-done.3
  110.3 0.0 copy-start.1
  110.3 0.0 copy-start.2
  110.3 0.8 shard_map.81
  111.2 0.0 copy-done.1
  111.2 0.0 copy-done.2
  111.2 0.8 shard_map.80
  111.9 0.0 collective-permute-done.7
  112.0 0.0 collective-permute-done.6
  112.0 0.0 collective-permute-done.5
  112.0 0.5 slice_bitcast_fusion
  (1 shorter events, 0.0 us)
Async XLA Ops:
  28.0 28.7 %all-to-all-start.1 = ((bf16[32,8,1152]{2,1,0:T(8,128)(2,1)}), bf16[32,8,1152]{2,1,0:T(8,128)(2,1)S(1)}, u32[]{:S(2)}, u32[]{:S(2)}) async-start(bf16[32,8,1152]{2,1,0:T(8,128)(2,1)} %bitcast.19), calls=%async_computation.1 | async-start | bytes 1179648 | tf_op jit(solution)/shard_map/all_to_all | solution.py:191
  39.7 8.5 %collective-permute-start = (bf16[64,1280]{1,0:T(8,128)(2,1)S(1)}, bf16[64,1280]{1,0:T(8,128)(2,1)S(1)}, u32[]{:S(2)}, u32[]{:S(2)}) collective-permute-start(bf16[64,1280]{1,0:T(8,128)(2,1)S(1)} %bitcast.16), channel_id=1, source_target_pairs={{0,128},{128,0},{1,129},{129,1},{2,130},{130,2},{3,131},{131,3},{4... | collective-permute-start | bytes 491528 | tf_op jit(solution)/shard_map/ppermute | solution.py:192
  43.6 9.1 %collective-permute-start.1 = (bf16[64,1280]{1,0:T(8,128)(2,1)S(1)}, bf16[64,1280]{1,0:T(8,128)(2,1)S(1)}, u32[]{:S(2)}, u32[]{:S(2)}) collective-permute-start(bf16[64,1280]{1,0:T(8,128)(2,1)S(1)} %bitcast.17), channel_id=1, source_target_pairs={{0,16},{16,0},{1,17},{17,1},{2,18},{18,2},{3,19},{19,3},{4,20},{20... | collective-permute-start | bytes 491528 | tf_op jit(solution)/shard_map/ppermute | solution.py:193
  48.2 4.6 %collective-permute-start.2 = (bf16[64,1280]{1,0:T(8,128)(2,1)S(1)}, bf16[64,1280]{1,0:T(8,128)(2,1)S(1)}, u32[]{:S(2)}, u32[]{:S(2)}) collective-permute-start(bf16[64,1280]{1,0:T(8,128)(2,1)S(1)} %collective-permute-done.b), channel_id=1, source_target_pairs={{0,16},{16,0},{1,17},{17,1},{2,18},{18,2},{3,19},{19,3},{4,20},{20... | collective-permute-start | bytes 491528 | tf_op jit(solution)/shard_map/ppermute | solution.py:194
  59.0 26.2 %all-to-all-start.2 = ((bf16[32,8,1280]{2,1,0:T(8,128)(2,1)}), bf16[32,8,1280]{2,1,0:T(8,128)(2,1)S(1)}, u32[]{:S(2)}, u32[]{:S(2)}) async-start(bf16[32,8,1280]{2,1,0:T(8,128)(2,1)} %bitcast.4), calls=%async_computation.2 | async-start | bytes 1310720 | tf_op jit(solution)/shard_map/all_to_all | solution.py:205
  67.0 5.4 %collective-permute-start.3 = (f32[128,1280]{1,0:T(8,128)S(1)}, f32[128,1280]{1,0:T(8,128)S(1)}, u32[]{:S(2)}, u32[]{:S(2)}) collective-permute-start(f32[128,1280]{1,0:T(8,128)S(1)} %get-tuple-element.17), channel_id=1, source_target_pairs={{0,16},{16,0},{1,17},{17,1},{2,18},{18,2},{3,19},{19,3},{4,20},{20... | collective-permute-start | bytes 1966088 | tf_op jit(solution)/shard_map/ppermute | solution.py:206
  72.5 12.4 %collective-permute-start.4 = (f32[64,1280]{1,0:T(8,128)S(1)}, f32[64,1280]{1,0:T(8,128)S(1)}, u32[]{:S(2)}, u32[]{:S(2)}) collective-permute-start(f32[64,1280]{1,0:T(8,128)S(1)} %get-tuple-element.19), channel_id=1, source_target_pairs={{0,128},{128,0},{1,129},{129,1},{2,130},{130,2},{3,131},{131,3},{4... | collective-permute-start | bytes 983048 | tf_op jit(solution)/shard_map/ppermute | solution.py:209
  98.3 12.0 %copy-start = (f32[8,1152]{1,0:T(8,128)S(1)}, f32[8,1152]{1,0:T(8,128)}, u32[]{:S(2)}) copy-start(f32[8,1152]{1,0:T(8,128)} %get-tuple-element.23.unit_ref) | copy-start | bytes 110596
  98.3 12.0 %copy-start.3 = (f32[8,1]{1,0:T(8,128)S(1)}, f32[8,1]{1,0:T(8,128)}, u32[]{:S(2)}) copy-start(f32[8,1]{1,0:T(8,128)} %get-tuple-element.24.norm_ref) | copy-start | bytes 100
  98.5 13.4 %collective-permute-start.7 = (f32[8,128]{1,0:T(8,128)S(1)}, f32[8,128]{1,0:T(8,128)S(1)}, u32[]{:S(2)}, u32[]{:S(2)}) collective-permute-start(f32[8,128]{1,0:T(8,128)S(1)} %shard_map.82), channel_id=1, source_target_pairs={{0,144},{16,128},{128,16},{144,0},{1,145},{17,129},{129,17},{145,1... | collective-permute-start | bytes 12296 | tf_op jit(solution)/shard_map/ppermute | solution.py:220
  106.1 5.9 %collective-permute-start.6 = (f32[8,128]{1,0:T(8,128)S(1)}, f32[8,128]{1,0:T(8,128)S(1)}, u32[]{:S(2)}, u32[]{:S(2)}) collective-permute-start(f32[8,128]{1,0:T(8,128)S(1)} %shard_map.82), channel_id=1, source_target_pairs={{0,128},{128,0},{1,129},{129,1},{2,130},{130,2},{3,131},{131,3},{4... | collective-permute-start | bytes 12296 | tf_op jit(solution)/shard_map/ppermute | solution.py:219
  108.2 3.8 %collective-permute-start.5 = (f32[8,128]{1,0:T(8,128)S(1)}, f32[8,128]{1,0:T(8,128)S(1)}, u32[]{:S(2)}, u32[]{:S(2)}) collective-permute-start(f32[8,128]{1,0:T(8,128)S(1)} %shard_map.82), channel_id=1, source_target_pairs={{0,16},{16,0},{1,17},{17,1},{2,18},{18,2},{3,19},{19,3},{4,20},{20... | collective-permute-start | bytes 12296 | tf_op jit(solution)/shard_map/ppermute | solution.py:218
  110.3 0.8 copy-start.1
  110.3 0.8 copy-start.2
